TPU v7x, 32 devices: a whole 2x2x4 slice. The times are simulated.
32 devices in a mesh: dp: 8 (over z, x), mp: 4 (over y, core).
Axes of the slice: x: 2, y: 2, z: 4, core: 2. Of those that a mesh axis runs over, the one named last changes fastest.
Arguments:
- tokens: bfloat16 [16384, 768], P('dp'), may hold values from -6 to 6
- cotangent: bfloat16 [16384, 768], P('dp'), may hold values from -1.796875 to 1.796875
- lengths: int32 [8, 8], P('dp'), may hold values from 1 to 400, 2048 in all within a row
- gold: int32 [64], replicated, may hold values from 0 to 8191
- passages: bfloat16 [8192, 768], P('dp'), may hold values from -2 to 2
- w_query: bfloat16 [768, 768], P('dp', 'mp'), may hold values from -0.21875 to 0.21875
- w_key: bfloat16 [768, 768], P('dp', 'mp'), may hold values from -0.21875 to 0.21875
- w_value: bfloat16 [768, 768], P('dp', 'mp'), may hold values from -0.21875 to 0.21875
- b_query: float32 [768], P('mp'), may hold values from -1.2 to 1.2
- b_value: float32 [768], P('mp'), may hold values from -1.2 to 1.2
- w_out: bfloat16 [768, 768], P('mp', 'dp'), may hold values from -0.875 to 0.875
- b_out: float32 [768], replicated, may hold values from -1.2 to 1.2
- gain_attn: float32 [768], replicated, may hold values from 0.5 to 1.5
- shift_attn: float32 [768], replicated, may hold values from -1.2 to 1.2
- w_up: bfloat16 [768, 3072], P('dp', 'mp'), may hold values from -0.21875 to 0.21875
- b_up: float32 [3072], P('mp'), may hold values from -1.2 to 1.2
- w_down: bfloat16 [3072, 768], P('mp', 'dp'), may hold values from -0.109375 to 0.109375
- b_down: float32 [768], replicated, may hold values from -1.2 to 1.2
- gain_ffn: float32 [768], replicated, may hold values from 0.5 to 1.5
- shift_ffn: float32 [768], replicated, may hold values from -1.2 to 1.2
Outputs:
- scores: float32 [64, 8192], P(None, 'dp')
- query_lse: float32 [64], P('dp')
- encoded: bfloat16 [16384, 768], P('dp')
- token_grad: float32 [16384, 768], P('dp')
- grad_w_query: float32 [768, 768], P('dp', 'mp')
- grad_w_key: float32 [768, 768], P('dp', 'mp')
- grad_w_value: float32 [768, 768], P('dp', 'mp')
- grad_b_query: float32 [768], P('mp')
- grad_b_value: float32 [768], P('mp')
- grad_w_out: float32 [768, 768], P('mp', 'dp')
- grad_b_out: float32 [768], replicated
- grad_gain_attn: float32 [768], replicated
- grad_shift_attn: float32 [768], replicated
- grad_w_up: float32 [768, 3072], P('dp', 'mp')
- grad_b_up: float32 [3072], P('mp')
- grad_w_down: float32 [3072, 768], P('mp', 'dp')
- grad_b_down: float32 [768], replicated
- grad_gain_ffn: float32 [768], replicated
- grad_shift_ffn: float32 [768], replicated
Inputs may be any that keep to these rules, and one draw needn't show every extreme that they name: Each row holds, in order, the lengths of the 8 documents packed into one sequence; every row sums to 2048 and its largest entry is 400. `gold`: the index of each query's correct passage among all 8192.
All inputs are finite; a program needn't handle non-finite values.
Results may differ from a plain program's by a relative error of at most 0.025.
Values may be sent and summed in bfloat16 or wider, within the bound.
A program may use at most 192 MiB of HBM per device.

v0:
```python
import jax
import jax.numpy as jnp
from jax import lax
from jax.sharding import PartitionSpec as P

HEAD = 64


EPSILON = 1e-05
NEGATIVE = -1e30


def cut_along(array, dim, devices):
    before, after = (array.shape[:dim], array.shape[dim + 1 :])
    return jnp.moveaxis(array.reshape(*before, devices, -1, *after), dim, 0)


def summed_on_arrival(array, axis, dim):
    pieces = cut_along(array, dim, lax.axis_size(axis))
    arrived = lax.all_to_all(pieces, axis, split_axis=0, concat_axis=0, tiled=True)
    return arrived.astype(jnp.float32).sum(axis=0)


def sent_together(arrays, axis, dim, along):
    both = jnp.concatenate(arrays, axis=along)
    filled, at, done = (summed_on_arrival(both, axis, dim), 0, [])
    for a in arrays:
        done.append(lax.slice_in_dim(filled, at, at + a.shape[along], axis=along))
        at += a.shape[along]
    return tuple(done)


def normalize(hidden, gain, shift):
    average = jnp.mean(hidden, axis=-1, keepdims=True)
    centred = hidden - average
    spread = jnp.mean(centred * centred, axis=-1, keepdims=True)
    factor = lax.rsqrt(spread + EPSILON)
    normed = centred * factor
    return (normed * gain + shift, normed, factor)


def normalize_back(grad_out, normed, factor, gain):
    grad_gain = jnp.sum(grad_out * normed, axis=0)
    grad_shift = jnp.sum(grad_out, axis=0)
    scaled = grad_out * gain
    grad_hidden = factor * (
        scaled
        - jnp.mean(scaled, axis=-1, keepdims=True)
        - normed * jnp.mean(scaled * normed, axis=-1, keepdims=True)
    )
    return (grad_hidden, grad_gain, grad_shift)


def document_marks(lengths, span):
    ends = jnp.cumsum(lengths, axis=-1)
    places = jnp.arange(span, dtype=jnp.int32)
    segments = jnp.sum((places[None, None, :] >= ends[:, :, None]).astype(jnp.int32), axis=1)
    return (segments, ends - lengths)


def contract_rows(left, right):
    return lax.dot_general(
        left, right, (((0,), (0,)), ((), ())), preferred_element_type=jnp.float32
    )


def contract_cols(left, right):
    return lax.dot_general(
        left, right, (((1,), (1,)), ((), ())), preferred_element_type=jnp.float32
    )


def gelu_exact(inputs):
    return jax.nn.gelu(inputs, approximate=False)


def block_scores(query_block, query_seg, key_rows, segments, score_scale):
    raw_scores = (
        jnp.einsum("bhe,mhe->hbm", query_block, key_rows, preferred_element_type=jnp.float32)
        * score_scale
    )
    same_doc = query_seg[:, None] == segments[None, :]
    return (raw_scores, same_doc)


def attend_block(packed, key_rows, value_rows, segments, score_scale):
    query_block, query_seg = packed
    raw_scores, same_doc = block_scores(query_block, query_seg, key_rows, segments, score_scale)
    masked = jnp.where(same_doc[None], raw_scores, NEGATIVE)
    row_peak = jnp.max(masked, axis=-1, keepdims=True)
    expo = jnp.exp(masked - row_peak)
    row_total = jnp.sum(expo, axis=-1, keepdims=True)
    soft_weights = expo / row_total
    context = jnp.einsum(
        "hbm,mhe->bhe",
        soft_weights.astype(jnp.bfloat16),
        value_rows,
        preferred_element_type=jnp.float32,
    )
    return (context, (row_peak + jnp.log(row_total))[..., 0])


def attend_back(carry, packed, key_rows, value_rows, segments, score_scale):
    grad_keys, grad_values = carry
    query_block, query_seg, log_totals, grad_context = packed
    raw_scores, same_doc = block_scores(query_block, query_seg, key_rows, segments, score_scale)
    soft_weights = jnp.where(same_doc[None], jnp.exp(raw_scores - log_totals[..., None]), 0.0)
    grad_soft = jnp.einsum(
        "bhe,mhe->hbm", grad_context, value_rows, preferred_element_type=jnp.float32
    )
    row_delta = jnp.sum(grad_soft * soft_weights, axis=-1, keepdims=True)
    grad_scores = (soft_weights * (grad_soft - row_delta)).astype(jnp.bfloat16)
    grad_query = (
        jnp.einsum("hbm,mhe->bhe", grad_scores, key_rows, preferred_element_type=jnp.float32)
        * score_scale
    )
    grad_keys = (
        grad_keys
        + jnp.einsum("hbm,bhe->mhe", grad_scores, query_block, preferred_element_type=jnp.float32)
        * score_scale
    )
    grad_values = grad_values + jnp.einsum(
        "hbm,bhe->mhe",
        soft_weights.astype(jnp.bfloat16),
        grad_context,
        preferred_element_type=jnp.float32,
    )
    return ((grad_keys, grad_values), grad_query)


def body(
    tokens,
    cotangent,
    lengths,
    gold,
    passages,
    w_query,
    w_key,
    w_value,
    b_query,
    b_value,
    w_out,
    b_out,
    gain_attn,
    shift_attn,
    w_up,
    b_up,
    w_down,
    b_down,
    gain_ffn,
    shift_ffn,
):
    full_query, full_key, full_value, full_out, full_up, full_down = (
        lax.all_gather(w_query, "dp", axis=0, tiled=True),
        lax.all_gather(w_key, "dp", axis=0, tiled=True),
        lax.all_gather(w_value, "dp", axis=0, tiled=True),
        lax.all_gather(w_out, "dp", axis=1, tiled=True),
        lax.all_gather(w_up, "dp", axis=0, tiled=True),
        lax.all_gather(w_down, "dp", axis=1, tiled=True),
    )
    length, model_width = tokens.shape
    head_cols = full_query.shape[1]
    head_count = head_cols // HEAD
    score_scale = HEAD ** (-0.5)
    block_rows = min(512, length)
    block_count = length // block_rows
    segments, starts = document_marks(lengths, length)
    segments = segments[0]
    starts = starts[0]
    inputs_f = tokens.astype(jnp.float32)
    query_rows = (jnp.dot(tokens, full_query, preferred_element_type=jnp.float32) + b_query).astype(
        jnp.bfloat16
    )
    key_rows = jnp.dot(tokens, full_key, preferred_element_type=jnp.float32).astype(jnp.bfloat16)
    value_rows = (jnp.dot(tokens, full_value, preferred_element_type=jnp.float32) + b_value).astype(
        jnp.bfloat16
    )
    query_heads = query_rows.reshape(block_count, block_rows, head_count, HEAD)
    key_heads = key_rows.reshape(length, head_count, HEAD)
    value_heads = value_rows.reshape(length, head_count, HEAD)
    seg_blocks = segments.reshape(block_count, block_rows)
    context, log_totals = lax.map(
        lambda packed: attend_block(packed, key_heads, value_heads, segments, score_scale),
        (query_heads, seg_blocks),
    )
    context_low = context.reshape(length, head_cols).astype(jnp.bfloat16)
    attn_part = jnp.dot(context_low, full_out, preferred_element_type=jnp.float32).astype(
        jnp.bfloat16
    )
    hidden_one = inputs_f + lax.psum(attn_part, "mp").astype(jnp.float32) + b_out
    normed_one, unit_one, factor_one = normalize(hidden_one, gain_attn, shift_attn)
    normed_low = normed_one.astype(jnp.bfloat16)
    activation = jnp.dot(normed_low, full_up, preferred_element_type=jnp.float32) + b_up
    gelu_low = gelu_exact(activation).astype(jnp.bfloat16)
    ffn_part = jnp.dot(gelu_low, full_down, preferred_element_type=jnp.float32).astype(jnp.bfloat16)
    hidden_two = normed_one + lax.psum(ffn_part, "mp").astype(jnp.float32) + b_down
    normed_two, unit_two, factor_two = normalize(hidden_two, gain_ffn, shift_ffn)
    encoded = normed_two.astype(jnp.bfloat16)
    first_rows = jnp.take(normed_two, starts, axis=0).astype(jnp.bfloat16)
    all_first = lax.all_gather(first_rows, "dp", axis=0, tiled=True)
    score_table = contract_cols(all_first, passages)
    row_peak = lax.pmax(jnp.max(score_table, axis=1), "dp")
    row_total = lax.psum(jnp.sum(jnp.exp(score_table - row_peak[:, None]), axis=1), "dp")
    own_count = first_rows.shape[0]
    whole_lse = row_peak + jnp.log(row_total)
    query_lse = lax.dynamic_slice_in_dim(whole_lse, lax.axis_index("dp") * own_count, own_count)
    soft_scores = jnp.exp(score_table - row_peak[:, None]) / row_total[:, None]
    first_column = lax.axis_index("dp") * score_table.shape[1]
    columns = first_column + jnp.arange(score_table.shape[1], dtype=jnp.int32)
    target = (gold[:, None] == columns[None, :]).astype(jnp.float32)
    grad_scores = (soft_scores - target).astype(jnp.bfloat16)
    grad_first = jnp.dot(grad_scores, passages, preferred_element_type=jnp.float32)
    own_grads = summed_on_arrival(grad_first.astype(jnp.bfloat16), "dp", 0)
    grad_two = cotangent.astype(jnp.float32).at[starts].add(own_grads)
    grad_hidden_two, grad_gain_two, grad_shift_two = normalize_back(
        grad_two, unit_two, factor_two, gain_ffn
    )
    grad_bias_down = jnp.sum(grad_hidden_two, axis=0)
    grad_ffn_low = grad_hidden_two.astype(jnp.bfloat16)
    grad_down = contract_rows(gelu_low, grad_ffn_low)
    grad_gelu = contract_cols(grad_ffn_low, full_down)
    _, gelu_pullback = jax.vjp(gelu_exact, activation)
    grad_act = gelu_pullback(grad_gelu)[0]
    grad_bias_up = jnp.sum(grad_act, axis=0)
    grad_act_low = grad_act.astype(jnp.bfloat16)
    grad_up = contract_rows(normed_low, grad_act_low)
    normed_part = contract_cols(grad_act_low, full_up).astype(jnp.bfloat16)
    grad_one = grad_hidden_two + lax.psum(normed_part, "mp").astype(jnp.float32)
    grad_hidden_one, grad_gain_one, grad_shift_one = normalize_back(
        grad_one, unit_one, factor_one, gain_attn
    )
    grad_bias_out = jnp.sum(grad_hidden_one, axis=0)
    grad_attn_low = grad_hidden_one.astype(jnp.bfloat16)
    grad_out = contract_rows(context_low, grad_attn_low)
    grad_context = contract_cols(grad_attn_low, full_out).astype(jnp.bfloat16)
    context_blocks = grad_context.reshape(block_count, block_rows, head_count, HEAD)
    zero_heads = jnp.zeros((length, head_count, HEAD), jnp.float32)
    (grad_keys, grad_values), grad_queries = lax.scan(
        lambda carry, packed: attend_back(
            carry, packed, key_heads, value_heads, segments, score_scale
        ),
        (zero_heads, zero_heads),
        (query_heads, seg_blocks, log_totals, context_blocks),
    )
    grad_queries = grad_queries.reshape(length, head_cols)
    grad_keys = grad_keys.reshape(length, head_cols)
    grad_values = grad_values.reshape(length, head_cols)
    grad_bias_query = jnp.sum(grad_queries, axis=0)
    grad_bias_value = jnp.sum(grad_values, axis=0)
    queries_low = grad_queries.astype(jnp.bfloat16)
    keys_low = grad_keys.astype(jnp.bfloat16)
    values_low = grad_values.astype(jnp.bfloat16)
    grad_query_w = contract_rows(tokens, queries_low)
    grad_key_w = contract_rows(tokens, keys_low)
    grad_value_w = contract_rows(tokens, values_low)
    input_part = (
        contract_cols(queries_low, full_query)
        + contract_cols(keys_low, full_key)
        + contract_cols(values_low, full_value)
    ).astype(jnp.bfloat16)
    sum_query, sum_key, sum_value, sum_out, sum_up, sum_down = (
        *sent_together(
            (
                grad_query_w.astype(jnp.bfloat16),
                grad_key_w.astype(jnp.bfloat16),
                grad_value_w.astype(jnp.bfloat16),
            ),
            "dp",
            0,
            1,
        ),
        summed_on_arrival(grad_out.astype(jnp.bfloat16), "dp", 1),
        summed_on_arrival(grad_up.astype(jnp.bfloat16), "dp", 0),
        summed_on_arrival(grad_down.astype(jnp.bfloat16), "dp", 1),
    )
    token_grad = grad_hidden_one + lax.psum(input_part, "mp").astype(jnp.float32)
    small_sums = lax.psum(
        (
            grad_bias_query,
            grad_bias_value,
            grad_bias_out,
            grad_gain_one,
            grad_shift_one,
            grad_bias_up,
            grad_bias_down,
            grad_gain_two,
            grad_shift_two,
        ),
        "dp",
    )
    return (
        score_table,
        query_lse,
        encoded,
        token_grad,
        sum_query,
        sum_key,
        sum_value,
        small_sums[0],
        small_sums[1],
        sum_out,
        small_sums[2],
        small_sums[3],
        small_sums[4],
        sum_up,
        small_sums[5],
        sum_down,
        small_sums[6],
        small_sums[7],
        small_sums[8],
    )


def solution(mesh):
    placed = (
        P("dp", None),
        P("dp", None),
        P("dp", None),
        P(),
        P("dp", None),
        P("dp", "mp"),
        P("dp", "mp"),
        P("dp", "mp"),
        P("mp"),
        P("mp"),
        P("mp", "dp"),
        P(),
        P(),
        P(),
        P("dp", "mp"),
        P("mp"),
        P("mp", "dp"),
        P(),
        P(),
        P(),
    )
    return jax.shard_map(
        body,
        mesh=mesh,
        in_specs=placed,
        out_specs=(
            P(None, "dp"),
            P("dp"),
            P("dp", None),
            P("dp", None),
            P("dp", "mp"),
            P("dp", "mp"),
            P("dp", "mp"),
            P("mp"),
            P("mp"),
            P("mp", "dp"),
            P(),
            P(),
            P(),
            P("dp", "mp"),
            P("mp"),
            P("mp", "dp"),
            P(),
            P(),
            P(),
        ),
        check_vma=False,
    )
```

profile of v0, /device:TPU:1, one launch (start us, length us, event | category | flops | bytes accessed | tf_op | source)
XLA Modules:
  0.0 911.8 jit_solution(3890375868098201737)
XLA Ops:
  11.9 26.2 %all_gather.24 = bf16[192,768]{0,1:T(8,128)(2,1)S(1)} all-gather(bf16[192,96]{0,1:T(8,128)(2,1)S(1)} %copy.58), channel_id=1, replica_groups=mesh['dp'=8,'mp'=4] {'dp'}, dimensions={1}, use_global_device_ids=true | all-gather | bytes 331776 | tf_op jit(solution)/shard_map/all_gather | solution.py:157
  38.1 25.2 %all_gather.21 = bf16[768,192]{1,0:T(8,128)(2,1)S(1)} all-gather(bf16[96,192]{1,0:T(8,128)(2,1)} %param.29), channel_id=1, replica_groups=mesh['dp'=8,'mp'=4] {'dp'}, dimensions={0}, use_global_device_ids=true | all-gather | bytes 331776 | tf_op jit(solution)/shard_map/all_gather | solution.py:154
  63.3 25.0 %all_gather.22 = bf16[768,192]{1,0:T(8,128)(2,1)S(1)} all-gather(bf16[96,192]{1,0:T(8,128)(2,1)} %param.30), channel_id=1, replica_groups=mesh['dp'=8,'mp'=4] {'dp'}, dimensions={0}, use_global_device_ids=true | all-gather | bytes 331776 | tf_op jit(solution)/shard_map/all_gather | solution.py:155
  88.3 27.0 %all_gather.23 = bf16[768,192]{1,0:T(8,128)(2,1)} all-gather(bf16[96,192]{1,0:T(8,128)(2,1)} %param.31), channel_id=1, replica_groups=mesh['dp'=8,'mp'=4] {'dp'}, dimensions={0}, use_global_device_ids=true | all-gather | bytes 331776 | tf_op jit(solution)/shard_map/all_gather | solution.py:156
  128.8 90.0 %while.29 = (s32[]{:T(128)}, bf16[4,512,3,64]{1,3,2,0:T(8,128)(2,1)}, f32[4,3,512]{2,1,0:T(4,128)}, s32[4,512]{1,0:T(4,128)}, s32[1,2048]{1,0:T(1,128)S(1)}, /*i...) while((s32[]{:T(128)}, ...), condition=%wide.region_5.6_spmd.clone, body=%wide.region_2.5_spmd.sunk.clone | while | flops 844102144 | bytes 50466980 | solution.py:182
  130.2 6.7 fusion.174
  136.9 6.8 fusion.175
  143.7 6.7 fusion.176
  152.7 6.7 fusion.174
  159.4 6.8 fusion.175
  166.2 6.7 fusion.176
  175.2 6.7 fusion.174
  181.9 6.8 fusion.175
  188.7 6.7 fusion.176
  197.7 6.7 fusion.174
  204.4 6.8 fusion.175
  211.3 6.7 fusion.176
  226.4 92.7 %all-reduce.6.cloned.1.call-done = bf16[2048,768]{1,0:T(8,128)(2,1)} async-done(((bf16[2048,768]{1,0:T(8,128)(2,1)}), bf16[2048,768]{1,0:T(8,128)(2,1)}) %all-reduce.6.cloned.1.call-update) | async-done | bytes 3145744 | tf_op jit(solution)/shard_map/psum | solution.py:190
  326.5 20.5 %multiply_convert_fusion.1 = (bf16[2048,768]{1,0:T(8,128)(2,1)}, f32[2048,768]{1,0:T(8,128)}, f32[2048,768]{1,0:T(8,128)}) fusion(f32[768]{0:T(1024)} %param.39, bf16[768,768]{1,0:T(8,128)(2,1)} %all-gather.3.cloned.1.call-done, f32[768]{0:T(1024)} %param.37, f32[768]{0:T(1024)} %param.36, f32[2048]{0:T(1024)S(1)} %add_rsqrt_fusion.1, ...), kind=kOutput, calls=%fused_computation.67 | convolution fusion | flops 2533883904 | bytes 23228416 | tf_op jit(solution)/shard_map/dot_general | solution.py:193
  347.1 6.6 convolution_convert_fusion.1
  353.7 68.6 %all-reduce.8.cloned.1.call-done = bf16[2048,768]{1,0:T(8,128)(2,1)} async-done(((bf16[2048,768]{1,0:T(8,128)(2,1)}), bf16[2048,768]{1,0:T(8,128)(2,1)}) %all-reduce.8.cloned.1.call-update) | async-done | bytes 3145744 | tf_op jit(solution)/shard_map/psum | solution.py:196
  435.6 24.6 %all_gather.27 = bf16[64,768]{1,0:T(8,128)(2,1)S(1)} all-gather(bf16[8,768]{1,0:T(8,128)(2,1)S(1)} %select_convert_fusion), channel_id=1, replica_groups=mesh['dp'=8,'mp'=4] {'dp'}, dimensions={0}, use_global_device_ids=true | all-gather | bytes 110592 | tf_op jit(solution)/shard_map/all_gather | solution.py:200
  460.9 17.5 %pmax.7 = f32[64]{0:T(128)S(1)} all-reduce(f32[64]{0:T(128)S(1)} %get-tuple-element.312), channel_id=1, replica_groups=mesh['dp'=8,'mp'=4] {'dp'}, use_global_device_ids=true, to_apply=%region_13.14 | all-reduce | flops 64 | bytes 512 | tf_op jit(solution)/shard_map/pmax | solution.py:202
  478.5 14.1 %psum.100 = f32[64]{0:T(128)S(1)} all-reduce(f32[64]{0:T(128)S(1)} %fusion.79), channel_id=1, replica_groups=mesh['dp'=8,'mp'=4] {'dp'}, use_global_device_ids=true, to_apply=%region_15.16 | all-reduce | flops 64 | bytes 512 | tf_op jit(solution)/shard_map/psum | solution.py:203
  503.0 6.1 scatter_fusion
  509.2 7.3 multiply_reduce_fusion.1
  519.2 9.2 %fusion.93 = (f32[768]{0:T(1024)}, bf16[2048,768]{1,0:T(8,128)(2,1)S(1)}) fusion(f32[2048,768]{1,0:T(8,128)S(1)} %bitcast.216, bf16[768,768]{0,1:T(8,128)(2,1)S(1)} %copy-done.59, f32[2048,768]{1,0:T(8,128)S(1)} %subtract_multiply_fusion.1, f32[2048,768]{1,0:T(8,128)} %get-tuple-element.311, f32[768]{0:T(1024)S(1)} %copy-done.60), kind=kOutput, calls=%fused_computation.160 | convolution fusion | flops 2442657024 | bytes 23205888 | tf_op jit(solution)/shard_map/dot_general | solution.py:68
  534.1 7.6 fusion.63
  546.5 7.4 fusion.66
  553.9 61.8 %all-reduce.10.cloned.1.call-done = bf16[2048,768]{1,0:T(8,128)(2,1)} async-done(((bf16[2048,768]{1,0:T(8,128)(2,1)}), bf16[2048,768]{1,0:T(8,128)(2,1)}) %all-reduce.10.cloned.1.call-update) | async-done | bytes 3145744 | tf_op jit(solution)/shard_map/psum | solution.py:228
  615.7 9.2 %multiply_reduce_fusion.2 = (f32[768]{0:T(1024)}, f32[2048]{0:T(1024)S(1)}, f32[2048]{0:T(1024)S(1)}, f32[768]{0:T(1024)}, f32[768]{0:T(1024)}) fusion(f32[2048,768]{1,0:T(8,128)} %copy-done.17, bf16[2048,768]{1,0:T(8,128)(2,1)} %all-reduce.10.cloned.1.call-done, f32[2048]{0:T(1024)} %copy-done.36, f32[2048]{0:T(1024)S(1)} %broadcast_multiply_fusion.5, ...), kind=kLoop, calls=%fused_computation.55 | loop fusion | flops 25159424 | bytes 15776768 | tf_op jit(solution)/shard_map/reduce_sum | solution.py:43
  624.9 6.0 fusion.86
  635.6 131.5 %while.30 = (s32[]{:T(128)}, f32[2048,3,64]{0,2,1:T(8,128)}, f32[2048,3,64]{0,2,1:T(8,128)}, f32[4,512,3,64]{1,3,2,0:T(8,128)}, bf16[4,512,3,64]{1,3,2,0:T(8,128...) while((s32[]{:T(128)}, f32[2048,3,64]{0,2,1:T(8,128)}, ...), condition=%wide.region_25.26_spmd.clone.clone, body=%wide.region_23.25_spmd.clone.sunk.clone | while | flops 2063563264 | bytes 134670672 | solution.py:238
  650.8 6.2 multiply_convert_fusion.4
  661.4 6.1 fusion.189
  683.9 6.2 multiply_convert_fusion.4
  694.5 6.1 fusion.189
  717.0 6.2 multiply_convert_fusion.4
  727.6 6.1 fusion.189
  744.3 5.8 multiply_reduce_fusion.11
  750.1 6.2 multiply_convert_fusion.4
  760.7 6.2 fusion.189
  792.2 7.9 all-to-all-done.3
  814.3 6.0 all-to-all-start.1
  820.5 7.3 add_convert_fusion
  828.6 33.5 %all-reduce = (f32[192]{0:T(256)}, f32[192]{0:T(256)}, f32[768]{0:T(1024)}, f32[768]{0:T(1024)}, f32[768]{0:T(1024)}, /*index=5*/f32[768]{0:T(1024)}, f32[768]{0:T(1024)}, f32[768]{0:T(1024)}, f32[768]{0:T(1024)}) all-reduce(f32[192]{0:T(256)S(1)} %reduce_sum.254, f32[192]{0:T(256)S(1)} %reduce_sum.256, ...), channel_id=1, replica_groups=mesh['dp'=8,'mp'=4] {'dp'}, use_global_device_ids=true, to_apply=%region_29.30 | all-reduce | flops 5760 | bytes 46080 | tf_op jit(solution)/shard_map/psum | solution.py:277
  868.1 29.1 %all-reduce.12.cloned.1.call-done = bf16[2048,768]{1,0:T(8,128)(2,1)} async-done(((bf16[2048,768]{1,0:T(8,128)(2,1)}), bf16[2048,768]{1,0:T(8,128)(2,1)}) %all-reduce.12.cloned.1.call-update) | async-done | bytes 3145744 | tf_op jit(solution)/shard_map/psum | solution.py:276
  897.3 7.0 convert_add_fusion
  (324 shorter events, 205.3 us)
Async XLA Ops:
  8.0 452.2 %copy-start = (bf16[1024,768]{1,0:T(8,128)(2,1)S(1)}, bf16[1024,768]{1,0:T(8,128)(2,1)}, u32[]{:S(2)}) copy-start(bf16[1024,768]{1,0:T(8,128)(2,1)} %param.28) | copy-start | bytes 4718596
  8.0 110.3 %copy-start.61 = (f32[192]{0:T(256)S(1)}, f32[192]{0:T(256)}, u32[]{:S(2)}) copy-start(f32[192]{0:T(256)} %param.32) | copy-start | bytes 2308
  8.0 311.1 %all-reduce.6.cloned.1.call-start = ((), (), s32[]{:S(2)}) async-start(), calls=%async_computation.5 | async-start | bytes 6291456 | tf_op jit(solution)/shard_map/psum | solution.py:190
  63.3 55.1 %copy-start.31 = (bf16[768,192]{1,0:T(8,128)(2,1)}, bf16[768,192]{1,0:T(8,128)(2,1)S(1)}, u32[]{:S(2)}) copy-start(bf16[768,192]{1,0:T(8,128)(2,1)S(1)} %all_gather.21) | copy-start | bytes 884740
  88.3 27.0 %copy-start.27 = (bf16[768,192]{1,0:T(8,128)(2,1)}, bf16[768,192]{1,0:T(8,128)(2,1)S(1)}, u32[]{:S(2)}) copy-start(bf16[768,192]{1,0:T(8,128)(2,1)S(1)} %all_gather.22) | copy-start | bytes 884740
  88.3 37.4 %copy-start.62 = (f32[192]{0:T(256)S(1)}, f32[192]{0:T(256)}, u32[]{:S(2)}) copy-start(f32[192]{0:T(256)} %param.33) | copy-start | bytes 2308
  218.8 104.5 %copy-start.7 = (bf16[2048,3,64]{0,2,1:T(8,128)(2,1)}, bf16[2048,3,64]{0,2,1:T(8,128)(2,1)S(1)}, u32[]{:S(2)}) copy-start(bf16[2048,3,64]{0,2,1:T(8,128)(2,1)S(1)} %get-tuple-element.554) | copy-start | bytes 2359300
  218.8 104.5 %copy-start.18 = (bf16[2048,3,64]{0,2,1:T(8,128)(2,1)}, bf16[2048,3,64]{0,2,1:T(8,128)(2,1)S(1)}, u32[]{:S(2)}) copy-start(bf16[2048,3,64]{0,2,1:T(8,128)(2,1)S(1)} %get-tuple-element.568) | copy-start | bytes 2359300
  218.8 100.3 %copy-start.38 = (f32[768]{0:T(1024)S(1)}, f32[768]{0:T(1024)}, u32[]{:S(2)}) copy-start(f32[768]{0:T(1024)} %param.35) | copy-start | bytes 9220
  225.0 101.5 %all-gather.3.cloned.1.call-start = ((), (), s32[]{:S(2)}) async-start(), calls=%async_computation.6 | async-start | bytes 1327104 | tf_op jit(solution)/shard_map/all_gather | solution.py:158
  225.6 121.4 %all-gather.5.cloned.1.call-start = ((), (), s32[]{:S(2)}) async-start(), calls=%async_computation.7 | async-start | bytes 1327104 | tf_op jit(solution)/shard_map/all_gather | solution.py:159
  226.2 196.2 %all-reduce.8.cloned.1.call-start = ((), (), s32[]{:S(2)}) async-start(), calls=%async_computation.8 | async-start | bytes 6291456 | tf_op jit(solution)/shard_map/psum | solution.py:196
  326.4 95.9 %copy-start.36 = (f32[2048]{0:T(1024)}, f32[2048]{0:T(1024)S(1)}, u32[]{:S(2)}) copy-start(f32[2048]{0:T(1024)S(1)} %add_rsqrt_fusion.1) | copy-start | bytes 24580
  347.0 75.3 %copy-start.39 = (f32[768]{0:T(1024)S(1)}, f32[768]{0:T(1024)}, u32[]{:S(2)}) copy-start(f32[768]{0:T(1024)} %param.35) | copy-start | bytes 9220
  347.0 75.3 %copy-start.42 = (f32[768]{0:T(1024)S(1)}, f32[768]{0:T(1024)}, u32[]{:S(2)}) copy-start(f32[768]{0:T(1024)} %param.36) | copy-start | bytes 9220
  347.1 75.3 %copy-start.50 = (f32[768]{0:T(1024)S(1)}, f32[768]{0:T(1024)}, u32[]{:S(2)}) copy-start(f32[768]{0:T(1024)} %param.41) | copy-start | bytes 9220
  347.1 75.3 %copy-start.52 = (f32[768]{0:T(1024)S(1)}, f32[768]{0:T(1024)}, u32[]{:S(2)}) copy-start(f32[768]{0:T(1024)} %param.37) | copy-start | bytes 9220
  428.7 64.0 %copy-start.64 = (s32[64]{0:T(128)S(1)}, s32[64]{0:T(128)}, u32[]{:S(2)}) copy-start(s32[64]{0:T(128)} %param.27) | copy-start | bytes 772
  460.9 42.1 %copy-start.35 = (f32[64,1024]{1,0:T(8,128)}, f32[64,1024]{1,0:T(8,128)S(1)}, u32[]{:S(2)}) copy-start(f32[64,1024]{1,0:T(8,128)S(1)} %get-tuple-element.313) | copy-start | bytes 786436
  478.3 23.8 %copy-start.54 = (f32[64]{0:T(128)}, f32[64]{0:T(128)S(1)}, u32[]{:S(2)}) copy-start(f32[64]{0:T(128)S(1)} %pmax.7) | copy-start | bytes 772
  492.6 9.5 %copy-start.65 = (f32[64]{0:T(128)}, f32[64]{0:T(128)S(1)}, u32[]{:S(2)}) copy-start(f32[64]{0:T(128)S(1)} %psum.100) | copy-start | bytes 772
  493.7 9.3 %all-to-all-start = ((bf16[8,8,768]{2,1,0:T(8,128)(2,1)}), bf16[8,8,768]{2,1,0:T(8,128)(2,1)S(1)}, u32[]{:S(2)}, u32[]{:S(2)}) async-start(bf16[8,8,768]{2,1,0:T(8,128)(2,1)} %fusion.75), calls=%async_computation | async-start | bytes 196608 | tf_op jit(solution)/shard_map/all_to_all | solution.py:20
  497.1 118.6 %all-reduce.10.cloned.1.call-start = ((), (), s32[]{:S(2)}) async-start(), calls=%async_computation.9 | async-start | bytes 6291456 | tf_op jit(solution)/shard_map/psum | solution.py:228
  503.0 13.4 %slice-start = ((s8[6291456]{0:T(1024)(128)(4,1)}), s8[2097152]{0:T(1024)(128)(4,1)S(1)}, s32[]{:S(2)}) async-start(s8[6291456]{0:T(1024)(128)(4,1)} %bitcast.193), calls=%async_computation.11 | async-start | bytes 4194304
  509.2 9.8 %slice-start.2 = ((s8[6291456]{0:T(1024)(128)(4,1)}), s8[4194304]{0:T(1024)(128)(4,1)S(1)}, s32[]{:S(2)}) async-start(s8[6291456]{0:T(1024)(128)(4,1)} %bitcast.215), calls=%async_computation.13 | async-start | bytes 8388608
  518.9 9.5 %copy-start.17 = (f32[2048,768]{1,0:T(8,128)}, f32[2048,768]{1,0:T(8,128)S(1)}, u32[]{:S(2)}) copy-start(f32[2048,768]{1,0:T(8,128)S(1)} %subtract_multiply_fusion.1) | copy-start | bytes 18874372
  519.2 10.9 %copy-start.58 = (bf16[768,768]{1,0:T(8,128)(2,1)S(1)}, bf16[768,768]{1,0:T(8,128)(2,1)}, u32[]{:S(2)}) copy-start(bf16[768,768]{1,0:T(8,128)(2,1)} %all-gather.3.cloned.1.call-done) | copy-start | bytes 3538948
  534.1 12.3 %copy-start.4 = (bf16[2048,768]{1,0:T(8,128)(2,1)S(1)}, bf16[2048,768]{1,0:T(8,128)(2,1)}, u32[]{:S(2)}) copy-start(bf16[2048,768]{1,0:T(8,128)(2,1)} %param.24) | copy-start | bytes 9437188
  541.8 225.4 %all-to-all-start.4 = ((bf16[8,768,96]{1,2,0:T(8,128)(2,1)}), bf16[8,768,96]{1,2,0:T(8,128)(2,1)}, u32[]{:S(2)}, u32[]{:S(2)}) async-start(bf16[8,768,96]{1,2,0:T(8,128)(2,1)} %bitcast.211), calls=%async_computation.4 | async-start | bytes 2359296 | tf_op jit(solution)/shard_map/all_to_all | solution.py:20
  615.7 9.2 %copy-start.12 = (bf16[2048,768]{1,0:T(8,128)(2,1)S(1)}, bf16[2048,768]{1,0:T(8,128)(2,1)}, u32[]{:S(2)}) copy-start(bf16[2048,768]{1,0:T(8,128)(2,1)} %all-reduce.6.cloned.1.call-done) | copy-start | bytes 9437188
  615.7 9.2 %copy-start.19 = (bf16[2048,768]{1,0:T(8,128)(2,1)S(1)}, bf16[2048,768]{1,0:T(8,128)(2,1)}, u32[]{:S(2)}) copy-start(bf16[2048,768]{1,0:T(8,128)(2,1)} %all-reduce.10.cloned.1.call-done) | copy-start | bytes 9437188
  615.7 9.2 %copy-start.37 = (f32[2048]{0:T(1024)S(1)}, f32[2048]{0:T(1024)}, u32[]{:S(2)}) copy-start(f32[2048]{0:T(1024)} %copy-done.36) | copy-start | bytes 24580
  615.7 9.2 %copy-start.40 = (f32[768]{0:T(1024)S(1)}, f32[768]{0:T(1024)}, u32[]{:S(2)}) copy-start(f32[768]{0:T(1024)} %param.35) | copy-start | bytes 9220
  615.7 9.2 %copy-start.43 = (f32[768]{0:T(1024)S(1)}, f32[768]{0:T(1024)}, u32[]{:S(2)}) copy-start(f32[768]{0:T(1024)} %param.36) | copy-start | bytes 9220
  657.0 10.6 %copy-start.26 = (bf16[4,512,3,64]{1,3,2,0:T(8,128)(2,1)S(1)}, bf16[4,512,3,64]{1,3,2,0:T(8,128)(2,1)}, u32[]{:S(2)}) copy-start(bf16[4,512,3,64]{1,3,2,0:T(8,128)(2,1)} %copy-done.25) | copy-start | bytes 2359300 | tf_op jit(solution)/shard_map/while
  690.1 10.6 %copy-start.26 = (bf16[4,512,3,64]{1,3,2,0:T(8,128)(2,1)S(1)}, bf16[4,512,3,64]{1,3,2,0:T(8,128)(2,1)}, u32[]{:S(2)}) copy-start(bf16[4,512,3,64]{1,3,2,0:T(8,128)(2,1)} %copy-done.25) | copy-start | bytes 2359300 | tf_op jit(solution)/shard_map/while
  723.2 10.6 %copy-start.26 = (bf16[4,512,3,64]{1,3,2,0:T(8,128)(2,1)S(1)}, bf16[4,512,3,64]{1,3,2,0:T(8,128)(2,1)}, u32[]{:S(2)}) copy-start(bf16[4,512,3,64]{1,3,2,0:T(8,128)(2,1)} %copy-done.25) | copy-start | bytes 2359300 | tf_op jit(solution)/shard_map/while
  756.3 10.6 %copy-start.26 = (bf16[4,512,3,64]{1,3,2,0:T(8,128)(2,1)S(1)}, bf16[4,512,3,64]{1,3,2,0:T(8,128)(2,1)}, u32[]{:S(2)}) copy-start(bf16[4,512,3,64]{1,3,2,0:T(8,128)(2,1)} %copy-done.25) | copy-start | bytes 2359300 | tf_op jit(solution)/shard_map/while
  767.1 32.9 %all-to-all-start.3 = ((bf16[8,96,768]{2,1,0:T(8,128)(2,1)}), bf16[8,96,768]{2,1,0:T(8,128)(2,1)}, u32[]{:S(2)}, u32[]{:S(2)}) async-start(bf16[8,96,768]{2,1,0:T(8,128)(2,1)} %bitcast.210), calls=%async_computation.3 | async-start | bytes 2359296 | tf_op jit(solution)/shard_map/all_to_all | solution.py:20
  788.4 16.4 %copy-start.34 = (bf16[768,192]{0,1:T(8,128)(2,1)S(1)}, bf16[768,192]{0,1:T(8,128)(2,1)}, u32[]{:S(2)}) copy-start(bf16[768,192]{0,1:T(8,128)(2,1)} %fusion.73) | copy-start | bytes 884740
  788.4 18.8 %copy-start.21 = (bf16[24,8,4,512]{3,1,2,0:T(8,128)(2,1)S(1)}, bf16[24,8,4,512]{3,1,2,0:T(8,128)(2,1)}, u32[]{:S(2)}) copy-start(bf16[24,8,4,512]{3,1,2,0:T(8,128)(2,1)} %copy-done.20) | copy-start | bytes 2359300
  788.4 18.8 %copy-start.32 = (bf16[768,192]{1,0:T(8,128)(2,1)S(1)}, bf16[768,192]{1,0:T(8,128)(2,1)}, u32[]{:S(2)}) copy-start(bf16[768,192]{1,0:T(8,128)(2,1)} %copy-done.31) | copy-start | bytes 884740
  800.1 14.2 %all-to-all-start.2 = ((bf16[8,192,96]{2,1,0:T(8,128)(2,1)}), bf16[8,192,96]{2,1,0:T(8,128)(2,1)S(1)}, u32[]{:S(2)}, u32[]{:S(2)}) async-start(bf16[8,192,96]{2,1,0:T(8,128)(2,1)} %bitcast.126), calls=%async_computation.2 | async-start | bytes 786432 | tf_op jit(solution)/shard_map/all_to_all | solution.py:20
  807.2 13.2 %copy-start.23 = (bf16[2048,3,64]{0,2,1:T(8,128)(2,1)S(1)}, bf16[2048,3,64]{0,2,1:T(8,128)(2,1)}, u32[]{:S(2)}) copy-start(bf16[2048,3,64]{0,2,1:T(8,128)(2,1)} %copy-done.22) | copy-start | bytes 2359300
  807.2 13.2 %copy-start.33 = (bf16[768,192]{1,0:T(8,128)(2,1)S(1)}, bf16[768,192]{1,0:T(8,128)(2,1)}, u32[]{:S(2)}) copy-start(bf16[768,192]{1,0:T(8,128)(2,1)} %all_gather.23) | copy-start | bytes 884740
  814.3 52.9 %all-to-all-start.1 = ((bf16[8,96,576]{2,1,0:T(8,128)(2,1)}), bf16[8,96,576]{2,1,0:T(8,128)(2,1)S(1)}, u32[]{:S(2)}, u32[]{:S(2)}) async-start(bf16[8,96,576]{2,1,0:T(8,128)(2,1)} %bitcast.19), calls=%async_computation.1 | async-start | bytes 1966080 | tf_op jit(solution)/shard_map/all_to_all | solution.py:20
  820.4 76.9 %all-reduce.12.cloned.1.call-start = ((), (), s32[]{:S(2)}) async-start(), calls=%async_computation.10 | async-start | bytes 6291456 | tf_op jit(solution)/shard_map/psum | solution.py:276
  867.4 36.9 %copy-start.1 = (bf16[1024,768]{1,0:T(8,128)(2,1)S(1)}, bf16[1024,768]{1,0:T(8,128)(2,1)}, u32[]{:S(2)}) copy-start(bf16[1024,768]{1,0:T(8,128)(2,1)} %param.28) | copy-start | bytes 4718596
  (59 other events, 287.9 us)
Sparse Core Ops, SparseCore 0:
  225.1 93.9 all-reduce.5
  353.8 68.5 all-reduce.7
  534.3 81.4 all-reduce.9
  827.9 69.2 all-reduce.11
Sparse Core Ops, SparseCore 1:
  227.7 65.4 all-gather.2
  295.2 39.9 all-gather.4
where the time goes:
time: 924 us; the launch traced here: 912 us
  waiting for transfers between devices  265 us (29%)
  matrix products  246 us (27%)
  blocking collectives  193 us (21%)
  other arithmetic  131 us (14%)
  local copies, waits for them, and re-layouts  35.2 us (4%)
  starting transfers between devices  24.6 us (3%)
  between operations  16.5 us (2%)
    psum x1, waiting for transfers between devices, body(): lax.psum(attn_part, 'mp').astype(jnp.float32)  92.7 us
    psum x1, waiting for transfers between devices, body(): lax.psum(ffn_part, 'mp').astype(jnp.float32)  68.6 us
    psum x1, waiting for transfers between devices, body(): grad_one = grad_hidden_two + lax.psum(normed_part, 'mp').astype(jnp.float32)  61.8 us
    dot_general x8, matrix products, block_scores(): jnp.einsum('bhe,mhe->hbm', query_block, key_rows, preferred_element_type=...  38.8 us
    psum x1, blocking collectives, body(): lax.psum((grad_bias_query, grad_bias_value, grad_bias_out, grad_gain_one,...  33.5 us
    dot_general x7, matrix products, contract_cols(): lax.dot_general(left, right, (((1,), (1,)), ((), ())), preferred_element_...  29.8 us
    psum x1, waiting for transfers between devices, body(): lax.psum(input_part, 'mp').astype(jnp.float32)  29.1 us
    reduce_sum x4, other arithmetic, attend_block(): row_total = jnp.sum(expo, axis=-1, keepdims=True)  27.3 us
  transfers between devices with their start and end apart: 11, of which 7 were waited for; matrix products, arithmetic and copies ran while one was open for 26% of the time, Pallas kernels for 0%

commit v1 on v0

v1 whole, which is shorter than its diff:
```python
import functools

import jax
import jax.numpy as jnp
from jax import lax
from jax.experimental import pallas as pl
from jax.experimental.pallas import tpu as pltpu
from jax.sharding import PartitionSpec as P

HEAD = 64
LONGEST = 400
QUERY_BLOCK = 256
EPSILON = 1e-05
NEGATIVE = -1e30
LANES = 128
KEY_AT = ((0, 0), (0, 1), (1, 0))
VALUE_AT = ((1, 1), (2, 0), (2, 1))
QUERY_AT = ((0, 0), (0, 1), (1, 0))
CONTEXT_AT = ((0, 1), (1, 0), (1, 1))
F32, BF16 = jnp.float32, jnp.bfloat16
VMEM, ANY, SMEM = pltpu.VMEM, pl.ANY, pltpu.SMEM


def dot(left, right, left_dim=1, right_dim=0):
    return lax.dot_general(
        left, right, (((left_dim,), (right_dim,)), ((), ())), preferred_element_type=F32
    )


def tile(index, count=1):
    return slice(index * LANES, (index + count) * LANES)


def half_mask(half, dtype):
    lane = lax.broadcasted_iota(jnp.int32, (1, LANES), 1)
    return jnp.where((lane >= HEAD) == (half == 1), 1.0, 0.0).astype(dtype)


def norm_stats(hidden):
    centred = hidden - jnp.mean(hidden, axis=-1, keepdims=True)
    factor = lax.rsqrt(jnp.mean(centred * centred, axis=-1, keepdims=True) + EPSILON)
    return centred * factor, factor


def norm_back(grad_out, normed, factor, gain):
    scaled = grad_out * gain
    inner = jnp.mean(scaled * normed, axis=-1, keepdims=True)
    return factor * (scaled - jnp.mean(scaled, axis=-1, keepdims=True) - normed * inner)


def gelu_and_slope(a):
    size = jnp.abs(a)
    t = 1.0 / (1.0 + (0.3275911 * 0.7071067811865476) * size)
    bell = jnp.exp(-0.5 * a * a)
    poly = t * (
        0.127414796 + t * (-0.142248368 + t * (0.7107068705 + t * (-0.7265760135 + t * 0.5307027145)))
    )
    tail = poly * bell
    phi = jnp.where(a >= 0.0, 1.0 - tail, tail)
    return a * phi, phi + a * bell * 0.3989422804014327


class Sizes:
    def __init__(self, length, width, groups):
        self.length, self.width, self.groups = length, width, groups
        self.own = length // groups
        self.window = min(length, self.own + 2 * LONGEST)
        self.block = min(QUERY_BLOCK, self.own)
        self.blocks = self.own // self.block
        self.keys = min(length, self.block + 2 * LONGEST)

    def window_start(self, me):
        return jnp.clip(self.own * me - LONGEST, 0, self.length - self.window)

    def own_offset(self, me):
        return pl.multiple_of(self.own * me - self.window_start(me), 16)

    def key_start(self, me, block):
        first = self.own * me + block * self.block
        return jnp.clip(first - LONGEST, 0, self.length - self.keys)

    def key_offset(self, me, block):
        return pl.multiple_of(self.key_start(me, block) - self.window_start(me), 16)


def document_bounds(lens, places):
    start = jnp.zeros_like(places)
    end = jnp.zeros_like(places)
    total = jnp.int32(0)
    for d in range(lens.shape[1]):
        count = lens[0, d]
        end = end + jnp.where(places >= total, count, 0)
        total = total + count
        start = start + jnp.where(places >= total, count, 0)
    return start, end


def fill_mask(sizes, me, lens, bias):
    for b in range(sizes.blocks):
        places = (
            sizes.own * me
            + b * sizes.block
            + lax.broadcasted_iota(jnp.int32, (1, sizes.block), 1)
        )
        start, end = document_bounds(lens, places)
        keys = sizes.key_start(me, b) + lax.broadcasted_iota(
            jnp.int32, (sizes.keys, sizes.block), 0
        )
        bias[b] = jnp.where((keys >= start) & (keys < end), 0.0, NEGATIVE)


def start_rows(sizes, me, lens):
    docs = lens.shape[1]
    row = lax.broadcasted_iota(jnp.int32, (docs, sizes.own), 0)
    place = sizes.own * me + lax.broadcasted_iota(jnp.int32, (docs, sizes.own), 1)
    picked = jnp.zeros((docs, sizes.own), F32)
    total = jnp.int32(0)
    for d in range(docs):
        picked = jnp.where((row == d) & (place == total), 1.0, picked)
        total = total + lens[0, d]
    return picked


def project(sizes, me, tokens, w_attn, biases, kv, q):
    cut = sizes.window // 2
    own = pl.ds(sizes.own_offset(me), sizes.own)

    @pl.loop(0, sizes.groups)
    def _(g):
        for part in range(2):
            rows = pl.ds(part * cut, cut)
            made = dot(tokens[rows, :], w_attn[g, :, tile(0, 3)]) + biases[g, :, tile(0, 3)]
            kv[g, rows, :] = made.astype(BF16)
        made = dot(tokens[own, :], w_attn[g, :, tile(3, 2)]) + biases[g, :, tile(3, 2)]
        q[g] = made.astype(BF16) * jnp.asarray(HEAD**-0.5, BF16)


def attend(sizes, me, kv, q, bias, lse, ctx):
    @pl.loop(0, sizes.groups)
    def _(g):
        @pl.loop(0, sizes.blocks)
        def _(b):
            keys = pl.ds(sizes.key_offset(me, b), sizes.keys)
            rows = pl.ds(pl.multiple_of(b * sizes.block, sizes.block), sizes.block)
            made = [jnp.zeros((HEAD, sizes.block), F32)]
            logs = []
            for j in range(3):
                kt, kh = KEY_AT[j]
                vt, vh = VALUE_AT[j]
                qt, _ = QUERY_AT[j]
                query = q[g, rows, tile(qt)] * half_mask(kh, BF16)
                s = dot(kv[g, keys, tile(kt)], query, 1, 1) + bias[b]
                peak = jnp.max(s, axis=0, keepdims=True)
                e = jnp.exp(s - peak)
                total = jnp.sum(e, axis=0, keepdims=True)
                mixed = dot(kv[g, keys, tile(vt)], e.astype(BF16), 0, 0)
                made.append(mixed[vh * HEAD : (vh + 1) * HEAD] / total)
                logs.append(peak + jnp.log(total))
            ctx[g, rows, :] = jnp.concatenate(made, axis=0).T.astype(BF16)
            for j in range(3):
                lse[g, b, j : j + 1, :] = logs[j]


def attend_back(sizes, me, kv, q, bias, lse, ctx, dctx, delta, dkv, dq):
    lane = lax.broadcasted_iota(jnp.int32, (8, 2 * LANES), 1)
    row = lax.broadcasted_iota(jnp.int32, (8, 2 * LANES), 0)
    pick = jnp.where(lane // HEAD == row + 1, 1.0, 0.0).astype(BF16)

    @pl.loop(0, sizes.groups)
    def _(g):
        product = dctx[g].astype(F32) * ctx[g].astype(F32)
        high = product.astype(BF16)
        low = (product - high.astype(F32)).astype(BF16)
        delta[...] = dot(pick, high, 1, 1) + dot(pick, low, 1, 1)
        dkv[g] = jnp.zeros_like(dkv[g])

        for b in range(sizes.blocks):
            keys = pl.ds(sizes.key_offset(me, b), sizes.keys)
            rows = slice(b * sizes.block, (b + 1) * sizes.block)
            made = []
            for j in range(3):
                kt, kh = KEY_AT[j]
                vt, vh = VALUE_AT[j]
                qt, _ = QUERY_AT[j]
                ct, _ = CONTEXT_AT[j]
                query = q[g, rows, tile(qt)] * half_mask(kh, BF16)
                grad = dctx[g, rows, tile(ct)] * half_mask(vh, BF16)
                s = dot(kv[g, keys, tile(kt)], query, 1, 1) + bias[b]
                p = jnp.exp(s - lse[g, b, j : j + 1, :])
                dp = dot(kv[g, keys, tile(vt)], grad, 1, 1)
                ds = (p * (dp - delta[j : j + 1, rows])).astype(BF16)
                dkv[g, keys, tile(kt)] += dot(ds, query)
                dkv[g, keys, tile(vt)] += dot(p.astype(BF16), grad)
                back = dot(kv[g, keys, tile(kt)], ds, 0, 0)
                made.append(back[kh * HEAD : (kh + 1) * HEAD] * HEAD**-0.5)
            made.append(jnp.zeros((HEAD, sizes.block), F32))
            dq[g, rows, :] = jnp.concatenate(made, axis=0).T


def forward_kernel(
    sizes,
    lens,
    tokens,
    weights,
    biases,
    b_out,
    gain_1,
    shift_1,
    b_down,
    gain_2,
    shift_2,
    encoded,
    cls,
    n_1,
    r_1,
    n_2,
    r_2,
    z,
    slope,
    kv,
    q,
    lse,
    ctx,
    x,
    w,
    bias,
    hidden,
    sems,
):
    me = lax.axis_index("mp")
    first = pl.multiple_of(sizes.window_start(me), 16)
    load = pltpu.make_async_copy(tokens.at[pl.ds(first, sizes.window)], x, sems.at[3])
    load.start()
    loads = []
    for s in range(3):
        loads.append(pltpu.make_async_copy(weights.at[:, s], w.at[s], sems.at[s]))
        loads[-1].start()
    fill_mask(sizes, me, lens, bias)
    load.wait()
    loads[0].wait()
    project(sizes, me, x, w.at[0], biases, kv, q)
    attend(sizes, me, kv, q, bias, lse, ctx)

    own = pl.ds(sizes.own_offset(me), sizes.own)
    hidden[...] = x[own, :].astype(F32) + b_out[...]
    for g in range(sizes.groups):
        hidden[...] += dot(ctx[g], w[0, g, :, tile(4, 2)], 1, 1)
    normed, factor = norm_stats(hidden[...])
    n_1[...] = normed
    r_1[...] = factor
    y_1 = normed * gain_1[...] + shift_1[...]
    hidden[...] = y_1 + b_down[...]
    encoded[...] = y_1.astype(BF16)
    loads[1].wait()
    loads[2].wait()

    @pl.loop(0, sizes.groups)
    def _(g):
        a = dot(encoded[...], w[1, g]) + biases[g, :, 5 * LANES :]
        out, grad = gelu_and_slope(a)
        z[g] = out.astype(BF16)
        slope[g] = grad.astype(BF16)
        hidden[...] += dot(z[g], w[2, g], 1, 1)

    normed, factor = norm_stats(hidden[...])
    n_2[...] = normed
    r_2[...] = factor
    y_2 = (normed * gain_2[...] + shift_2[...]).astype(BF16)
    encoded[...] = y_2
    cls[...] = dot(start_rows(sizes, me, lens).astype(BF16), y_2)


def backward_kernel(
    sizes,
    lens,
    cotangent,
    dcls,
    weights,
    gain_1,
    shift_1,
    gain_2,
    n_1,
    r_1,
    n_2,
    r_2,
    z,
    slope,
    kv,
    q,
    lse,
    ctx,
    dh_1,
    dkv,
    dq,
    grads,
    grads_out,
    small,
    w_attn,
    w_up,
    w_down,
    cot,
    dh,
    low,
    other,
    turned,
    stage,
    dctx,
    delta,
    bias,
    sems,
    out_sems,
):
    me = lax.axis_index("mp")
    load_cot = pltpu.make_async_copy(
        cotangent.at[pl.ds(pl.multiple_of(sizes.own * me, 16), sizes.own)], cot, sems.at[3]
    )
    load_cot.start()
    loads = []
    for s, buffer in ((2, w_down), (1, w_up), (0, w_attn)):
        loads.append(pltpu.make_async_copy(weights.at[:, s], buffer, sems.at[s]))
        loads[-1].start()
    fill_mask(sizes, me, lens, bias)
    picked = start_rows(sizes, me, lens).astype(BF16)
    high = dcls[...].astype(BF16)
    low_part = (dcls[...] - high.astype(F32)).astype(BF16)
    load_cot.wait()
    dy = cot[...].astype(F32) + dot(picked, high, 0, 0) + dot(picked, low_part, 0, 0)
    small[0:1, :] = jnp.sum(dy * n_2[...], axis=0, keepdims=True)
    small[1:2, :] = jnp.sum(dy, axis=0, keepdims=True)
    grad = norm_back(dy, n_2[...], r_2[...], gain_2[...])
    small[2:3, :] = jnp.sum(grad, axis=0, keepdims=True)
    dh[...] = grad
    low[...] = grad.astype(BF16)
    turned[0] = grad.T.astype(BF16)
    y_1 = n_1[...] * gain_1[...] + shift_1[...]
    other[...] = y_1.astype(BF16)
    turned[1] = y_1.T.astype(BF16)
    for load in loads:
        load.wait()

    def out_copy(section, g, slot):
        return pltpu.make_async_copy(
            stage.at[slot], grads.at[section, g], out_sems.at[slot]
        )

    @pl.loop(0, sizes.groups)
    def _(g):
        @pl.when(g > 0)
        def _():
            out_copy(1, 0, 0).wait()
            out_copy(1, 0, 1).wait()

        stage[1] = dot(turned[0], z[g]).astype(BF16)
        out_copy(1, g, 1).start()
        da = dot(low[...], w_down[g]) * slope[g].astype(F32)
        small[pl.ds(8 + g, 1), :] = jnp.sum(da, axis=0, keepdims=True)
        da_low = da.astype(BF16)
        stage[0] = dot(turned[1], da_low).astype(BF16)
        out_copy(0, g, 0).start()
        dh[...] += dot(da_low, w_up[g], 1, 1)

    dy = dh[...]
    small[3:4, :] = jnp.sum(dy * n_1[...], axis=0, keepdims=True)
    small[4:5, :] = jnp.sum(dy, axis=0, keepdims=True)
    grad = norm_back(dy, n_1[...], r_1[...], gain_1[...])
    small[5:6, :] = jnp.sum(grad, axis=0, keepdims=True)
    small[6:8, :] = jnp.zeros_like(small[6:8, :])
    small[12:16, :] = jnp.zeros_like(small[12:16, :])
    dh_1[...] = grad
    low[...] = grad.astype(BF16)
    turned[0] = grad.T.astype(BF16)

    @pl.loop(0, sizes.groups)
    def _(g):
        dctx[g] = dot(low[...], w_attn[g, :, tile(4, 2)]).astype(BF16)
        grads_out[g] = dot(turned[0], ctx[g])

    attend_back(sizes, me, kv, q, bias, lse, ctx, dctx, delta, dkv, dq)
    out_copy(1, 0, 0).wait()
    out_copy(1, 0, 1).wait()


def input_kernel(sizes, tokens, weights, dkv, dq, dh_1, grads_out, token_grad, grads, small, turned, low):
    turned[...] = tokens[...].astype(F32).T.astype(BF16)
    total = dh_1[...]
    for g in range(sizes.groups):
        small[g, :, tile(0, 3)] = jnp.sum(dkv[g], axis=0, keepdims=True)
        small[g, :, tile(3, 2)] = jnp.sum(dq[g], axis=0, keepdims=True)
        low[:, tile(0, 3)] = dkv[g].astype(BF16)
        low[:, tile(3, 2)] = dq[g].astype(BF16)
        total = total + dot(low[...], weights[g, :, tile(0, 5)], 1, 1)
        made = dot(turned[...], low[...])
        grads[g, :, tile(0, 4)] = made[:, tile(0, 4)].astype(BF16)
        grads[g, :, tile(4)] = (made[:, tile(4)] + grads_out[g, :, tile(0)]).astype(BF16)
        grads[g, :, tile(5)] = grads_out[g, :, tile(1)].astype(BF16)
    token_grad[...] = total.astype(BF16)


def specs(*spaces):
    return [pl.BlockSpec(memory_space=s) for s in spaces]


def params(**more):
    return pltpu.CompilerParams(vmem_limit_bytes=62 * 2**20, **more)


def run_forward(sizes, lengths, tokens, weights, biases, rows):
    own, width, groups = sizes.own, sizes.width, sizes.groups
    docs = lengths.shape[1]
    shape = jax.ShapeDtypeStruct
    outs = (
        shape((own, width), BF16),
        shape((docs, width), F32),
        shape((own, width), F32),
        shape((own, 1), F32),
        shape((own, width), F32),
        shape((own, 1), F32),
        shape((groups, own, width), BF16),
        shape((groups, own, width), BF16),
        shape((groups, sizes.window, 3 * LANES), BF16),
        shape((groups, own, 2 * LANES), BF16),
        shape((groups, sizes.blocks, 8, sizes.block), F32),
        shape((groups, own, 2 * LANES), BF16),
    )
    return pl.pallas_call(
        functools.partial(forward_kernel, sizes),
        out_shape=outs,
        in_specs=specs(SMEM, ANY, ANY, *[VMEM] * 7),
        out_specs=specs(*[VMEM] * len(outs)),
        scratch_shapes=[
            pltpu.VMEM((sizes.window, width), BF16),
            pltpu.VMEM((3, groups, width, width), BF16),
            pltpu.VMEM((sizes.blocks, sizes.keys, sizes.block), F32),
            pltpu.VMEM((own, width), F32),
            pltpu.SemaphoreType.DMA((4,)),
        ],
        compiler_params=params(),
        name="forward",
    )(lengths, tokens, weights, biases, *rows)


def run_backward(sizes, lengths, cotangent, dcls, weights, gain_1, shift_1, gain_2, saved):
    own, width, groups = sizes.own, sizes.width, sizes.groups
    shape = jax.ShapeDtypeStruct
    outs = (
        shape((own, width), F32),
        shape((groups, sizes.window, 3 * LANES), F32),
        shape((groups, own, 2 * LANES), F32),
        shape((2, groups, width, width), BF16),
        shape((groups, width, 2 * LANES), F32),
        shape((16, width), F32),
    )
    return pl.pallas_call(
        functools.partial(backward_kernel, sizes),
        out_shape=outs,
        in_specs=specs(SMEM, ANY, VMEM, ANY, *[VMEM] * (3 + len(saved))),
        out_specs=specs(VMEM, VMEM, VMEM, ANY, VMEM, VMEM),
        scratch_shapes=[
            pltpu.VMEM((groups, width, width), BF16),
            pltpu.VMEM((groups, width, width), BF16),
            pltpu.VMEM((groups, width, width), BF16),
            pltpu.VMEM((own, width), BF16),
            pltpu.VMEM((own, width), F32),
            pltpu.VMEM((own, width), BF16),
            pltpu.VMEM((own, width), BF16),
            pltpu.VMEM((2, width, own), BF16),
            pltpu.VMEM((2, width, width), BF16),
            pltpu.VMEM((groups, own, 2 * LANES), BF16),
            pltpu.VMEM((8, own), F32),
            pltpu.VMEM((sizes.blocks, sizes.keys, sizes.block), F32),
            pltpu.SemaphoreType.DMA((4,)),
            pltpu.SemaphoreType.DMA((2,)),
        ],
        compiler_params=params(),
        name="backward",
    )(lengths, cotangent, dcls, weights, gain_1, shift_1, gain_2, *saved)


def run_input(sizes, own_tokens, w_attn, dkv, dq, dh_1, grads_out):
    own, width, groups = sizes.own, sizes.width, sizes.groups
    shape = jax.ShapeDtypeStruct
    outs = (
        shape((own, width), BF16),
        shape((groups, width, width), BF16),
        shape((groups, 1, 5 * LANES), F32),
    )
    return pl.pallas_call(
        functools.partial(input_kernel, sizes),
        out_shape=outs,
        in_specs=specs(*[VMEM] * 6),
        out_specs=specs(*[VMEM] * 3),
        scratch_shapes=[pltpu.VMEM((width, own), BF16), pltpu.VMEM((own, 5 * LANES), BF16)],
        compiler_params=params(),
        name="inputs",
    )(own_tokens, w_attn, dkv, dq, dh_1, grads_out)


def cut_along(array, dim, devices):
    before, after = (array.shape[:dim], array.shape[dim + 1 :])
    return jnp.moveaxis(array.reshape(*before, devices, -1, *after), dim, 0)


def summed_on_arrival(array, axis, dim):
    pieces = cut_along(array, dim, lax.axis_size(axis))
    arrived = lax.all_to_all(pieces, axis, split_axis=0, concat_axis=0, tiled=True)
    return arrived.astype(F32).sum(axis=0)


def score(cls, passages, gold):
    all_first = lax.all_gather(cls, "dp", axis=0, tiled=True)
    table = dot(all_first, passages, 1, 1)
    peak = lax.pmax(jnp.max(table, axis=1), "dp")
    total = lax.psum(jnp.sum(jnp.exp(table - peak[:, None]), axis=1), "dp")
    own = cls.shape[0]
    lse = lax.dynamic_slice_in_dim(peak + jnp.log(total), lax.axis_index("dp") * own, own)
    soft = jnp.exp(table - peak[:, None]) / total[:, None]
    first = lax.axis_index("dp") * table.shape[1]
    columns = first + jnp.arange(table.shape[1], dtype=jnp.int32)
    target = (gold[:, None] == columns[None, :]).astype(F32)
    grad = dot((soft - target).astype(BF16), passages)
    return table, lse, summed_on_arrival(grad.astype(BF16), "dp", 0)


def body(
    tokens,
    cotangent,
    lengths,
    gold,
    passages,
    w_query,
    w_key,
    w_value,
    b_query,
    b_value,
    w_out,
    b_out,
    gain_attn,
    shift_attn,
    w_up,
    b_up,
    w_down,
    b_down,
    gain_ffn,
    shift_ffn,
):
    groups = lax.axis_size("mp")
    sizes = Sizes(tokens.shape[0], tokens.shape[1], groups)
    me = lax.axis_index("mp")
    head_cols = w_query.shape[1]
    packed = jnp.stack(
        [jnp.concatenate([w_key, w_value, w_query, w_out.T], axis=1), w_up, w_down.T]
    )
    whole = lax.all_gather(lax.all_gather(packed, "dp", axis=1, tiled=True), "mp", axis=0)
    zeros = jnp.zeros((head_cols,), F32)
    own_bias = jnp.concatenate([zeros, b_value, b_query, zeros[:HEAD], b_up])
    biases = lax.all_gather(own_bias[None], "mp", axis=0)
    rows = [r[None] for r in (b_out, gain_attn, shift_attn, b_down, gain_ffn, shift_ffn)]
    encoded, cls, *saved = run_forward(sizes, lengths, tokens, whole, biases, rows)
    cls = lax.psum(cls, "mp").astype(BF16)
    table, lse, dcls = score(cls, passages, gold)
    n_1, r_1, n_2, r_2, z, slope, kv, q, logs, ctx = saved
    dh_1, dkv, dq, grads_ffn, grads_out, small = run_backward(
        sizes, lengths, cotangent, dcls, whole, rows[1], rows[2], rows[4], saved
    )
    halo, own = LONGEST, sizes.own
    offset = own * me - sizes.window_start(me)
    to_left = lax.dynamic_slice_in_dim(dkv, offset - halo, halo, axis=1).astype(BF16)
    to_right = lax.dynamic_slice_in_dim(dkv, offset + own, halo, axis=1).astype(BF16)
    from_right = lax.ppermute(to_left, "mp", [(i, i - 1) for i in range(1, groups)])
    from_left = lax.ppermute(to_right, "mp", [(i, i + 1) for i in range(groups - 1)])
    dkv = lax.dynamic_slice_in_dim(dkv, offset, own, axis=1)
    dkv = dkv.at[:, own - halo :].add(from_right.astype(F32))
    dkv = dkv.at[:, :halo].add(from_left.astype(F32))
    own_tokens = lax.dynamic_slice_in_dim(tokens, own * me, own, axis=0)
    token_part, grads_attn, small_attn = run_input(
        sizes, own_tokens, whole[:, 0], dkv, dq, dh_1, grads_out
    )
    token_grad = lax.all_gather(token_part, "mp", axis=0, tiled=True).astype(F32)
    encoded = lax.all_gather(encoded, "mp", axis=0, tiled=True)
    grads = jnp.stack([grads_attn, grads_ffn[0], grads_ffn[1]])
    grads = summed_on_arrival(grads, "mp", 1)[:, 0].astype(BF16)
    grads = summed_on_arrival(grads, "dp", 1)
    small, small_attn = lax.psum((small, small_attn), ("dp", "mp"))
    mine = lax.dynamic_index_in_dim(small_attn[:, 0], me, 0, keepdims=False)
    up_bias = lax.dynamic_index_in_dim(small, 8 + me, 0, keepdims=False)
    c = head_cols
    return (
        table,
        lse,
        encoded,
        token_grad,
        grads[0, :, 2 * c : 3 * c],
        grads[0, :, :c],
        grads[0, :, c : 2 * c],
        mine[2 * c : 3 * c],
        mine[c : 2 * c],
        grads[0, :, 3 * c :].T,
        small[5],
        small[3],
        small[4],
        grads[1],
        up_bias,
        grads[2].T,
        small[2],
        small[0],
        small[1],
    )


def solution(mesh):
    by_dp, shared, cross = P("dp", None), P(), P("dp", "mp")
    return jax.shard_map(
        body,
        mesh=mesh,
        in_specs=(
            by_dp,
            by_dp,
            by_dp,
            shared,
            by_dp,
            cross,
            cross,
            cross,
            P("mp"),
            P("mp"),
            P("mp", "dp"),
            shared,
            shared,
            shared,
            cross,
            P("mp"),
            P("mp", "dp"),
            shared,
            shared,
            shared,
        ),
        out_specs=(
            P(None, "dp"),
            P("dp"),
            by_dp,
            by_dp,
            cross,
            cross,
            cross,
            P("mp"),
            P("mp"),
            P("mp", "dp"),
            shared,
            shared,
            shared,
            cross,
            P("mp"),
            P("mp", "dp"),
            shared,
            shared,
            shared,
        ),
        check_vma=False,
    )
```

time: 924 us -> 732 us (0.79); the launches traced: 912 us -> 729 us
  matrix products: 246 us -> 1.78 us
  Pallas kernels: 0 us -> 111 us
  other arithmetic: 131 us -> 35.2 us
  waiting for transfers between devices: 265 us -> 323 us
  blocking collectives: 193 us -> 172 us
  starting transfers between devices: 24.6 us -> 35.3 us
    psum x4 -> x0, waiting for transfers between devices: 252 us -> none  [the longest x1 92.7 us: body(): lax.psum(attn_part, 'mp').astype(jnp.float32)]
    dot_general x48 -> x2, matrix products: 246 us -> 1.78 us  [dot(): lax.dot_general(left, right, (((left_dim,), (right_dim,)), ((), ())), pre...]
    all_to_all x5 -> x3, waiting for transfers between devices: 12.1 us -> 172 us  [summed_on_arrival(): lax.all_to_all(pieces, axis, split_axis=0, concat_axis=0, tiled=True)]
    all_gather x2 -> x4, waiting for transfers between devices: 0.03 us -> 148 us  [the longest x1 81.8 us: body(): lax.all_gather(lax.all_gather(packed, 'dp', axis=1, tiled=True), 'mp', ax...]
    pallas_call x0 -> x3, Pallas kernels: none -> 111 us  [the longest x1 51.9 us: run_backward(): pl.pallas_call(functools.partial(backward_kernel, sizes), out_shape=outs,...]
    all_gather x5 -> x2, blocking collectives: 128 us -> 31.4 us  [the longest x1 24.4 us: score(): all_first = lax.all_gather(cls, 'dp', axis=0, tiled=True)]
    psum x2 -> x3, blocking collectives: 47.5 us -> 123 us  [the longest x1 98.5 us: body(): small, small_attn = lax.psum((small, small_attn), ('dp', 'mp'))]
    reduce_sum x20 -> x4, other arithmetic: 72.5 us -> 13.8 us  [the longest x3 13.6 us: summed_on_arrival(): return arrived.astype(F32).sum(axis=0)]
  transfers between devices with their start and end apart: 11 -> 9, of which waited for: 7 -> 5; matrix products, arithmetic and copies ran while one was open for 26% -> 5% of each run, Pallas kernels for 0% -> 0%
where the time goes in v1:
time: 732 us; the launch traced here: 729 us
  waiting for transfers between devices  323 us (44%)
  blocking collectives  172 us (23%)
  Pallas kernels  111 us (15%)
  local copies, waits for them, and re-layouts  37 us (5%)
  starting transfers between devices  35.3 us (5%)
  other arithmetic  35.2 us (5%)
  between operations  14.1 us (2%)
    all_to_all x3, waiting for transfers between devices, summed_on_arrival(): lax.all_to_all(pieces, axis, split_axis=0, concat_axis=0, tiled=True)  172 us
    psum x1, blocking collectives, body(): small, small_attn = lax.psum((small, small_attn), ('dp', 'mp'))  98.5 us
    all_gather x1, waiting for transfers between devices, body(): lax.all_gather(lax.all_gather(packed, 'dp', axis=1, tiled=True), 'mp', ax...  81.8 us
    all_gather x1, waiting for transfers between devices, body(): lax.all_gather(packed, 'dp', axis=1, tiled=True)  66.4 us
    pallas_call x1, Pallas kernels, run_backward(): pl.pallas_call(functools.partial(backward_kernel, sizes), out_shape=outs,...  51.9 us
    pallas_call x1, Pallas kernels, run_forward(): pl.pallas_call(functools.partial(forward_kernel, sizes), out_shape=outs,...  46.2 us
    all_gather x1, blocking collectives, score(): all_first = lax.all_gather(cls, 'dp', axis=0, tiled=True)  24.4 us
    pmax x1, blocking collectives, score(): peak = lax.pmax(jnp.max(table, axis=1), 'dp')  17.5 us
  transfers between devices with their start and end apart: 9, of which 5 were waited for; matrix products, arithmetic and copies ran while one was open for 5% of the time, Pallas kernels for 0%

profile of v1, /device:TPU:1, one launch (start us, length us, event | category | flops | bytes accessed | tf_op | source)
XLA Modules:
  0.0 729.5 jit_solution(3996959515002294866)
XLA Ops:
  7.3 1.0 copy.50
  8.3 1.0 maximum_bitcast_fusion.1
  9.3 1.8 pad_maximum_fusion
  11.2 66.4 %all-gather.8.cloned.1.call-done = bf16[3,768,768]{2,1,0:T(8,128)(2,1)} async-done(((bf16[3,96,768]{2,1,0:T(8,128)(2,1)}), bf16[3,768,768]{2,1,0:T(8,128)(2,1)}) %all-gather.8.cloned.1.call-update) | async-done | bytes 3538960 | tf_op jit(solution)/shard_map/all_gather | solution.py:553
  77.6 0.6 broadcast_in_dim.28.gain_1
  79.5 0.6 broadcast_in_dim.27.b_out
  81.2 7.0 all-gather.2.biases
  88.3 81.8 %all-gather.14.cloned.1.call-done = bf16[12,768,768]{2,1,0:T(8,128)(2,1)} async-done(((bf16[3,768,768]{2,1,0:T(8,128)(2,1)}), bf16[12,768,768]{2,1,0:T(8,128)(2,1)}) %all-gather.14.cloned.1.call-update) | async-done | bytes 14155792 | tf_op jit(solution)/shard_map/all_gather | solution.py:553
  170.1 46.2 %forward.1 = (bf16[512,768]{1,0:T(8,128)(2,1)}, f32[8,768]{1,0:T(8,128)}, f32[512,768]{1,0:T(8,128)}, f32[512,1]{1,0:T(8,128)}, f32[512,768]{1,0:T(8,128)}, /*in...) custom-call(s32[1,8]{1,0:T(1,128)} %lens.3, ...), custom_call_target="tpu_custom_call" | custom-call | tf_op jit(solution)/shard_map/forward/pallas_call | solution.py:425
  216.3 10.9 %psum.28 = bf16[8,768]{1,0:T(8,128)(2,1)S(1)} all-reduce(f32[8,768]{1,0:T(8,128)} %get-tuple-element.64), channel_id=1, replica_groups=mesh['dp'=8,'mp'=4] {'mp'}, use_global_device_ids=true, to_apply=%region_0.0 | all-reduce | flops 6144 | bytes 36864 | tf_op jit(solution)/shard_map/psum | solution.py:559
  227.2 24.4 %all_gather.25 = bf16[64,768]{1,0:T(8,128)(2,1)S(1)} all-gather(bf16[8,768]{1,0:T(8,128)(2,1)S(1)} %psum.28), channel_id=1, replica_groups=mesh['dp'=8,'mp'=4] {'dp'}, dimensions={0}, use_global_device_ids=true | all-gather | bytes 110592 | tf_op jit(solution)/shard_map/all_gather | solution.py:510
  251.5 0.7 fusion.7
  252.2 17.5 %pmax.7 = f32[64]{0:T(128)S(1)} all-reduce(f32[64]{0:T(128)S(1)} %get-tuple-element.180), channel_id=1, replica_groups=mesh['dp'=8,'mp'=4] {'dp'}, use_global_device_ids=true, to_apply=%region_2.0 | all-reduce | flops 64 | bytes 512 | tf_op jit(solution)/shard_map/pmax | solution.py:512
  269.9 13.7 %psum.29 = f32[64]{0:T(128)S(1)} all-reduce(f32[64]{0:T(128)S(1)} %fusion.2), channel_id=1, replica_groups=mesh['dp'=8,'mp'=4] {'dp'}, use_global_device_ids=true, to_apply=%region_4.0 | all-reduce | flops 64 | bytes 512 | tf_op jit(solution)/shard_map/psum | solution.py:513
  283.6 1.1 fusion.1
  284.7 3.5 all-to-all-start
  288.3 5.7 all-to-all-done
  294.0 0.6 convert_reduce_fusion.1.dcls
  294.6 51.9 %backward.1 = (f32[512,768]{1,0:T(8,128)}, f32[4,1312,384]{2,1,0:T(8,128)}, f32[4,512,256]{2,1,0:T(8,128)}, bf16[2,4,768,768]{3,2,1,0:T(8,128)(2,1)}, f32[4,768,256]{2,1,0:T(8,128)}, /*index=5*/f32[16,768]{1,0:T(8,128)}) custom-call(s32[1,8]{1,0:T(1,128)} %lens.3, bf16[2048,768]{1,0:T(8,128)(2,1)} %cotangent.1, f32[8,768]{1,0:T(8,128)} %convert_reduce_fusion.1.dcls, ...), custom_call_target="tpu_custom_call" | custom-call | tf_op jit(solution)/shard_map/backward/pallas_call | solution.py:453
  346.5 4.0 dynamic-slice_convert_fusion
  350.5 17.0 %collective-permute-start = (bf16[4,400,384]{2,1,0:T(8,128)(2,1)}, bf16[4,400,384]{2,1,0:T(8,128)(2,1)}, u32[]{:S(2)}, u32[]{:S(2)}) collective-permute-start(bf16[4,400,384]{2,1,0:T(8,128)(2,1)} %get-tuple-element.171), channel_id=1, source_target_pairs={{1,0},{2,1},{3,2},{5,4},{6,5},{7,6},{9,8},{10,9},{11,10},{13,12},{... | collective-permute-start | bytes 3686408 | tf_op jit(solution)/shard_map/ppermute | solution.py:569
  367.5 3.3 collective-permute-start.1
  370.8 2.1 constant_dynamic-slice_fusion.3.tokens
  373.0 5.2 slice_bitcast_fusion.weights
  378.1 1.2 copy-done.2
  379.4 1.9 constant_dynamic-slice_fusion.2
  381.3 2.1 collective-permute-done
  383.4 3.1 add_dynamic-update-slice_fusion
  386.5 3.3 fusion.dkv
  389.8 12.8 %inputs.1 = (bf16[512,768]{1,0:T(8,128)(2,1)}, bf16[4,768,768]{2,1,0:T(8,128)(2,1)}, f32[4,1,640]{2,1,0:T(1,128)}) custom-call(bf16[512,768]{1,0:T(8,128)(2,1)} %constant_dynamic-slice_fusion.3.tokens, bf16[4,768,768]{2,1,0:T(8,128)(2,1)} %slice_bitcast_fusion.weights, f32[4,512,384]{2,1,0:T(8,128)} %fusion.dkv, f32[4,512,256]{2,1,0:T(8,128)} %get-tuple-element.77.dq, ...), custom_call_target="tpu_custom_call" | custom-call | tf_op jit(solution)/shard_map/inputs/pallas_call | solution.py:487
  402.6 7.2 maximum_bitcast_fusion
  409.8 5.8 copy.52
  415.6 6.6 all-to-all-start.1
  422.3 0.7 all-gather.10.cloned.1.call-update
  423.0 166.1 %all-to-all-done.1 = bf16[4,3,1,768,768]{4,3,1,2,0:T(8,128)(2,1)} async-done(((bf16[4,3,1,768,768]{4,3,1,2,0:T(8,128)(2,1)}), bf16[4,3,1,768,768]{4,3,1,2,0:T(8,128)(2,1)}, u32[]{:S(2)}, u32[]{:S(2)}) %all-to-all-start.1) | async-done | bytes 14155808 | tf_op jit(solution)/shard_map/all_to_all | solution.py:505
  589.1 10.4 %reduce_sum.41 = bf16[3,768,768]{2,1,0:T(8,128)(2,1)} reduce(bf16[4,3,1,768,768]{4,3,1,2,0:T(8,128)(2,1)} %all-to-all-done.1, bf16[]{:T(256)} %constant.119.clone.1), dimensions={0,2}, to_apply=%region_6.7 | reduce | flops 5308416 | bytes 17694722 | tf_op jit(solution)/shard_map/reduce_sum | solution.py:506
  599.4 4.0 copy.53
  603.5 4.6 all-to-all-start.2
  608.7 0.6 dynamic_slice.25
  609.3 98.5 %all-reduce = (f32[4,1,640]{2,1,0:T(1,128)S(1)}, f32[16,768]{1,0:T(8,128)S(1)}) all-reduce(f32[4,1,640]{2,1,0:T(1,128)S(1)} %copy-done.5, f32[16,768]{1,0:T(8,128)S(1)} %copy-done.4), channel_id=1, replica_groups=mesh['dp'=8,'mp'=4] {'dp','mp'}, use_global_device_ids=true, to_apply=%region_8.9 | all-reduce | flops 14848 | bytes 118784 | tf_op jit(solution)/shard_map/psum | solution.py:583
  707.8 0.6 constant_dynamic-slice_fusion.1
  708.4 0.7 slice_reduce_fusion
  709.1 5.1 convert_element_type.48
  714.2 2.6 convert_reduce_fusion
  716.7 0.8 slice_bitcast_fusion.1
  717.6 0.7 slice_bitcast_fusion.3
  718.3 0.7 copy.54
  719.1 3.9 copy.59
  (53 shorter events, 3.4 us)
Async XLA Ops:
  7.2 244.3 %copy-start = (bf16[1024,768]{1,0:T(8,128)(2,1)S(1)}, bf16[1024,768]{1,0:T(8,128)(2,1)}, u32[]{:S(2)}) copy-start(bf16[1024,768]{1,0:T(8,128)(2,1)} %param.28) | copy-start | bytes 4718596
  7.2 70.4 %copy-start.6 = (f32[768]{0:T(1024)S(1)}, f32[768]{0:T(1024)}, u32[]{:S(2)}) copy-start(f32[768]{0:T(1024)} %param.36) | copy-start | bytes 9220
  7.2 71.0 %copy-start.7 = (f32[768]{0:T(1024)S(1)}, f32[768]{0:T(1024)}, u32[]{:S(2)}) copy-start(f32[768]{0:T(1024)} %param.37) | copy-start | bytes 9220
  7.2 71.6 %copy-start.8 = (f32[768]{0:T(1024)S(1)}, f32[768]{0:T(1024)}, u32[]{:S(2)}) copy-start(f32[768]{0:T(1024)} %param.42) | copy-start | bytes 9220
  7.2 72.1 %copy-start.14 = (f32[192]{0:T(256)S(1)}, f32[192]{0:T(256)}, u32[]{:S(2)}) copy-start(f32[192]{0:T(256)} %param.32) | copy-start | bytes 2308
  7.3 72.1 %copy-start.13 = (f32[192]{0:T(256)S(1)}, f32[192]{0:T(256)}, u32[]{:S(2)}) copy-start(f32[192]{0:T(256)} %param.33) | copy-start | bytes 2308
  7.3 72.1 %copy-start.12 = (f32[768]{0:T(1024)S(1)}, f32[768]{0:T(1024)}, u32[]{:S(2)}) copy-start(f32[768]{0:T(1024)} %param.39) | copy-start | bytes 9220
  7.3 72.2 %copy-start.9 = (f32[768]{0:T(1024)S(1)}, f32[768]{0:T(1024)}, u32[]{:S(2)}) copy-start(f32[768]{0:T(1024)} %param.35) | copy-start | bytes 9220
  7.3 72.8 %copy-start.10 = (f32[768]{0:T(1024)S(1)}, f32[768]{0:T(1024)}, u32[]{:S(2)}) copy-start(f32[768]{0:T(1024)} %param.41) | copy-start | bytes 9220
  7.3 73.4 %copy-start.11 = (f32[768]{0:T(1024)S(1)}, f32[768]{0:T(1024)}, u32[]{:S(2)}) copy-start(f32[768]{0:T(1024)} %param.43) | copy-start | bytes 9220
  7.3 70.3 %all-gather.8.cloned.1.call-start = ((), (), s32[]{:S(2)}) async-start(), calls=%async_computation.3 | async-start | bytes 3981312 | tf_op jit(solution)/shard_map/all_gather | solution.py:553
  11.1 159.0 %all-gather.14.cloned.1.call-start = ((), (), s32[]{:S(2)}) async-start(), calls=%async_computation.6 | async-start | bytes 17694720 | tf_op jit(solution)/shard_map/all_gather | solution.py:553
  170.1 113.5 %copy-start.15 = (s32[64]{0:T(128)S(1)}, s32[64]{0:T(128)}, u32[]{:S(2)}) copy-start(s32[64]{0:T(128)} %param.27) | copy-start | bytes 772
  252.2 94.3 %copy-start.3 = (f32[64,1024]{1,0:T(8,128)}, f32[64,1024]{1,0:T(8,128)S(1)}, u32[]{:S(2)}) copy-start(f32[64,1024]{1,0:T(8,128)S(1)} %get-tuple-element.201) | copy-start | bytes 786436
  284.7 9.3 %all-to-all-start = ((bf16[8,8,768]{2,1,0:T(8,128)(2,1)}), bf16[8,8,768]{2,1,0:T(8,128)(2,1)S(1)}, u32[]{:S(2)}, u32[]{:S(2)}) async-start(bf16[8,8,768]{2,1,0:T(8,128)(2,1)} %fusion.1), calls=%async_computation | async-start | bytes 196608 | tf_op jit(solution)/shard_map/all_to_all | solution.py:505
  350.5 32.9 %collective-permute-start = (bf16[4,400,384]{2,1,0:T(8,128)(2,1)}, bf16[4,400,384]{2,1,0:T(8,128)(2,1)}, u32[]{:S(2)}, u32[]{:S(2)}) collective-permute-start(bf16[4,400,384]{2,1,0:T(8,128)(2,1)} %get-tuple-element.171), channel_id=1, source_target_pairs={{1,0},{2,1},{3,2},{5,4},{6,5},{7,6},{9,8},{10,9},{11,10},{13,12},{... | collective-permute-start | bytes 3686408 | tf_op jit(solution)/shard_map/ppermute | solution.py:569
  367.5 18.9 %collective-permute-start.1 = (bf16[4,400,384]{2,1,0:T(8,128)(2,1)S(1)}, bf16[4,400,384]{2,1,0:T(8,128)(2,1)S(1)}, u32[]{:S(2)}, u32[]{:S(2)}) collective-permute-start(bf16[4,400,384]{2,1,0:T(8,128)(2,1)S(1)} %get-tuple-element.170), channel_id=1, source_target_pairs={{0,1},{1,2},{2,3},{4,5},{5,6},{6,7},{8,9},{9,10},{10,11},{12,13},{... | collective-permute-start | bytes 3686408 | tf_op jit(solution)/shard_map/ppermute | solution.py:570
  373.0 6.4 copy-start.2
  415.6 173.4 %all-to-all-start.1 = ((bf16[4,3,1,768,768]{4,3,1,2,0:T(8,128)(2,1)}), bf16[4,3,1,768,768]{4,3,1,2,0:T(8,128)(2,1)}, u32[]{:S(2)}, u32[]{:S(2)}) async-start(bf16[4,3,1,768,768]{4,3,1,2,0:T(8,128)(2,1)} %copy.52), calls=%async_computation.1 | async-start | bytes 28311552 | tf_op jit(solution)/shard_map/all_to_all | solution.py:505
  422.2 286.9 %all-gather.10.cloned.1.call-start = ((), (), s32[]{:S(2)}) async-start(), calls=%async_computation.4 | async-start | bytes 3932160 | tf_op jit(solution)/shard_map/all_gather | solution.py:579
  603.5 5.8 copy-start.4
  603.5 5.8 copy-start.5
  603.5 110.7 %all-to-all-start.2 = ((bf16[8,3,96,768]{3,2,1,0:T(8,128)(2,1)}), bf16[8,3,96,768]{3,2,1,0:T(8,128)(2,1)}, u32[]{:S(2)}, u32[]{:S(2)}) async-start(bf16[8,3,96,768]{3,2,1,0:T(8,128)(2,1)} %copy.53), calls=%async_computation.2 | async-start | bytes 7077888 | tf_op jit(solution)/shard_map/all_to_all | solution.py:505
  608.1 101.0 %all-gather.12.cloned.1.call-start = ((), (), s32[]{:S(2)}) async-start(), calls=%async_computation.5 | async-start | bytes 3932160 | tf_op jit(solution)/shard_map/all_gather | solution.py:578
  719.1 3.9 copy-start.1
Sparse Core Ops, SparseCore 0:
  11.2 66.2 all-gather.7
  79.1 90.9 all-gather.13
  424.6 42.0 all-gather.9
  610.2 30.9 all-gather.11

commit v2 on v1

--- a/solution.py
+++ b/solution.py
@@ -135,11 +135,13 @@
         q[g] = made.astype(BF16) * jnp.asarray(HEAD**-0.5, BF16)
 
 
-def attend(sizes, me, kv, q, bias, lse, ctx):
+def attend(sizes, me, kv, q, bias, lse, ctx, tick=None):
     @pl.loop(0, sizes.groups)
     def _(g):
         @pl.loop(0, sizes.blocks)
         def _(b):
+            if tick is not None:
+                tick(g * sizes.blocks + b)
             keys = pl.ds(sizes.key_offset(me, b), sizes.keys)
             rows = pl.ds(pl.multiple_of(b * sizes.block, sizes.block), sizes.block)
             made = [jnp.zeros((HEAD, sizes.block), F32)]
@@ -197,11 +199,233 @@
             dq[g, rows, :] = jnp.concatenate(made, axis=0).T
 
 
-def forward_kernel(
+class Loads:
+    def __init__(self, weights, w, sems):
+        self.copies = [pltpu.make_async_copy(weights.at[s], w.at[s], sems.at[s]) for s in range(3)]
+
+    def begin(self):
+        for copy in self.copies:
+            copy.start()
+
+    def ready(self, section):
+        self.copies[section].wait()
+
+    def tick(self, step):
+        pass
+
+    def end(self):
+        pass
+
+
+MESH = pl.DeviceIdType.MESH
+
+
+class Place:
+    def __init__(self):
+        self.dp, self.mp = lax.axis_index("dp"), lax.axis_index("mp")
+        self.z, self.x, self.y, self.core = self.dp // 2, self.dp % 2, self.mp // 2, self.mp % 2
+        flip = 1 - self.core
+        self.across = 2 * (1 - self.y) + self.core
+        self.sibling = (self.dp, 2 * self.y + flip)
+        x_peer = 2 * self.z + 1 - self.x
+        self.first = (self.dp + flip * (x_peer - self.dp), self.mp + self.core * (self.across - self.mp))
+        self.second = (self.dp + self.core * (x_peer - self.dp), self.mp + flip * (self.across - self.mp))
+        self.zs = [self.z, self.z + 1 - 2 * (self.z % 2), (self.z + 2) % 4, 3 - self.z]
+        self.line = [(2 * z + self.x, self.mp) for z in self.zs]
+        self.own_column = (self.mp, self.x)
+        self.first_column = (
+            self.mp + self.core * (self.across - self.mp),
+            self.x + flip * (1 - 2 * self.x),
+        )
+        self.second_columns = (
+            (self.mp + flip * (self.across - self.mp), self.x + self.core * (1 - 2 * self.x)),
+            (self.across, 1 - self.x),
+        )
+        self.diagonal = (self.dp, 2 * (1 - self.y) + flip)
+        self.peers = [*self.line[1:], self.first, self.second, self.sibling, self.diagonal]
+
+
+def greet(peers):
+    barrier = pltpu.get_barrier_semaphore()
+    for peer in peers:
+        pl.semaphore_signal(barrier, inc=1, device_id=peer, device_id_type=MESH)
+    pl.semaphore_wait(barrier, len(peers))
+
+
+class Gather:
+    def __init__(self, place, packed, own_bias, w, biases, kept, send, recv, local, bias_sems):
+        self.at, self.packed, self.w, self.kept = place, packed, w, kept
+        self.own_bias, self.biases = own_bias, biases
+        self.send_sems, self.recv_sems, self.local, self.bias_sems = send, recv, local, bias_sems
+        self.rows = packed.shape[1]
+        self.shards = w.shape[2] // self.rows
+
+    def shard(self, s, g, d):
+        return self.w.at[s, g, pl.ds(pl.multiple_of(d * self.rows, 16), self.rows)]
+
+    def copy(self, s, g, d, slot, peer, source=None):
+        here = self.shard(s, g, d)
+        return pltpu.make_async_remote_copy(
+            src_ref=here if source is None else source,
+            dst_ref=here,
+            send_sem=self.send_sems.at[s, slot],
+            recv_sem=self.recv_sems.at[s, g * self.shards + d],
+            device_id=peer,
+            device_id_type=MESH,
+        )
+
+    def arrived(self, s, g, d):
+        self.copy(s, g, d, 0, self.at.sibling).wait_recv()
+
+    def own_copy(self, s):
+        return pltpu.make_async_copy(
+            self.packed.at[s], self.shard(s, self.at.mp, self.at.dp), self.local.at[s]
+        )
+
+    def along_z(self, s):
+        at = self.at
+        for k in range(1, 4):
+            self.copy(s, at.mp, at.dp, k - 1, at.line[k], self.packed.at[s]).start()
+
+    def own_out(self, s):
+        at = self.at
+        self.own_copy(s).start()
+        source = self.packed.at[s]
+        self.copy(s, at.mp, at.dp, 3, at.first, source).start()
+        self.copy(s, at.mp, at.dp, 7, at.second, source).start()
+        self.copy(s, at.mp, at.dp, 15, at.sibling, source).start()
+
+    def from_z(self, s, k):
+        at, (g, x) = self.at, self.at.own_column
+        d = 2 * at.zs[k] + x
+        self.arrived(s, g, d)
+        self.copy(s, g, d, 3 + k, at.first).start()
+        self.copy(s, g, d, 7 + k, at.second).start()
+        self.copy(s, g, d, 15 + k, at.sibling).start()
+
+    def from_first(self, s, k):
+        at, (g, x) = self.at, self.at.first_column
+        d = 2 * at.zs[k] + x
+        self.arrived(s, g, d)
+        self.copy(s, g, d, 11 + k, at.second).start()
+        self.copy(s, g, d, 19 + k, at.sibling).start()
+
+    def from_second(self, s, k):
+        at, (g, x) = self.at, self.at.second_columns[k // 4]
+        d = 2 * at.zs[k % 4] + x
+        self.arrived(s, g, d)
+        self.copy(s, g, d, 23 + k, at.sibling).start()
+
+    def from_sibling(self, s):
+        at = self.at
+        for g in (at.sibling[1], at.diagonal[1]):
+
+            @pl.loop(0, self.shards)
+            def _(d):
+                self.arrived(s, g, d)
+
+    def keep(self, s):
+        return pltpu.make_async_copy(self.w.at[s], self.kept.at[s], self.local.at[3 + s])
+
+    def bias_copy(self, k, peer):
+        return pltpu.make_async_remote_copy(
+            src_ref=self.own_bias,
+            dst_ref=self.biases.at[self.at.mp],
+            send_sem=self.bias_sems.at[0, k],
+            recv_sem=self.bias_sems.at[1, k],
+            device_id=peer,
+            device_id_type=MESH,
+        )
+
+    def bias_copies(self):
+        at = self.at
+        across = (at.dp, at.across)
+        return [self.bias_copy(k, peer) for k, peer in enumerate((at.sibling, across, at.diagonal))]
+
+    def begin(self):
+        greet(self.at.peers)
+        self.along_z(0)
+        self.own_out(0)
+        for copy in self.bias_copies():
+            copy.start()
+        self.biases[self.at.mp] = self.own_bias[...]
+
+    def ready(self, section):
+        if section == 0:
+            self.from_z(0, 1)
+            self.from_z(0, 2)
+            self.from_z(0, 3)
+            self.along_z(1)
+            for k in range(4):
+                self.from_first(0, k)
+            self.own_out(1)
+            for k in range(8):
+                self.from_second(0, k)
+            for copy in self.bias_copies():
+                copy.wait_recv()
+            self.steps(0)
+            self.from_sibling(0)
+        elif section == 1:
+            self.steps(9)
+            self.from_sibling(1)
+        else:
+            self.steps(10)
+            self.from_sibling(2)
+        self.own_copy(section).wait()
+        self.keep(section).start()
+
+    def steps(self, step):
+        if step == 0:
+            for k in range(1, 4):
+                self.from_z(1, k)
+            self.along_z(2)
+        elif step == 2:
+            self.from_first(1, 0)
+            self.from_first(1, 1)
+        elif step == 3:
+            self.from_first(1, 2)
+            self.from_first(1, 3)
+        elif step == 4:
+            self.own_out(2)
+            for k in range(1, 4):
+                self.from_z(2, k)
+        elif step == 5:
+            for k in range(4):
+                self.from_second(1, k)
+        elif step == 6:
+            for k in range(4, 8):
+                self.from_second(1, k)
+        elif step == 7:
+            self.from_first(2, 0)
+            self.from_first(2, 1)
+        elif step == 9:
+            self.from_first(2, 2)
+            self.from_first(2, 3)
+        elif step == 10:
+            for k in range(8):
+                self.from_second(2, k)
+
+    def tick(self, step):
+        for k in range(2, 8):
+            pl.when(step == k)(functools.partial(self.steps, k))
+
+    def end(self):
+        for copy in self.bias_copies():
+            copy.wait_send()
+        for s in range(3):
+
+            @pl.loop(0, 31)
+            def _(slot):
+                self.copy(s, 0, 0, slot, self.at.sibling).wait_send()
+
+            self.keep(s).wait()
+
+
+def forward_math(
     sizes,
+    source,
     lens,
     tokens,
-    weights,
     biases,
     b_out,
     gain_1,
@@ -215,9 +439,9 @@
     r_1,
     n_2,
     r_2,
-    z,
-    slope,
-    kv,
+    z_out,
+    slope_out,
+    kv_out,
     q,
     lse,
     ctx,
@@ -225,21 +449,23 @@
     w,
     bias,
     hidden,
+    kv,
+    z,
+    slope,
     sems,
 ):
     me = lax.axis_index("mp")
     first = pl.multiple_of(sizes.window_start(me), 16)
-    load = pltpu.make_async_copy(tokens.at[pl.ds(first, sizes.window)], x, sems.at[3])
+    load = pltpu.make_async_copy(tokens.at[pl.ds(first, sizes.window)], x, sems.at[0])
     load.start()
-    loads = []
-    for s in range(3):
-        loads.append(pltpu.make_async_copy(weights.at[:, s], w.at[s], sems.at[s]))
-        loads[-1].start()
+    source.begin()
     fill_mask(sizes, me, lens, bias)
     load.wait()
-    loads[0].wait()
+    source.ready(0)
     project(sizes, me, x, w.at[0], biases, kv, q)
-    attend(sizes, me, kv, q, bias, lse, ctx)
+    save_kv = pltpu.make_async_copy(kv, kv_out, sems.at[1])
+    save_kv.start()
+    attend(sizes, me, kv, q, bias, lse, ctx, source.tick)
 
     own = pl.ds(sizes.own_offset(me), sizes.own)
     hidden[...] = x[own, :].astype(F32) + b_out[...]
@@ -251,8 +477,7 @@
     y_1 = normed * gain_1[...] + shift_1[...]
     hidden[...] = y_1 + b_down[...]
     encoded[...] = y_1.astype(BF16)
-    loads[1].wait()
-    loads[2].wait()
+    source.ready(1)
 
     @pl.loop(0, sizes.groups)
     def _(g):
@@ -260,6 +485,15 @@
         out, grad = gelu_and_slope(a)
         z[g] = out.astype(BF16)
         slope[g] = grad.astype(BF16)
+
+    save_z = pltpu.make_async_copy(z, z_out, sems.at[2])
+    save_slope = pltpu.make_async_copy(slope, slope_out, sems.at[3])
+    save_z.start()
+    save_slope.start()
+    source.ready(2)
+
+    @pl.loop(0, sizes.groups)
+    def _(g):
         hidden[...] += dot(z[g], w[2, g], 1, 1)
 
     normed, factor = norm_stats(hidden[...])
@@ -268,6 +502,25 @@
     y_2 = (normed * gain_2[...] + shift_2[...]).astype(BF16)
     encoded[...] = y_2
     cls[...] = dot(start_rows(sizes, me, lens).astype(BF16), y_2)
+    source.end()
+    save_kv.wait()
+    save_z.wait()
+    save_slope.wait()
+
+
+def forward_kernel(sizes, lens, tokens, weights, biases, *rest):
+    *refs, w, bias, hidden, kv, z, slope, sems, loads = rest
+    source = Loads(weights, w, loads)
+    forward_math(sizes, source, lens, tokens, biases, *refs, w, bias, hidden, kv, z, slope, sems)
+
+
+def gathering_kernel(sizes, lens, tokens, packed, own_bias, *rest):
+    rows, (kept, *outs) = rest[:6], rest[6:]
+    *refs, w, bias, hidden, kv, z, slope, sems, biases, send, recv, local, bias_sems = outs
+    source = Gather(Place(), packed, own_bias, w, biases, kept, send, recv, local, bias_sems)
+    forward_math(
+        sizes, source, lens, tokens, biases, *rows, *refs, w, bias, hidden, kv, z, slope, sems
+    )
 
 
 def backward_kernel(
@@ -317,7 +570,7 @@
     load_cot.start()
     loads = []
     for s, buffer in ((2, w_down), (1, w_up), (0, w_attn)):
-        loads.append(pltpu.make_async_copy(weights.at[:, s], buffer, sems.at[s]))
+        loads.append(pltpu.make_async_copy(weights.at[s], buffer, sems.at[s]))
         loads[-1].start()
     fill_mask(sizes, me, lens, bias)
     picked = start_rows(sizes, me, lens).astype(BF16)
@@ -404,11 +657,11 @@
     return pltpu.CompilerParams(vmem_limit_bytes=62 * 2**20, **more)
 
 
-def run_forward(sizes, lengths, tokens, weights, biases, rows):
+def run_forward(sizes, lengths, tokens, weights, biases, rows, gathers):
     own, width, groups = sizes.own, sizes.width, sizes.groups
     docs = lengths.shape[1]
     shape = jax.ShapeDtypeStruct
-    outs = (
+    outs = [
         shape((own, width), BF16),
         shape((docs, width), F32),
         shape((own, width), F32),
@@ -421,20 +674,39 @@
         shape((groups, own, 2 * LANES), BF16),
         shape((groups, sizes.blocks, 8, sizes.block), F32),
         shape((groups, own, 2 * LANES), BF16),
-    )
+    ]
+    spaces = [*[VMEM] * 6, ANY, ANY, ANY, *[VMEM] * 3]
+    scratch = [
+        pltpu.VMEM((sizes.window, width), BF16),
+        pltpu.VMEM((3, groups, width, width), BF16),
+        pltpu.VMEM((sizes.blocks, sizes.keys, sizes.block), F32),
+        pltpu.VMEM((own, width), F32),
+        pltpu.VMEM((groups, sizes.window, 3 * LANES), BF16),
+        pltpu.VMEM((groups, own, width), BF16),
+        pltpu.VMEM((groups, own, width), BF16),
+        pltpu.SemaphoreType.DMA((4,)),
+    ]
+    if gathers:
+        outs.insert(0, shape((3, groups, width, width), BF16))
+        spaces.insert(0, ANY)
+        scratch += [
+            pltpu.VMEM((groups, 1, biases.shape[1]), F32),
+            pltpu.SemaphoreType.DMA((3, 31)),
+            pltpu.SemaphoreType.DMA((3, 32)),
+            pltpu.SemaphoreType.DMA((6,)),
+            pltpu.SemaphoreType.DMA((2, 3)),
+        ]
+        kernel, more = gathering_kernel, {"collective_id": 0, "has_side_effects": True}
+    else:
+        scratch.append(pltpu.SemaphoreType.DMA((3,)))
+        kernel, more = forward_kernel, {}
     return pl.pallas_call(
-        functools.partial(forward_kernel, sizes),
+        functools.partial(kernel, sizes),
         out_shape=outs,
-        in_specs=specs(SMEM, ANY, ANY, *[VMEM] * 7),
-        out_specs=specs(*[VMEM] * len(outs)),
-        scratch_shapes=[
-            pltpu.VMEM((sizes.window, width), BF16),
-            pltpu.VMEM((3, groups, width, width), BF16),
-            pltpu.VMEM((sizes.blocks, sizes.keys, sizes.block), F32),
-            pltpu.VMEM((own, width), F32),
-            pltpu.SemaphoreType.DMA((4,)),
-        ],
-        compiler_params=params(),
+        in_specs=specs(SMEM, ANY, VMEM if gathers else ANY, *[VMEM] * 7),
+        out_specs=specs(*spaces),
+        scratch_shapes=scratch,
+        compiler_params=params(**more),
         name="forward",
     )(lengths, tokens, weights, biases, *rows)
 
@@ -550,12 +822,17 @@
     packed = jnp.stack(
         [jnp.concatenate([w_key, w_value, w_query, w_out.T], axis=1), w_up, w_down.T]
     )
-    whole = lax.all_gather(lax.all_gather(packed, "dp", axis=1, tiled=True), "mp", axis=0)
     zeros = jnp.zeros((head_cols,), F32)
-    own_bias = jnp.concatenate([zeros, b_value, b_query, zeros[:HEAD], b_up])
-    biases = lax.all_gather(own_bias[None], "mp", axis=0)
+    own_bias = jnp.concatenate([zeros, b_value, b_query, zeros[:HEAD], b_up])[None]
     rows = [r[None] for r in (b_out, gain_attn, shift_attn, b_down, gain_ffn, shift_ffn)]
-    encoded, cls, *saved = run_forward(sizes, lengths, tokens, whole, biases, rows)
+    if lax.axis_size("dp") == 8 and groups == 4:
+        whole, encoded, cls, *saved = run_forward(
+            sizes, lengths, tokens, packed, own_bias, rows, True
+        )
+    else:
+        whole = lax.all_gather(lax.all_gather(packed, "dp", axis=1, tiled=True), "mp", axis=1)
+        biases = lax.all_gather(own_bias, "mp", axis=0)
+        encoded, cls, *saved = run_forward(sizes, lengths, tokens, whole, biases, rows, False)
     cls = lax.psum(cls, "mp").astype(BF16)
     table, lse, dcls = score(cls, passages, gold)
     n_1, r_1, n_2, r_2, z, slope, kv, q, logs, ctx = saved
@@ -573,7 +850,7 @@
     dkv = dkv.at[:, :halo].add(from_left.astype(F32))
     own_tokens = lax.dynamic_slice_in_dim(tokens, own * me, own, axis=0)
     token_part, grads_attn, small_attn = run_input(
-        sizes, own_tokens, whole[:, 0], dkv, dq, dh_1, grads_out
+        sizes, own_tokens, whole[0], dkv, dq, dh_1, grads_out
     )
     token_grad = lax.all_gather(token_part, "mp", axis=0, tiled=True).astype(F32)
     encoded = lax.all_gather(encoded, "mp", axis=0, tiled=True)

time: 732 us -> 619 us (0.85)
  waiting for transfers between devices: 323 us -> 175 us
  Pallas kernels: 111 us -> 149 us
  blocking collectives: 172 us -> 163 us
    all_gather x2 -> x0, waiting for transfers between devices: 148 us -> none  [the longest x1 81.8 us: body(): lax.all_gather(lax.all_gather(packed, 'dp', axis=1, tiled=True), 'mp', ax...]
    pallas_call x1, Pallas kernels: 46.2 us -> 84 us  [run_forward(): pl.pallas_call(functools.partial(kernel, sizes), out_shape=outs, in_specs...]
  transfers between devices with their start and end apart: 9 -> 7, of which waited for: 5 -> 3; matrix products, arithmetic and copies ran while one was open for 5% -> 5% of each run, Pallas kernels for 0% -> 0%
where the time goes in v2:
time: 619 us; the launch traced here: 616 us
  waiting for transfers between devices  175 us (28%)
  blocking collectives  163 us (26%)
  Pallas kernels  149 us (24%)
  local copies, waits for them, and re-layouts  42.4 us (7%)
  other arithmetic  35.2 us (6%)
  starting transfers between devices  34.9 us (6%)
  between operations  14.3 us (2%)
    all_to_all x3, waiting for transfers between devices, summed_on_arrival(): lax.all_to_all(pieces, axis, split_axis=0, concat_axis=0, tiled=True)  172 us
    psum x1, blocking collectives, body(): small, small_attn = lax.psum((small, small_attn), ('dp', 'mp'))  98.3 us
    pallas_call x1, Pallas kernels, run_forward(): pl.pallas_call(functools.partial(kernel, sizes), out_shape=outs, in_specs...  84 us
    pallas_call x1, Pallas kernels, run_backward(): pl.pallas_call(functools.partial(backward_kernel, sizes), out_shape=outs,...  52 us
    all_gather x1, blocking collectives, score(): all_first = lax.all_gather(cls, 'dp', axis=0, tiled=True)  24.3 us
    ppermute x1, starting transfers between devices, body(): lax.ppermute(to_left, 'mp', [(i, i - 1) for i in range(1, groups)])  16.7 us
    pmax x1, blocking collectives, score(): peak = lax.pmax(jnp.max(table, axis=1), 'dp')  16.2 us
    all_to_all x3, starting transfers between devices, summed_on_arrival(): lax.all_to_all(pieces, axis, split_axis=0, concat_axis=0, tiled=True)  14.8 us
  transfers between devices with their start and end apart: 7, of which 3 were waited for; matrix products, arithmetic and copies ran while one was open for 5% of the time, Pallas kernels for 0%

profile of v2, /device:TPU:1, one launch (start us, length us, event | category | flops | bytes accessed | tf_op | source)
XLA Modules:
  0.0 615.9 jit_solution(18205910916432870366)
XLA Ops:
  7.2 1.4 broadcast_in_dim.32.rest_1_.gain_1
  8.6 1.3 broadcast_in_dim.33.rest_2_.shift_1
  9.9 1.3 broadcast_in_dim.35.rest_4_.gain_2
  11.1 0.9 copy.44
  12.0 0.8 concatenate.11
  13.4 1.3 broadcast_in_dim.31.rest_0_
  14.7 1.3 broadcast_in_dim.34.rest_3_
  16.0 1.3 broadcast_in_dim.36.rest_5_
  17.2 0.9 maximum_bitcast_fusion.1
  18.2 1.8 pad_maximum_fusion.packed
  20.0 84.0 %forward.1 = (bf16[3,4,768,768]{3,2,1,0:T(8,128)(2,1)}, bf16[512,768]{1,0:T(8,128)(2,1)}, f32[8,768]{1,0:T(8,128)}, f32[512,768]{1,0:T(8,128)}, f32[512,1]{1,0:T...) custom-call(s32[1,8]{1,0:T(1,128)} %lens.3, ...), custom_call_target="tpu_custom_call" | custom-call | tf_op jit(solution)/shard_map/forward/pallas_call | solution.py:703
  104.0 10.8 %psum.28 = bf16[8,768]{1,0:T(8,128)(2,1)S(1)} all-reduce(f32[8,768]{1,0:T(8,128)} %get-tuple-element.65), channel_id=1, replica_groups=mesh['dp'=8,'mp'=4] {'mp'}, use_global_device_ids=true, to_apply=%region_0.0 | all-reduce | flops 6144 | bytes 36864 | tf_op jit(solution)/shard_map/psum | solution.py:836
  114.9 24.3 %all_gather.9 = bf16[64,768]{1,0:T(8,128)(2,1)S(1)} all-gather(bf16[8,768]{1,0:T(8,128)(2,1)S(1)} %psum.28), channel_id=1, replica_groups=mesh['dp'=8,'mp'=4] {'dp'}, dimensions={0}, use_global_device_ids=true | all-gather | bytes 110592 | tf_op jit(solution)/shard_map/all_gather | solution.py:782
  139.2 0.7 fusion.7
  139.9 16.2 %pmax.7 = f32[64]{0:T(128)S(1)} all-reduce(f32[64]{0:T(128)S(1)} %get-tuple-element.163), channel_id=1, replica_groups=mesh['dp'=8,'mp'=4] {'dp'}, use_global_device_ids=true, to_apply=%region_2.0 | all-reduce | flops 64 | bytes 512 | tf_op jit(solution)/shard_map/pmax | solution.py:784
  156.3 13.7 %psum.29 = f32[64]{0:T(128)S(1)} all-reduce(f32[64]{0:T(128)S(1)} %fusion.2), channel_id=1, replica_groups=mesh['dp'=8,'mp'=4] {'dp'}, use_global_device_ids=true, to_apply=%region_4.0 | all-reduce | flops 64 | bytes 512 | tf_op jit(solution)/shard_map/psum | solution.py:785
  170.0 1.1 fusion.1
  171.1 3.5 all-to-all-start
  174.6 5.7 all-to-all-done
  181.0 52.0 %backward.1 = (f32[512,768]{1,0:T(8,128)}, f32[4,1312,384]{2,1,0:T(8,128)}, f32[4,512,256]{2,1,0:T(8,128)}, bf16[2,4,768,768]{3,2,1,0:T(8,128)(2,1)}, f32[4,768,256]{2,1,0:T(8,128)}, /*index=5*/f32[16,768]{1,0:T(8,128)}) custom-call(s32[1,8]{1,0:T(1,128)} %lens.3, bf16[2048,768]{1,0:T(8,128)(2,1)} %cotangent.1, f32[8,768]{1,0:T(8,128)} %convert_reduce_fusion.1.dcls, ...), custom_call_target="tpu_custom_call" | custom-call | tf_op jit(solution)/shard_map/backward/pallas_call | solution.py:725
  232.9 4.0 dynamic-slice_convert_fusion
  237.0 16.7 %collective-permute-start = (bf16[4,400,384]{2,1,0:T(8,128)(2,1)}, bf16[4,400,384]{2,1,0:T(8,128)(2,1)}, u32[]{:S(2)}, u32[]{:S(2)}) collective-permute-start(bf16[4,400,384]{2,1,0:T(8,128)(2,1)} %get-tuple-element.154), channel_id=1, source_target_pairs={{1,0},{2,1},{3,2},{5,4},{6,5},{7,6},{9,8},{10,9},{11,10},{13,12},{... | collective-permute-start | bytes 3686408 | tf_op jit(solution)/shard_map/ppermute | solution.py:846
  253.7 3.3 collective-permute-start.1
  257.0 2.1 constant_dynamic-slice_fusion.3.tokens
  259.1 5.2 slice_bitcast_fusion.weights
  264.3 1.2 copy-done.2
  265.5 1.9 constant_dynamic-slice_fusion.2
  267.4 2.2 collective-permute-done
  269.6 3.1 add_dynamic-update-slice_fusion
  272.6 3.4 fusion.dkv
  276.0 12.8 %inputs.1 = (bf16[512,768]{1,0:T(8,128)(2,1)}, bf16[4,768,768]{2,1,0:T(8,128)(2,1)}, f32[4,1,640]{2,1,0:T(1,128)}) custom-call(bf16[512,768]{1,0:T(8,128)(2,1)} %constant_dynamic-slice_fusion.3.tokens, bf16[4,768,768]{2,1,0:T(8,128)(2,1)} %slice_bitcast_fusion.weights, f32[4,512,384]{2,1,0:T(8,128)} %fusion.dkv, f32[4,512,256]{2,1,0:T(8,128)} %get-tuple-element.79.dq, ...), custom_call_target="tpu_custom_call" | custom-call | tf_op jit(solution)/shard_map/inputs/pallas_call | solution.py:759
  288.9 7.2 %maximum_bitcast_fusion = bf16[4,3,1,768,768]{4,3,0,1,2:T(8,128)(2,1)S(1)} fusion(bf16[2,4,768,768]{3,2,1,0:T(8,128)(2,1)} %get-tuple-element.84, bf16[1,4,768,768]{3,2,1,0:T(8,128)(2,1)} %bitcast.41), kind=kLoop, calls=%fused_computation | loop fusion | flops 7077888 | bytes 28311552 | tf_op jit(solution)/shard_map/transpose | solution.py:772
  296.0 5.8 copy.45
  301.8 6.6 %all-to-all-start.1 = ((bf16[4,3,1,768,768]{4,3,1,2,0:T(8,128)(2,1)}), bf16[4,3,1,768,768]{4,3,1,2,0:T(8,128)(2,1)}, u32[]{:S(2)}, u32[]{:S(2)}) async-start(bf16[4,3,1,768,768]{4,3,1,2,0:T(8,128)(2,1)} %copy.45), calls=%async_computation.1 | async-start | bytes 28311552 | tf_op jit(solution)/shard_map/all_to_all | solution.py:777
  308.5 0.7 all-gather.3.cloned.1.call-update
  309.2 166.0 %all-to-all-done.1 = bf16[4,3,1,768,768]{4,3,1,2,0:T(8,128)(2,1)} async-done(((bf16[4,3,1,768,768]{4,3,1,2,0:T(8,128)(2,1)}), bf16[4,3,1,768,768]{4,3,1,2,0:T(8,128)(2,1)}, u32[]{:S(2)}, u32[]{:S(2)}) %all-to-all-start.1) | async-done | bytes 14155808 | tf_op jit(solution)/shard_map/all_to_all | solution.py:777
  475.2 10.4 %reduce_sum.41 = bf16[3,768,768]{2,1,0:T(8,128)(2,1)} reduce(bf16[4,3,1,768,768]{4,3,1,2,0:T(8,128)(2,1)} %all-to-all-done.1, bf16[]{:T(256)} %constant.119.clone.1), dimensions={0,2}, to_apply=%region_6.7 | reduce | flops 5308416 | bytes 17694722 | tf_op jit(solution)/shard_map/reduce_sum | solution.py:778
  485.5 4.0 copy.46
  489.6 4.6 all-to-all-start.2
  494.3 0.7 all-gather.5.cloned.1.call-update
  495.6 98.3 %all-reduce = (f32[4,1,640]{2,1,0:T(1,128)S(1)}, f32[16,768]{1,0:T(8,128)S(1)}) all-reduce(f32[4,1,640]{2,1,0:T(1,128)S(1)} %copy-done.5, f32[16,768]{1,0:T(8,128)S(1)} %copy-done.4), channel_id=1, replica_groups=mesh['dp'=8,'mp'=4] {'dp','mp'}, use_global_device_ids=true, to_apply=%region_8.9 | all-reduce | flops 14848 | bytes 118784 | tf_op jit(solution)/shard_map/psum | solution.py:860
  594.5 0.7 slice_reduce_fusion
  595.2 5.1 convert_element_type.48
  600.3 2.6 convert_reduce_fusion
  602.9 0.8 slice_bitcast_fusion.1
  603.7 0.7 slice_bitcast_fusion.3
  604.5 0.7 copy.47
  605.2 3.9 copy.51
  (28 shorter events, 2.8 us)
Async XLA Ops:
  7.2 132.0 %copy-start = (bf16[1024,768]{1,0:T(8,128)(2,1)S(1)}, bf16[1024,768]{1,0:T(8,128)(2,1)}, u32[]{:S(2)}) copy-start(bf16[1024,768]{1,0:T(8,128)(2,1)} %param.28) | copy-start | bytes 4718596
  20.0 150.0 %copy-start.6 = (s32[64]{0:T(128)S(1)}, s32[64]{0:T(128)}, u32[]{:S(2)}) copy-start(s32[64]{0:T(128)} %param.27) | copy-start | bytes 772
  139.9 93.0 %copy-start.3 = (f32[64,1024]{1,0:T(8,128)}, f32[64,1024]{1,0:T(8,128)S(1)}, u32[]{:S(2)}) copy-start(f32[64,1024]{1,0:T(8,128)S(1)} %get-tuple-element.184) | copy-start | bytes 786436
  171.1 9.3 %all-to-all-start = ((bf16[8,8,768]{2,1,0:T(8,128)(2,1)}), bf16[8,8,768]{2,1,0:T(8,128)(2,1)S(1)}, u32[]{:S(2)}, u32[]{:S(2)}) async-start(bf16[8,8,768]{2,1,0:T(8,128)(2,1)} %fusion.1), calls=%async_computation | async-start | bytes 196608 | tf_op jit(solution)/shard_map/all_to_all | solution.py:777
  237.0 32.6 %collective-permute-start = (bf16[4,400,384]{2,1,0:T(8,128)(2,1)}, bf16[4,400,384]{2,1,0:T(8,128)(2,1)}, u32[]{:S(2)}, u32[]{:S(2)}) collective-permute-start(bf16[4,400,384]{2,1,0:T(8,128)(2,1)} %get-tuple-element.154), channel_id=1, source_target_pairs={{1,0},{2,1},{3,2},{5,4},{6,5},{7,6},{9,8},{10,9},{11,10},{13,12},{... | collective-permute-start | bytes 3686408 | tf_op jit(solution)/shard_map/ppermute | solution.py:846
  253.7 19.0 %collective-permute-start.1 = (bf16[4,400,384]{2,1,0:T(8,128)(2,1)S(1)}, bf16[4,400,384]{2,1,0:T(8,128)(2,1)S(1)}, u32[]{:S(2)}, u32[]{:S(2)}) collective-permute-start(bf16[4,400,384]{2,1,0:T(8,128)(2,1)S(1)} %get-tuple-element.153), channel_id=1, source_target_pairs={{0,1},{1,2},{2,3},{4,5},{5,6},{6,7},{8,9},{9,10},{10,11},{12,13},{... | collective-permute-start | bytes 3686408 | tf_op jit(solution)/shard_map/ppermute | solution.py:847
  259.1 6.4 %copy-start.2 = (f32[4,1312,384]{2,1,0:T(8,128)S(1)}, f32[4,1312,384]{2,1,0:T(8,128)}, u32[]{:S(2)}) copy-start(f32[4,1312,384]{2,1,0:T(8,128)} %get-tuple-element.78) | copy-start | bytes 24182788
  301.8 173.3 %all-to-all-start.1 = ((bf16[4,3,1,768,768]{4,3,1,2,0:T(8,128)(2,1)}), bf16[4,3,1,768,768]{4,3,1,2,0:T(8,128)(2,1)}, u32[]{:S(2)}, u32[]{:S(2)}) async-start(bf16[4,3,1,768,768]{4,3,1,2,0:T(8,128)(2,1)} %copy.45), calls=%async_computation.1 | async-start | bytes 28311552 | tf_op jit(solution)/shard_map/all_to_all | solution.py:777
  308.5 286.7 %all-gather.3.cloned.1.call-start = ((), (), s32[]{:S(2)}) async-start(), calls=%async_computation.3 | async-start | bytes 3932160 | tf_op jit(solution)/shard_map/all_gather | solution.py:856
  489.6 6.0 copy-start.4
  489.6 6.0 copy-start.5
  489.6 110.7 %all-to-all-start.2 = ((bf16[8,3,96,768]{3,2,1,0:T(8,128)(2,1)}), bf16[8,3,96,768]{3,2,1,0:T(8,128)(2,1)}, u32[]{:S(2)}, u32[]{:S(2)}) async-start(bf16[8,3,96,768]{3,2,1,0:T(8,128)(2,1)} %copy.46), calls=%async_computation.2 | async-start | bytes 7077888 | tf_op jit(solution)/shard_map/all_to_all | solution.py:777
  494.2 101.0 %all-gather.5.cloned.1.call-start = ((), (), s32[]{:S(2)}) async-start(), calls=%async_computation.4 | async-start | bytes 3932160 | tf_op jit(solution)/shard_map/all_gather | solution.py:855
  605.2 3.9 copy-start.1
Sparse Core Ops, SparseCore 0:
  310.9 42.1 all-gather.2
  496.6 30.9 all-gather.4

commit v3 on v2

--- a/solution.py
+++ b/solution.py
@@ -163,40 +163,49 @@
                 lse[g, b, j : j + 1, :] = logs[j]
 
 
-def attend_back(sizes, me, kv, q, bias, lse, ctx, dctx, delta, dkv, dq):
+def delta_rows(dctx, ctx):
     lane = lax.broadcasted_iota(jnp.int32, (8, 2 * LANES), 1)
     row = lax.broadcasted_iota(jnp.int32, (8, 2 * LANES), 0)
     pick = jnp.where(lane // HEAD == row + 1, 1.0, 0.0).astype(BF16)
-
+    product = dctx.astype(F32) * ctx.astype(F32)
+    high = product.astype(BF16)
+    low = (product - high.astype(F32)).astype(BF16)
+    return dot(pick, high, 1, 1) + dot(pick, low, 1, 1)
+
+
+def attend_back_block(sizes, me, g, b, kv, q, bias, lse, dctx, delta, dkv):
+    keys = pl.ds(sizes.key_offset(me, b), sizes.keys)
+    rows = slice(b * sizes.block, (b + 1) * sizes.block)
+    made = []
+    for j in range(3):
+        kt, kh = KEY_AT[j]
+        vt, vh = VALUE_AT[j]
+        qt, _ = QUERY_AT[j]
+        ct, _ = CONTEXT_AT[j]
+        query = q[g, rows, tile(qt)] * half_mask(kh, BF16)
+        grad = dctx[g, rows, tile(ct)] * half_mask(vh, BF16)
+        s = dot(kv[keys, tile(kt)], query, 1, 1) + bias[b]
+        p = jnp.exp(s - lse[g, b, j : j + 1, :])
+        dp = dot(kv[keys, tile(vt)], grad, 1, 1)
+        ds = (p * (dp - delta[j : j + 1, rows])).astype(BF16)
+        dkv[keys, tile(kt)] += dot(ds, query)
+        dkv[keys, tile(vt)] += dot(p.astype(BF16), grad)
+        back = dot(kv[keys, tile(kt)], ds, 0, 0)
+        made.append(back[kh * HEAD : (kh + 1) * HEAD] * HEAD**-0.5)
+    made.append(jnp.zeros((HEAD, sizes.block), F32))
+    return jnp.concatenate(made, axis=0).T
+
+
+def attend_back(sizes, me, kv, q, bias, lse, ctx, dctx, delta, dkv, dq):
     @pl.loop(0, sizes.groups)
     def _(g):
-        product = dctx[g].astype(F32) * ctx[g].astype(F32)
-        high = product.astype(BF16)
-        low = (product - high.astype(F32)).astype(BF16)
-        delta[...] = dot(pick, high, 1, 1) + dot(pick, low, 1, 1)
+        delta[...] = delta_rows(dctx[g], ctx[g])
         dkv[g] = jnp.zeros_like(dkv[g])
-
         for b in range(sizes.blocks):
-            keys = pl.ds(sizes.key_offset(me, b), sizes.keys)
             rows = slice(b * sizes.block, (b + 1) * sizes.block)
-            made = []
-            for j in range(3):
-                kt, kh = KEY_AT[j]
-                vt, vh = VALUE_AT[j]
-                qt, _ = QUERY_AT[j]
-                ct, _ = CONTEXT_AT[j]
-                query = q[g, rows, tile(qt)] * half_mask(kh, BF16)
-                grad = dctx[g, rows, tile(ct)] * half_mask(vh, BF16)
-                s = dot(kv[g, keys, tile(kt)], query, 1, 1) + bias[b]
-                p = jnp.exp(s - lse[g, b, j : j + 1, :])
-                dp = dot(kv[g, keys, tile(vt)], grad, 1, 1)
-                ds = (p * (dp - delta[j : j + 1, rows])).astype(BF16)
-                dkv[g, keys, tile(kt)] += dot(ds, query)
-                dkv[g, keys, tile(vt)] += dot(p.astype(BF16), grad)
-                back = dot(kv[g, keys, tile(kt)], ds, 0, 0)
-                made.append(back[kh * HEAD : (kh + 1) * HEAD] * HEAD**-0.5)
-            made.append(jnp.zeros((HEAD, sizes.block), F32))
-            dq[g, rows, :] = jnp.concatenate(made, axis=0).T
+            dq[g, rows, :] = attend_back_block(
+                sizes, me, g, b, kv.at[g], q, bias, lse, dctx, delta, dkv.at[g]
+            )
 
 
 class Loads:
@@ -633,6 +642,681 @@
     out_copy(1, 0, 1).wait()
 
 
+def remote(source, target, send, recv, peer):
+    return pltpu.make_async_remote_copy(
+        src_ref=source,
+        dst_ref=target,
+        send_sem=send,
+        recv_sem=recv,
+        device_id=peer,
+        device_id_type=MESH,
+    )
+
+
+def square(parts, index):
+    side = parts.shape[1]
+    return parts.at[pl.ds(pl.multiple_of(index * side, side), side)]
+
+
+class Spread:
+    def __init__(self, place, source, whole, send, recv, local):
+        self.at, self.source, self.whole = place, source, whole
+        self.send, self.recv, self.local = send, recv, local
+        self.count = source.shape[0]
+
+    def rows(self, mp):
+        return self.whole.at[pl.ds(pl.multiple_of(mp * self.count, 16), self.count)]
+
+    def copy(self, k):
+        at = self.at
+        target = self.rows(at.across if k == 2 else at.mp)
+        source = target if k == 2 else self.source
+        peer = (at.dp, at.across) if k == 1 else at.sibling
+        return remote(source, target, self.send.at[k], self.recv.at[k], peer)
+
+    def own(self):
+        return pltpu.make_async_copy(self.source, self.rows(self.at.mp), self.local)
+
+    def begin(self):
+        self.copy(1).start()
+        self.copy(0).start()
+        self.own().start()
+
+    def forward(self):
+        self.copy(1).wait_recv()
+        self.copy(2).start()
+
+    def end(self):
+        self.copy(0).wait()
+        self.copy(1).wait_send()
+        self.copy(2).wait()
+        self.own().wait()
+
+
+class Scatter:
+    STAGE = (0, 2, 0)
+    HELD = (8, 6, 4)
+
+    def __init__(self, place, parts, inbox, by_second, by_first, by_line, shards, sems):
+        self.at, self.parts, self.inbox, self.shards = place, parts, inbox, shards
+        self.by_second, self.by_first, self.by_line = by_second, by_first, by_line
+        self.core_sems, self.second_sems, self.first_sems, self.line_sems = sems
+        self.rows = shards.shape[1]
+
+    def shard(self, s, g, d):
+        first = (self.HELD[s] + g // 2) * self.parts.shape[1] + d * self.rows
+        return self.parts.at[pl.ds(pl.multiple_of(first, 16), self.rows)]
+
+    def part(self, index):
+        return square(self.parts, index)
+
+    def to_sibling(self, s, k):
+        at = self.STAGE[s] + k
+        return remote(
+            self.part(at),
+            self.inbox.at[at],
+            self.core_sems.at[0, s, k],
+            self.core_sems.at[1, s, k],
+            self.at.sibling,
+        )
+
+    def to_second(self, s, k):
+        g, x = self.at.second_columns[1 - k // 4]
+        return remote(
+            self.shard(s, g, 2 * (k % 4) + x),
+            self.by_second.at[s, k],
+            self.second_sems.at[0, s, k],
+            self.second_sems.at[1, s, k],
+            self.at.second,
+        )
+
+    def to_first(self, s, k):
+        g, x = self.at.first_column
+        return remote(
+            self.shard(s, g, 2 * k + x),
+            self.by_first.at[s, k],
+            self.first_sems.at[0, s, k],
+            self.first_sems.at[1, s, k],
+            self.at.first,
+        )
+
+    def to_line(self, s, j):
+        at = self.at
+        return remote(
+            self.shard(s, at.mp, 2 * at.zs[j] + at.x),
+            self.by_line.at[s, j - 1],
+            self.line_sems.at[0, s, j - 1],
+            self.line_sems.at[1, s, j - 1],
+            at.line[j],
+        )
+
+    def chip_sum(self, s):
+        for k in range(2):
+            self.to_sibling(s, k).wait_recv()
+            held, more = self.part(self.HELD[s] + k), self.inbox.at[self.STAGE[s] + k]
+
+            @pl.loop(0, held.shape[0] // self.rows)
+            def _(d):
+                rows = pl.ds(pl.multiple_of(d * self.rows, 16), self.rows)
+                held[rows, :] = (held[rows, :].astype(F32) + more[rows, :].astype(F32)).astype(BF16)
+
+        for k in range(8):
+            self.to_second(s, k).start()
+
+    def from_second(self, s):
+        g, x = self.at.first_column
+        for k in range(4):
+            self.to_second(s, k).wait_recv()
+            mine = self.shard(s, g, 2 * k + x)
+            mine[...] = (mine[...].astype(F32) + self.by_second[s, k].astype(F32)).astype(BF16)
+            self.to_first(s, k).start()
+
+    def from_first(self, s):
+        at = self.at
+        for k in range(4):
+            self.to_second(s, 4 + k).wait_recv()
+            self.to_first(s, k).wait_recv()
+        for j in (3, 2, 1, 0):
+            z = at.zs[j]
+            mine = self.shard(s, at.mp, 2 * z + at.x)
+            total = (
+                mine[...].astype(F32)
+                + self.by_second[s, 4 + z].astype(F32)
+                + self.by_first[s, z].astype(F32)
+            )
+            if j:
+                mine[...] = total.astype(BF16)
+                self.to_line(s, j).start()
+            else:
+                self.shards[s] = total
+
+    def from_line(self, s):
+        for j in range(1, 4):
+            self.to_line(s, j).wait_recv()
+            self.shards[s] += self.by_line[s, j - 1].astype(F32)
+
+    def sent_to_sibling(self, s):
+        for k in range(2):
+            self.to_sibling(s, k).wait_send()
+
+    def end(self):
+        for s in range(3):
+            for k in range(8):
+                self.to_second(s, k).wait_send()
+            for k in range(4):
+                self.to_first(s, k).wait_send()
+            for j in range(1, 4):
+                self.to_line(s, j).wait_send()
+
+
+class SmallSums:
+    def __init__(self, place, sums, inbox, sems):
+        self.at, self.sums, self.inbox, self.sems = place, sums, inbox, sems
+        at = place
+        self.peers = [at.sibling, (2 * at.z + 1 - at.x, at.mp), (at.dp, at.across), *at.line[1:]]
+
+    def copy(self, k):
+        return remote(
+            self.sums.at[min(k, 3)],
+            self.inbox.at[k],
+            self.sems.at[0, k],
+            self.sems.at[1, k],
+            self.peers[k],
+        )
+
+    def begin(self):
+        self.copy(0).start()
+
+    def step(self, k):
+        self.copy(k).wait_recv()
+        self.sums[k + 1] = self.sums[k] + self.inbox[k]
+        for nxt in (k + 1,) if k < 2 else (3, 4, 5):
+            self.copy(nxt).start()
+
+    def end(self, out):
+        for k in range(3, 6):
+            self.copy(k).wait_recv()
+        out[...] = (self.sums[3] + self.inbox[3]) + (self.inbox[4] + self.inbox[5])
+        for k in range(6):
+            self.copy(k).wait_send()
+
+
+def fold(rows):
+    half = rows.shape[1] // 2
+    return jnp.concatenate([rows[:, :half], rows[:, half:]], axis=0).astype(BF16)
+
+
+def unfold(packed):
+    wide = packed.astype(F32)
+    return jnp.concatenate([wide[:8], wide[8:]], axis=1)
+
+
+class Scoring:
+    def __init__(self, place, ways, cls, gold, passages, scores, lse, buffers, sems):
+        self.at, self.ways, self.cls, self.gold = place, ways, cls, gold
+        self.passages, self.scores, self.lse = passages, scores, lse
+        self.part, self.parts, self.firsts, self.rows = buffers[:4]
+        self.sent, self.got, self.stats, self.got_stats = buffers[4:]
+        self.mp_sems, self.sems = sems
+        at = place
+        self.mates = (at.sibling, (at.dp, at.across), at.diagonal)
+        self.others = [(lax.rem(at.dp + k, ways), at.mp) for k in range(1, ways)]
+
+    def mate(self, k):
+        return remote(
+            self.part, self.parts.at[k], self.mp_sems.at[0, k], self.mp_sems.at[1, k], self.mates[k]
+        )
+
+    def first_copy(self, k):
+        mine = self.firsts.at[self.at.dp]
+        return remote(
+            mine, mine, self.sems.at[0, 0, k - 1], self.sems.at[0, 1, k - 1], self.others[k - 1]
+        )
+
+    def back_copy(self, which, k):
+        peer = self.others[k - 1]
+        return remote(
+            self.sent.at[which, peer[0]],
+            self.got.at[which, self.at.dp],
+            self.sems.at[1 + which, 0, k - 1],
+            self.sems.at[1 + which, 1, k - 1],
+            peer,
+        )
+
+    def stat_copy(self, k):
+        peer = self.others[k - 1]
+        return remote(
+            self.stats.at[peer[0]],
+            self.got_stats.at[self.at.dp],
+            self.sems.at[3, 0, k - 1],
+            self.sems.at[3, 1, k - 1],
+            peer,
+        )
+
+    def start_cls(self):
+        self.part[...] = fold(self.cls[...])
+        for k in range(3):
+            self.mate(k).start()
+
+    def start_gold(self):
+        columns = self.at.dp * self.passages.shape[0] + lax.broadcasted_iota(
+            jnp.int32, (self.gold.shape[0], self.passages.shape[0]), 1
+        )
+        target = jnp.where(self.gold[...] == columns, 1.0, 0.0).astype(BF16)
+        self.put(0, dot(target, self.passages[...]))
+        for k in range(1, self.ways):
+            self.back_copy(0, k).start()
+
+    def put(self, which, rows):
+        for d in range(self.ways):
+            self.sent[which, d] = fold(rows[8 * d : 8 * d + 8])
+        self.got[which, self.at.dp] = self.sent[which, self.at.dp]
+
+    def start_firsts(self):
+        total = self.part[...].astype(F32)
+        for k in range(3):
+            self.mate(k).wait_recv()
+            total = total + self.parts[k].astype(F32)
+        self.firsts[self.at.dp] = total.astype(BF16)
+        for k in range(1, self.ways):
+            self.first_copy(k).start()
+
+    def start_back(self):
+        for k in range(1, self.ways):
+            self.first_copy(k).wait_recv()
+        for d in range(self.ways):
+            self.rows[8 * d : 8 * d + 8, :] = unfold(self.firsts[d])
+        table = dot(self.rows[...].astype(BF16), self.passages[...], 1, 1)
+        self.scores[...] = table
+        peak = jnp.max(table, axis=1, keepdims=True)
+        e = jnp.exp(table - peak)
+        total = jnp.sum(e, axis=1, keepdims=True)
+        lane = lax.broadcasted_iota(jnp.int32, (8, LANES), 1)
+        for d in range(self.ways):
+            rows = slice(8 * d, 8 * d + 8)
+            self.stats[d] = jnp.where(lane == 0, peak[rows], total[rows])
+        self.got_stats[self.at.dp] = self.stats[self.at.dp]
+        for k in range(1, self.ways):
+            self.stat_copy(k).start()
+        self.put(1, dot(e.astype(BF16), self.passages[...]))
+        for k in range(1, self.ways):
+            self.back_copy(1, k).start()
+
+    def result(self):
+        for k in range(1, self.ways):
+            self.back_copy(0, k).wait_recv()
+            self.stat_copy(k).wait_recv()
+        peaks = [self.got_stats[d][:, 0:1] for d in range(self.ways)]
+        top = functools.reduce(jnp.maximum, peaks)
+        scales = [jnp.exp(peak - top) for peak in peaks]
+        total = sum(scale * self.got_stats[d][:, 1:2] for d, scale in enumerate(scales))
+        self.lse[...] = top + jnp.log(total)
+        for k in range(1, self.ways):
+            self.back_copy(1, k).wait_recv()
+        grad = -sum(unfold(self.got[0, d]) for d in range(self.ways))
+        for d in range(self.ways):
+            grad = grad + (scales[d] / total) * unfold(self.got[1, d])
+        return grad
+
+    def end(self):
+        for k in range(3):
+            self.mate(k).wait_send()
+        for k in range(1, self.ways):
+            self.first_copy(k).wait_send()
+            self.back_copy(0, k).wait_send()
+            self.back_copy(1, k).wait_send()
+            self.stat_copy(k).wait_send()
+
+
+class Halo:
+    def __init__(self, sizes, place, dkv, sent, got, sems):
+        self.sizes, self.at, self.dkv, self.sent, self.got, self.sems = sizes, place, dkv, sent, got, sems
+        self.has = (place.mp > 0, place.mp < sizes.groups - 1)
+        offset = sizes.own_offset(place.mp)
+        self.starts = (offset - LONGEST, offset + sizes.own)
+        self.into = (sizes.own - LONGEST, 0)
+
+    def copy(self, g, side):
+        slot = g % 2
+        return remote(
+            self.sent.at[slot, side],
+            self.got.at[g, side],
+            self.sems.at[0, slot, side],
+            self.sems.at[1, g, side],
+            (self.at.dp, self.at.mp + 2 * side - 1),
+        )
+
+    def start(self, g):
+        for side in range(2):
+
+            @pl.when(self.has[side])
+            def _():
+                pl.when(g > 1)(self.copy(g, side).wait_send)
+                rows = pl.ds(pl.multiple_of(self.starts[side], 16), LONGEST)
+                self.sent[g % 2, side] = self.dkv[rows, :].astype(BF16)
+                self.copy(g, side).start()
+
+    def add(self, g, own):
+        for side in range(2):
+
+            @pl.when(self.has[1 - side])
+            def _():
+                self.copy(g, side).wait_recv()
+                rows = pl.ds(self.into[side], LONGEST)
+                own[rows, :] += self.got[g, side].astype(F32)
+
+    def end(self):
+        for side in range(2):
+
+            @pl.when(self.has[side])
+            def _():
+                self.copy(2, side).wait_send()
+                self.copy(3, side).wait_send()
+
+
+def finish_kernel(
+    sizes,
+    lens,
+    cls,
+    gold,
+    gain_1,
+    shift_1,
+    gain_2,
+    r_1,
+    r_2,
+    lse,
+    tokens,
+    cotangent,
+    passages,
+    encoded,
+    weights,
+    n_1_in,
+    n_2_in,
+    z_in,
+    slope_in,
+    kv_in,
+    q_in,
+    ctx_in,
+    scores,
+    query_lse,
+    small_out,
+    shards,
+    encoded_whole,
+    token_whole,
+    w,
+    ffn,
+    parts,
+    inbox,
+    by_second,
+    by_first,
+    by_line,
+    kv,
+    q,
+    ctx,
+    dctx,
+    dkv,
+    own_kv,
+    halo_sent,
+    halo_got,
+    n_1,
+    work,
+    rows_low,
+    row_in,
+    turned,
+    low,
+    bias,
+    delta,
+    sums,
+    sums_in,
+    part,
+    parts_in,
+    firsts,
+    first_rows,
+    back_sent,
+    back_got,
+    stats,
+    stats_got,
+    load_sems,
+    kv_sems,
+    ffn_sems,
+    spread_sems,
+    core_sems,
+    second_sems,
+    first_sems,
+    line_sems,
+    halo_sems,
+    small_sems,
+    mp_sems,
+    score_sems,
+):
+    at = Place()
+    me = at.mp
+    own_rows = pl.ds(pl.multiple_of(sizes.own * me, 16), sizes.own)
+    ways = firsts.shape[0]
+    table = parts.at[pl.ds(Scatter.HELD[0] * sizes.width, passages.shape[0])]
+    scatter = Scatter(
+        at, parts, inbox, by_second, by_first, by_line, shards,
+        (core_sems, second_sems, first_sems, line_sems),
+    )
+    halo = Halo(sizes, at, dkv, halo_sent, halo_got, halo_sems)
+    spread = Spread(at, encoded, encoded_whole, spread_sems.at[0, 0], spread_sems.at[0, 1], load_sems.at[8])
+    token_spread = Spread(
+        at, rows_low, token_whole, spread_sems.at[1, 0], spread_sems.at[1, 1], load_sems.at[9]
+    )
+    small = SmallSums(at, sums, sums_in, small_sems)
+
+    def load(k, source, target):
+        return pltpu.make_async_copy(source, target, load_sems.at[k])
+
+    loads = [
+        load(0, passages, table),
+        load(1, cotangent.at[own_rows], row_in),
+        load(2, n_2_in, work.at[1]),
+        load(3, n_1_in, n_1),
+        load(5, q_in, q),
+        load(6, ctx_in, ctx),
+    ]
+
+    def kv_load(g):
+        return pltpu.make_async_copy(kv_in.at[g], kv.at[g % 2], kv_sems.at[g % 2])
+
+    for copy in loads:
+        copy.start()
+    kv_load(0).start()
+
+    def group_of(i):
+        return jnp.where(i < 2, 1 - at.core + 2 * i, at.core + 2 * (i - 2))
+
+    def ffn_loads(i):
+        slot, g = i % 2, group_of(i)
+        return [
+            pltpu.make_async_copy(weights.at[2, g], w.at[2 * slot], ffn_sems.at[slot, 0]),
+            pltpu.make_async_copy(weights.at[1, g], w.at[2 * slot + 1], ffn_sems.at[slot, 1]),
+            pltpu.make_async_copy(z_in.at[g], ffn.at[slot, 0], ffn_sems.at[slot, 2]),
+            pltpu.make_async_copy(slope_in.at[g], ffn.at[slot, 1], ffn_sems.at[slot, 3]),
+        ]
+
+    for copy in ffn_loads(0):
+        copy.start()
+
+    scoring = Scoring(
+        at,
+        ways,
+        cls,
+        gold,
+        table,
+        scores,
+        query_lse,
+        (part, parts_in, firsts, first_rows, back_sent, back_got, stats, stats_got),
+        (mp_sems, score_sems),
+    )
+    greet([*scoring.mates, *scoring.others])
+    scoring.start_cls()
+    loads[0].wait()
+    scoring.start_gold()
+    scoring.start_firsts()
+    spread.begin()
+    fill_mask(sizes, me, lens, bias)
+    picked = start_rows(sizes, me, lens).astype(BF16)
+    loads[3].wait()
+    turned[1] = (n_1[...] * gain_1[...] + shift_1[...]).T.astype(BF16)
+    scoring.start_back()
+    loads[1].wait()
+    loads[2].wait()
+    dcls = scoring.result()
+    high = dcls.astype(BF16)
+    rest = (dcls - high.astype(F32)).astype(BF16)
+    dy = row_in[...].astype(F32) + dot(picked, high, 0, 0) + dot(picked, rest, 0, 0)
+    mine = sums.at[0]
+    mine[0:1, :] = jnp.sum(dy * work[1], axis=0, keepdims=True)
+    mine[1:2, :] = jnp.sum(dy, axis=0, keepdims=True)
+    grad = norm_back(dy, work[1], r_2[...], gain_2[...])
+    mine[2:3, :] = jnp.sum(grad, axis=0, keepdims=True)
+    work[0] = grad
+    rows_low[...] = grad.astype(BF16)
+    turned[0] = grad.T.astype(BF16)
+
+    for half in range(2):
+
+        @pl.loop(2 * half, 2 * half + 2)
+        def _(i):
+            slot, g = i % 2, group_of(i)
+            for copy in ffn_loads(i):
+                copy.wait()
+
+            @pl.when(i < 3)
+            def _():
+                for copy in ffn_loads(i + 1):
+                    copy.start()
+
+            k = i - 2 * half
+            into = [(Scatter.HELD if half else Scatter.STAGE)[s] + k for s in range(3)]
+            square(parts, into[2])[...] = dot(turned[0], ffn[slot, 0]).astype(BF16)
+            if not half:
+                scatter.to_sibling(2, k).start()
+            da = dot(rows_low[...], w[2 * slot]) * ffn[slot, 1].astype(F32)
+            mine[pl.ds(8 + g, 1), :] = jnp.sum(da, axis=0, keepdims=True)
+            da_low = da.astype(BF16)
+            square(parts, into[1])[...] = dot(turned[1], da_low).astype(BF16)
+            if not half:
+                scatter.to_sibling(1, k).start()
+            work[0] += dot(da_low, w[2 * slot + 1], 1, 1)
+
+    load_w = pltpu.make_async_copy(weights.at[0], w, load_sems.at[7])
+    load_w.start()
+    load_x = load(1, tokens.at[own_rows], row_in)
+    load_x.start()
+    scatter.chip_sum(2)
+    scatter.chip_sum(1)
+    scatter.sent_to_sibling(2)
+
+    dy = work[0]
+    mine[3:4, :] = jnp.sum(dy * n_1[...], axis=0, keepdims=True)
+    mine[4:5, :] = jnp.sum(dy, axis=0, keepdims=True)
+    grad = norm_back(dy, n_1[...], r_1[...], gain_1[...])
+    mine[5:6, :] = jnp.sum(grad, axis=0, keepdims=True)
+    mine[6:8, :] = jnp.zeros((2, sizes.width), F32)
+    mine[12:24, :] = jnp.zeros((12, sizes.width), F32)
+    work[1] = grad
+    rows_low[...] = grad.astype(BF16)
+    turned[0] = grad.T.astype(BF16)
+    load_x.wait()
+    turned[1] = row_in[...].astype(F32).T.astype(BF16)
+    spread.forward()
+    load_w.wait()
+    for copy in loads[4:]:
+        copy.wait()
+
+    @pl.loop(0, sizes.groups)
+    def _(g):
+        dctx[g] = dot(rows_low[...], w[g, :, tile(4, 2)]).astype(BF16)
+
+    def step(k):
+        if k == 2:
+            scatter.from_second(2)
+        elif k == 4:
+            scatter.from_first(2)
+        elif k == 5:
+            scatter.from_second(1)
+        elif k == 6:
+            scatter.from_line(2)
+
+    def tick(now):
+        for k in (2, 4, 5, 6):
+            pl.when(now == k)(functools.partial(step, k))
+
+    def finalize(g):
+        slot = g % 2
+        halo.add(g, own_kv.at[slot])
+        dkv_own = own_kv[slot]
+        mine[pl.ds(16 + g, 1), tile(0, 3)] = jnp.sum(dkv_own, axis=0, keepdims=True)
+        low[slot, :, tile(0, 3)] = dkv_own.astype(BF16)
+        work[1] += dot(low[slot], w[g, :, tile(0, 5)], 1, 1)
+        into = jnp.where(g % 2 == at.core, Scatter.HELD[0], Scatter.STAGE[0]) + g // 2
+        made = dot(turned[1], low[slot])
+        more = dot(turned[0], ctx[g])
+        target = square(parts, into)
+        target[:, tile(0, 4)] = made[:, tile(0, 4)].astype(BF16)
+        target[:, tile(4)] = (made[:, tile(4)] + more[:, tile(0)]).astype(BF16)
+        target[:, tile(5)] = more[:, tile(1)].astype(BF16)
+
+        @pl.when(g % 2 != at.core)
+        def _():
+            scatter.to_sibling(0, g // 2).start()
+
+    own = pl.ds(sizes.own_offset(me), sizes.own)
+
+    @pl.loop(0, sizes.groups)
+    def _(g):
+        slot = g % 2
+        kv_load(g).wait()
+
+        @pl.when(g < sizes.groups - 1)
+        def _():
+            kv_load(g + 1).start()
+
+        delta[...] = delta_rows(dctx[g], ctx[g])
+        dkv[...] = jnp.zeros_like(dkv)
+        for b in range(sizes.blocks):
+            tick(g * sizes.blocks + b)
+            rows = slice(b * sizes.block, (b + 1) * sizes.block)
+            dq = attend_back_block(
+                sizes, me, g, b, kv.at[slot], q, bias, lse, dctx, delta, dkv
+            )
+            total = jnp.sum(dq, axis=0, keepdims=True)
+            mine[pl.ds(16 + g, 1), tile(3, 2)] += total
+            low[slot, rows, tile(3, 2)] = dq.astype(BF16)
+        halo.start(g)
+        own_kv[slot] = dkv[own, :]
+
+        @pl.when(g > 0)
+        def _():
+            finalize(g - 1)
+
+    scatter.from_first(1)
+    finalize(sizes.groups - 1)
+    small.begin()
+    rows_low[...] = work[1].astype(BF16)
+    scatter.chip_sum(0)
+    token_spread.begin()
+    small.step(0)
+    scatter.from_line(1)
+    scatter.from_second(0)
+    small.step(1)
+    scatter.from_first(0)
+    small.step(2)
+    token_spread.forward()
+    scatter.from_line(0)
+    small.end(small_out)
+    scatter.sent_to_sibling(1)
+    scatter.sent_to_sibling(0)
+    scatter.end()
+    halo.end()
+    scoring.end()
+    spread.end()
+    token_spread.end()
+
+
 def input_kernel(sizes, tokens, weights, dkv, dq, dh_1, grads_out, token_grad, grads, small, turned, low):
     turned[...] = tokens[...].astype(F32).T.astype(BF16)
     total = dh_1[...]
@@ -654,7 +1338,7 @@
 
 
 def params(**more):
-    return pltpu.CompilerParams(vmem_limit_bytes=62 * 2**20, **more)
+    return pltpu.CompilerParams(vmem_limit_bytes=63 * 2**20, **more)
 
 
 def run_forward(sizes, lengths, tokens, weights, biases, rows, gathers):
@@ -767,6 +1451,80 @@
     )(own_tokens, w_attn, dkv, dq, dh_1, grads_out)
 
 
+def run_finish(sizes, small_in, large_in):
+    own, width, groups = sizes.own, sizes.width, sizes.groups
+    tokens, passages = large_in[0], large_in[2]
+    queries = small_in[2].shape[0]
+    ways = queries // 8
+    shard = width // ways
+    shape = jax.ShapeDtypeStruct
+    outs = (
+        shape((queries, passages.shape[0]), F32),
+        shape((8, 1), F32),
+        shape((24, width), F32),
+        shape((3, shard, width), F32),
+        shape(tokens.shape, BF16),
+        shape(tokens.shape, BF16),
+    )
+    dma = pltpu.SemaphoreType.DMA
+    scratch = [
+        pltpu.VMEM((groups, width, width), BF16),
+        pltpu.VMEM((2, 2, own, width), BF16),
+        pltpu.VMEM((10 * width, width), BF16),
+        pltpu.VMEM((4, width, width), BF16),
+        pltpu.VMEM((3, 8, shard, width), BF16),
+        pltpu.VMEM((3, 4, shard, width), BF16),
+        pltpu.VMEM((3, 3, shard, width), BF16),
+        pltpu.VMEM((2, sizes.window, 3 * LANES), BF16),
+        pltpu.VMEM((groups, own, 2 * LANES), BF16),
+        pltpu.VMEM((groups, own, 2 * LANES), BF16),
+        pltpu.VMEM((groups, own, 2 * LANES), BF16),
+        pltpu.VMEM((sizes.window, 3 * LANES), F32),
+        pltpu.VMEM((2, own, 3 * LANES), F32),
+        pltpu.VMEM((2, 2, LONGEST, 3 * LANES), BF16),
+        pltpu.VMEM((groups, 2, LONGEST, 3 * LANES), BF16),
+        pltpu.VMEM((own, width), F32),
+        pltpu.VMEM((2, own, width), F32),
+        pltpu.VMEM((own, width), BF16),
+        pltpu.VMEM((own, width), BF16),
+        pltpu.VMEM((2, width, own), BF16),
+        pltpu.VMEM((2, own, 5 * LANES), BF16),
+        pltpu.VMEM((sizes.blocks, sizes.keys, sizes.block), F32),
+        pltpu.VMEM((8, own), F32),
+        pltpu.VMEM((4, 24, width), F32),
+        pltpu.VMEM((6, 24, width), F32),
+        pltpu.VMEM((16, width // 2), BF16),
+        pltpu.VMEM((3, 16, width // 2), BF16),
+        pltpu.VMEM((ways, 16, width // 2), BF16),
+        pltpu.VMEM((queries, width), F32),
+        pltpu.VMEM((2, ways, 16, width // 2), BF16),
+        pltpu.VMEM((2, ways, 16, width // 2), BF16),
+        pltpu.VMEM((ways, 8, LANES), F32),
+        pltpu.VMEM((ways, 8, LANES), F32),
+        dma((10,)),
+        dma((2,)),
+        dma((2, 4)),
+        dma((2, 2, 3)),
+        dma((2, 3, 2)),
+        dma((2, 3, 8)),
+        dma((2, 3, 4)),
+        dma((2, 3, 3)),
+        dma((2, 4, 2)),
+        dma((2, 6)),
+        dma((2, 3)),
+        dma((4, 2, ways - 1)),
+    ]
+    return pl.pallas_call(
+        functools.partial(finish_kernel, sizes),
+        out_shape=outs,
+        in_specs=specs(SMEM, *[VMEM] * (len(small_in) - 1), *[ANY] * len(large_in)),
+        out_specs=specs(*[VMEM] * 4, ANY, ANY),
+        scratch_shapes=scratch,
+        compiler_params=params(collective_id=1, has_side_effects=True),
+        name="finish",
+    )(*small_in, *large_in)
+
+
 def cut_along(array, dim, devices):
     before, after = (array.shape[:dim], array.shape[dim + 1 :])
     return jnp.moveaxis(array.reshape(*before, devices, -1, *after), dim, 0)
@@ -791,6 +1549,39 @@
     target = (gold[:, None] == columns[None, :]).astype(F32)
     grad = dot((soft - target).astype(BF16), passages)
     return table, lse, summed_on_arrival(grad.astype(BF16), "dp", 0)
+
+
+def plain_layer(sizes, tokens, cotangent, lengths, gold, passages, packed, own_bias, rows):
+    me, groups = lax.axis_index("mp"), sizes.groups
+    whole = lax.all_gather(lax.all_gather(packed, "dp", axis=1, tiled=True), "mp", axis=1)
+    biases = lax.all_gather(own_bias, "mp", axis=0)
+    encoded, cls, *saved = run_forward(sizes, lengths, tokens, whole, biases, rows, False)
+    cls = lax.psum(cls, "mp").astype(BF16)
+    table, lse, dcls = score(cls, passages, gold)
+    n_1, r_1, n_2, r_2, z, slope, kv, q, logs, ctx = saved
+    dh_1, dkv, dq, grads_ffn, grads_out, small = run_backward(
+        sizes, lengths, cotangent, dcls, whole, rows[1], rows[2], rows[4], saved
+    )
+    halo, own = LONGEST, sizes.own
+    offset = own * me - sizes.window_start(me)
+    to_left = lax.dynamic_slice_in_dim(dkv, offset - halo, halo, axis=1).astype(BF16)
+    to_right = lax.dynamic_slice_in_dim(dkv, offset + own, halo, axis=1).astype(BF16)
+    from_right = lax.ppermute(to_left, "mp", [(i, i - 1) for i in range(1, groups)])
+    from_left = lax.ppermute(to_right, "mp", [(i, i + 1) for i in range(groups - 1)])
+    dkv = lax.dynamic_slice_in_dim(dkv, offset, own, axis=1)
+    dkv = dkv.at[:, own - halo :].add(from_right.astype(F32))
+    dkv = dkv.at[:, :halo].add(from_left.astype(F32))
+    own_tokens = lax.dynamic_slice_in_dim(tokens, own * me, own, axis=0)
+    token_part, grads_attn, small_attn = run_input(
+        sizes, own_tokens, whole[0], dkv, dq, dh_1, grads_out
+    )
+    token_grad = lax.all_gather(token_part, "mp", axis=0, tiled=True).astype(F32)
+    encoded = lax.all_gather(encoded, "mp", axis=0, tiled=True)
+    grads = jnp.stack([grads_attn, grads_ffn[0], grads_ffn[1]])
+    grads = summed_on_arrival(grads, "mp", 1)[:, 0].astype(BF16)
+    grads = summed_on_arrival(grads, "dp", 1)
+    small, small_attn = lax.psum((small, small_attn), ("dp", "mp"))
+    return table, lse, encoded, token_grad, grads, small, small_attn[:, 0]
 
 
 def body(
@@ -825,42 +1616,23 @@
     zeros = jnp.zeros((head_cols,), F32)
     own_bias = jnp.concatenate([zeros, b_value, b_query, zeros[:HEAD], b_up])[None]
     rows = [r[None] for r in (b_out, gain_attn, shift_attn, b_down, gain_ffn, shift_ffn)]
+    c = head_cols
     if lax.axis_size("dp") == 8 and groups == 4:
-        whole, encoded, cls, *saved = run_forward(
+        whole, encoded, cls, n_1, r_1, n_2, r_2, z, slope, kv, q, logs, ctx = run_forward(
             sizes, lengths, tokens, packed, own_bias, rows, True
         )
+        table, lse, small, grads, encoded, token_part = run_finish(
+            sizes,
+            (lengths, cls, gold[:, None], rows[1], rows[2], rows[4], r_1, r_2, logs),
+            (tokens, cotangent, passages, encoded, whole, n_1, n_2, z, slope, kv, q, ctx),
+        )
+        lse, token_grad, small_attn = lse[:, 0], token_part.astype(F32), small[16:20]
     else:
-        whole = lax.all_gather(lax.all_gather(packed, "dp", axis=1, tiled=True), "mp", axis=1)
-        biases = lax.all_gather(own_bias, "mp", axis=0)
-        encoded, cls, *saved = run_forward(sizes, lengths, tokens, whole, biases, rows, False)
-    cls = lax.psum(cls, "mp").astype(BF16)
-    table, lse, dcls = score(cls, passages, gold)
-    n_1, r_1, n_2, r_2, z, slope, kv, q, logs, ctx = saved
-    dh_1, dkv, dq, grads_ffn, grads_out, small = run_backward(
-        sizes, lengths, cotangent, dcls, whole, rows[1], rows[2], rows[4], saved
-    )
-    halo, own = LONGEST, sizes.own
-    offset = own * me - sizes.window_start(me)
-    to_left = lax.dynamic_slice_in_dim(dkv, offset - halo, halo, axis=1).astype(BF16)
-    to_right = lax.dynamic_slice_in_dim(dkv, offset + own, halo, axis=1).astype(BF16)
-    from_right = lax.ppermute(to_left, "mp", [(i, i - 1) for i in range(1, groups)])
-    from_left = lax.ppermute(to_right, "mp", [(i, i + 1) for i in range(groups - 1)])
-    dkv = lax.dynamic_slice_in_dim(dkv, offset, own, axis=1)
-    dkv = dkv.at[:, own - halo :].add(from_right.astype(F32))
-    dkv = dkv.at[:, :halo].add(from_left.astype(F32))
-    own_tokens = lax.dynamic_slice_in_dim(tokens, own * me, own, axis=0)
-    token_part, grads_attn, small_attn = run_input(
-        sizes, own_tokens, whole[0], dkv, dq, dh_1, grads_out
-    )
-    token_grad = lax.all_gather(token_part, "mp", axis=0, tiled=True).astype(F32)
-    encoded = lax.all_gather(encoded, "mp", axis=0, tiled=True)
-    grads = jnp.stack([grads_attn, grads_ffn[0], grads_ffn[1]])
-    grads = summed_on_arrival(grads, "mp", 1)[:, 0].astype(BF16)
-    grads = summed_on_arrival(grads, "dp", 1)
-    small, small_attn = lax.psum((small, small_attn), ("dp", "mp"))
-    mine = lax.dynamic_index_in_dim(small_attn[:, 0], me, 0, keepdims=False)
+        table, lse, encoded, token_grad, grads, small, small_attn = plain_layer(
+            sizes, tokens, cotangent, lengths, gold, passages, packed, own_bias, rows
+        )
+    mine = lax.dynamic_index_in_dim(small_attn, me, 0, keepdims=False)
     up_bias = lax.dynamic_index_in_dim(small, 8 + me, 0, keepdims=False)
-    c = head_cols
     return (
         table,
         lse,

time: 619 us -> 258 us (0.42)
  waiting for transfers between devices: 175 us -> 0 us
  blocking collectives: 163 us -> 0 us
  Pallas kernels: 149 us -> 228 us
  starting transfers between devices: 34.9 us -> 0 us
  other arithmetic: 35.2 us -> 8.6 us
  local copies, waits for them, and re-layouts: 42.4 us -> 18.3 us
  between operations: 14.3 us -> 0.75 us
    all_to_all x3 -> x0, waiting for transfers between devices: 172 us -> none  [summed_on_arrival(): lax.all_to_all(pieces, axis, split_axis=0, concat_axis=0, tiled=True)]
    psum x3 -> x0, blocking collectives: 123 us -> none  [the longest x1 98.3 us: body(): small, small_attn = lax.psum((small, small_attn), ('dp', 'mp'))]
    pallas_call x2 -> x1, Pallas kernels: 64.8 us -> 143 us  [run_finish(): pl.pallas_call(functools.partial(finish_kernel, sizes), out_shape=outs, i...]
    all_gather x1 -> x0, blocking collectives: 24.3 us -> none  [score(): all_first = lax.all_gather(cls, 'dp', axis=0, tiled=True)]
    ppermute x2 -> x0, starting transfers between devices: 20 us -> none  [the longest x1 16.7 us: body(): lax.ppermute(to_left, 'mp', [(i, i - 1) for i in range(1, groups)])]
    pmax x1 -> x0, blocking collectives: 16.2 us -> none  [score(): peak = lax.pmax(jnp.max(table, axis=1), 'dp')]
    all_to_all x3 -> x0, starting transfers between devices: 14.8 us -> none  [summed_on_arrival(): lax.all_to_all(pieces, axis, split_axis=0, concat_axis=0, tiled=True)]
    reduce_sum x4 -> x0, other arithmetic: 13.8 us -> none  [the longest x3 13.6 us: summed_on_arrival(): return arrived.astype(F32).sum(axis=0)]
  transfers between devices with their start and end apart: 7 -> 0, of which waited for: 3 -> 0; matrix products, arithmetic and copies ran while one was open for 5% -> 0% of each run, Pallas kernels for 0% -> 0%
where the time goes in v3:
time: 258 us; the launch traced here: 255 us
  Pallas kernels  228 us (88%)
  local copies, waits for them, and re-layouts  18.3 us (7%)
  other arithmetic  8.6 us (3%)
    pallas_call x1, Pallas kernels, run_finish(): pl.pallas_call(functools.partial(finish_kernel, sizes), out_shape=outs, i...  143 us
    pallas_call x1, Pallas kernels, run_forward(): pl.pallas_call(functools.partial(kernel, sizes), out_shape=outs, in_specs...  84.2 us
    broadcast_in_dim x6, local copies, waits for them, and re-layouts, body(): r[None]  7.6 us
    convert_element_type x1, other arithmetic, body(): token_part.astype(F32)  5.23 us

profile of v3, /device:TPU:1, one launch (start us, length us, event | category | flops | bytes accessed | tf_op | source)
XLA Modules:
  0.0 255.4 jit_solution(8478155498384426630)
XLA Ops:
  0.7 0.0 copy-start.4
  0.7 1.3 broadcast_in_dim.30.rest_1_.gain_1
  1.9 1.3 broadcast_in_dim.31.rest_2_.shift_1
  3.2 1.3 broadcast_in_dim.33.rest_4_.gain_2
  4.5 0.9 copy.42
  5.4 1.0 maximum_bitcast_fusion
  6.3 1.8 pad_maximum_fusion.packed
  8.1 0.8 concatenate.7
  8.9 0.6 broadcast_in_dim.28.own_bias
  9.5 1.3 broadcast_in_dim.29.rest_0_
  10.8 1.3 broadcast_in_dim.32.rest_3_
  12.1 1.3 broadcast_in_dim.34.rest_5_
  13.3 84.2 %forward.1 = (bf16[3,4,768,768]{3,2,1,0:T(8,128)(2,1)}, bf16[512,768]{1,0:T(8,128)(2,1)}, f32[8,768]{1,0:T(8,128)}, f32[512,768]{1,0:T(8,128)}, f32[512,1]{1,0:T...) custom-call(s32[1,8]{1,0:T(1,128)} %lens.3, ...), custom_call_target="tpu_custom_call" | custom-call | tf_op jit(solution)/shard_map/forward/pallas_call | solution.py:1387
  97.5 0.0 copy-done.4
  97.5 0.7 copy.43.gold
  98.2 143.5 %finish.1 = (f32[64,1024]{1,0:T(8,128)}, f32[8,1]{1,0:T(8,128)}, f32[24,768]{1,0:T(8,128)}, f32[3,96,768]{2,1,0:T(8,128)}, bf16[2048,768]{1,0:T(8,128)(2,1)}, /*index=5*/bf16[2048,768]{1,0:T(8,128)(2,1)}) custom-call(s32[1,8]{1,0:T(1,128)} %lens.3, f32[8,768]{1,0:T(8,128)} %get-tuple-element.38.cls, s32[64,1]{1,0:T(8,128)} %copy.43.gold, ...), custom_call_target="tpu_custom_call" | custom-call | tf_op jit(solution)/shard_map/finish/pallas_call | solution.py:1517
  241.8 0.0 copy-start.1
  241.8 0.0 copy-start.3
  241.8 0.0 copy-start.2
  241.8 0.0 copy-start
  241.8 5.2 %convert_element_type.3 = f32[2048,768]{1,0:T(8,128)} convert(bf16[2048,768]{1,0:T(8,128)(2,1)} %get-tuple-element.54) | non-fusion elementwise | flops 1572864 | bytes 9437184 | tf_op jit(solution)/shard_map/convert_element_type | solution.py:1629
  247.0 0.0 copy-done.1
  247.0 0.8 slice_bitcast_fusion
  247.9 0.7 slice_bitcast_fusion.2
  248.6 0.7 copy.44
  249.4 1.6 slice_reduce_fusion
  251.0 0.7 slice.58
  251.7 0.6 fusion
  252.4 0.0 copy-done.3
  252.4 0.6 reduce
  253.0 0.0 copy-done.2
  253.0 0.7 copy.47
  253.7 0.0 copy-done
  253.7 1.7 copy.48
  (2 shorter events, 0.0 us)
Async XLA Ops:
  0.7 96.9 %copy-start.4 = (s32[64]{0:T(128)S(1)}, s32[64]{0:T(128)}, u32[]{:S(2)}) copy-start(s32[64]{0:T(128)} %param.23) | copy-start | bytes 772
  241.8 5.3 %copy-start.1 = (f32[3,96,768]{2,1,0:T(8,128)S(1)}, f32[3,96,768]{2,1,0:T(8,128)}, u32[]{:S(2)}) copy-start(f32[3,96,768]{2,1,0:T(8,128)} %get-tuple-element.55) | copy-start | bytes 2654212
  241.8 10.6 %copy-start.3 = (f32[8,1]{1,0:T(8,128)S(1)}, f32[8,1]{1,0:T(8,128)}, u32[]{:S(2)}) copy-start(f32[8,1]{1,0:T(8,128)} %get-tuple-element.52) | copy-start | bytes 100
  241.8 11.2 %copy-start.2 = (f32[64,1024]{1,0:T(8,128)S(1)}, f32[64,1024]{1,0:T(8,128)}, u32[]{:S(2)}) copy-start(f32[64,1024]{1,0:T(8,128)} %get-tuple-element.129) | copy-start | bytes 786436
  241.8 11.9 %copy-start = (bf16[2048,768]{1,0:T(8,128)(2,1)S(1)}, bf16[2048,768]{1,0:T(8,128)(2,1)}, u32[]{:S(2)}) copy-start(bf16[2048,768]{1,0:T(8,128)(2,1)} %get-tuple-element.131) | copy-start | bytes 9437188

commit v4 on v3

--- a/solution.py
+++ b/solution.py
@@ -60,6 +60,10 @@
     return a * phi, phi + a * bell * 0.3989422804014327
 
 
+def as_row(ref):
+    return ref[...].reshape(1, ref.shape[0])
+
+
 class Sizes:
     def __init__(self, length, width, groups):
         self.length, self.width, self.groups = length, width, groups
@@ -121,12 +125,13 @@
     return picked
 
 
-def project(sizes, me, tokens, w_attn, biases, kv, q):
+def project(sizes, me, group, span, tokens, w_attn, biases, kv, q):
     cut = sizes.window // 2
     own = pl.ds(sizes.own_offset(me), sizes.own)
 
-    @pl.loop(0, sizes.groups)
-    def _(g):
+    @pl.loop(*span)
+    def _(i):
+        g = group(i)
         for part in range(2):
             rows = pl.ds(part * cut, cut)
             made = dot(tokens[rows, :], w_attn[g, :, tile(0, 3)]) + biases[g, :, tile(0, 3)]
@@ -135,13 +140,14 @@
         q[g] = made.astype(BF16) * jnp.asarray(HEAD**-0.5, BF16)
 
 
-def attend(sizes, me, kv, q, bias, lse, ctx, tick=None):
-    @pl.loop(0, sizes.groups)
-    def _(g):
+def attend(sizes, me, group, span, tick, kv, q, bias, lse, ctx):
+    @pl.loop(*span)
+    def _(i):
+        g = group(i)
+
         @pl.loop(0, sizes.blocks)
         def _(b):
-            if tick is not None:
-                tick(g * sizes.blocks + b)
+            tick(i * sizes.blocks + b)
             keys = pl.ds(sizes.key_offset(me, b), sizes.keys)
             rows = pl.ds(pl.multiple_of(b * sizes.block, sizes.block), sizes.block)
             made = [jnp.zeros((HEAD, sizes.block), F32)]
@@ -216,6 +222,15 @@
         for copy in self.copies:
             copy.start()
 
+    def group(self, i):
+        return i
+
+    def near_heads(self):
+        self.copies[0].wait()
+
+    def far_heads(self):
+        pass
+
     def ready(self, section):
         self.copies[section].wait()
 
@@ -227,6 +242,17 @@
 
 
 MESH = pl.DeviceIdType.MESH
+
+
+class Route:
+    def __init__(self, at, turn):
+        flip, x_peer = 1 - turn, 2 * at.z + 1 - at.x
+        near = at.mp + turn * (at.across - at.mp)
+        far = at.mp + flip * (at.across - at.mp)
+        self.first = (at.dp + flip * (x_peer - at.dp), near)
+        self.second = (at.dp + turn * (x_peer - at.dp), far)
+        self.first_column = (near, at.x + flip * (1 - 2 * at.x))
+        self.second_columns = ((far, at.x + turn * (1 - 2 * at.x)), (at.across, 1 - at.x))
 
 
 class Place:
@@ -236,38 +262,54 @@
         flip = 1 - self.core
         self.across = 2 * (1 - self.y) + self.core
         self.sibling = (self.dp, 2 * self.y + flip)
-        x_peer = 2 * self.z + 1 - self.x
-        self.first = (self.dp + flip * (x_peer - self.dp), self.mp + self.core * (self.across - self.mp))
-        self.second = (self.dp + self.core * (x_peer - self.dp), self.mp + flip * (self.across - self.mp))
+        self.x_peer = (2 * self.z + 1 - self.x, self.mp)
+        self.y_peer = (self.dp, self.across)
+        self.diagonal = (self.dp, 2 * (1 - self.y) + flip)
         self.zs = [self.z, self.z + 1 - 2 * (self.z % 2), (self.z + 2) % 4, 3 - self.z]
         self.line = [(2 * z + self.x, self.mp) for z in self.zs]
+        self.by_core = Route(self, self.core)
+        self.x_first, self.y_first = Route(self, 0), Route(self, 1)
         self.own_column = (self.mp, self.x)
-        self.first_column = (
-            self.mp + self.core * (self.across - self.mp),
-            self.x + flip * (1 - 2 * self.x),
-        )
-        self.second_columns = (
-            (self.mp + flip * (self.across - self.mp), self.x + self.core * (1 - 2 * self.x)),
-            (self.across, 1 - self.x),
-        )
-        self.diagonal = (self.dp, 2 * (1 - self.y) + flip)
-        self.peers = [*self.line[1:], self.first, self.second, self.sibling, self.diagonal]
-
-
-def greet(peers):
+        self.peers = [*self.line[1:], self.x_peer, self.y_peer, self.sibling, self.diagonal]
+
+
+def signal(peers):
     barrier = pltpu.get_barrier_semaphore()
     for peer in peers:
         pl.semaphore_signal(barrier, inc=1, device_id=peer, device_id_type=MESH)
-    pl.semaphore_wait(barrier, len(peers))
+
+
+def arrive(peers):
+    pl.semaphore_wait(pltpu.get_barrier_semaphore(), len(peers))
+
+
+GATHER_STEPS = {
+    "begin": (("along", 0), ("out", 0), ("out", 1), ("out", 2)),
+    "near": (("z", 0, 1, 2, 3), ("along", 1), ("first", 0, 0, 1, 2, 3)),
+    0: (("z", 1, 1, 2, 3), ("along", 2)),
+    1: (("second", 0, 0, 1, 2, 3),),
+    2: (("first", 1, 0, 1), ("second", 0, 4, 5)),
+    3: (("first", 1, 2, 3), ("second", 0, 6, 7)),
+    4: (("z", 2, 1, 2, 3),),
+    5: (("second", 1, 0, 1, 2, 3),),
+    6: (("second", 1, 4, 5, 6, 7),),
+    7: (("first", 2, 0, 1),),
+    8: (("first", 2, 2, 3),),
+    9: (("second", 2, 0, 1, 2, 3, 4, 5, 6, 7),),
+}
 
 
 class Gather:
+    ROUTES = ("x_first", "by_core", "by_core")
+    Z_LATER = (False, False, False)
+
     def __init__(self, place, packed, own_bias, w, biases, kept, send, recv, local, bias_sems):
         self.at, self.packed, self.w, self.kept = place, packed, w, kept
         self.own_bias, self.biases = own_bias, biases
         self.send_sems, self.recv_sems, self.local, self.bias_sems = send, recv, local, bias_sems
-        self.rows = packed.shape[1]
+        self.rows = packed[1].shape[0]
         self.shards = w.shape[2] // self.rows
+        self.routes = [getattr(place, name) for name in self.ROUTES]
 
     def shard(self, s, g, d):
         return self.w.at[s, g, pl.ds(pl.multiple_of(d * self.rows, 16), self.rows)]
@@ -288,50 +330,55 @@
 
     def own_copy(self, s):
         return pltpu.make_async_copy(
-            self.packed.at[s], self.shard(s, self.at.mp, self.at.dp), self.local.at[s]
+            self.packed[s], self.shard(s, self.at.mp, self.at.dp), self.local.at[s]
         )
 
     def along_z(self, s):
         at = self.at
         for k in range(1, 4):
-            self.copy(s, at.mp, at.dp, k - 1, at.line[k], self.packed.at[s]).start()
+            self.copy(s, at.mp, at.dp, k - 1, at.line[k], self.packed[s]).start()
 
     def own_out(self, s):
         at = self.at
         self.own_copy(s).start()
-        source = self.packed.at[s]
-        self.copy(s, at.mp, at.dp, 3, at.first, source).start()
-        self.copy(s, at.mp, at.dp, 7, at.second, source).start()
+        source = self.packed[s]
+        self.copy(s, at.mp, at.dp, 3, self.routes[s].first, source).start()
+        self.copy(s, at.mp, at.dp, 7, self.routes[s].second, source).start()
         self.copy(s, at.mp, at.dp, 15, at.sibling, source).start()
 
     def from_z(self, s, k):
         at, (g, x) = self.at, self.at.own_column
         d = 2 * at.zs[k] + x
         self.arrived(s, g, d)
-        self.copy(s, g, d, 3 + k, at.first).start()
-        self.copy(s, g, d, 7 + k, at.second).start()
+        if not self.Z_LATER[s]:
+            self.copy(s, g, d, 3 + k, self.routes[s].first).start()
+        self.copy(s, g, d, 7 + k, self.routes[s].second).start()
         self.copy(s, g, d, 15 + k, at.sibling).start()
 
     def from_first(self, s, k):
-        at, (g, x) = self.at, self.at.first_column
+        at, (g, x) = self.at, self.routes[s].first_column
         d = 2 * at.zs[k] + x
         self.arrived(s, g, d)
-        self.copy(s, g, d, 11 + k, at.second).start()
+        if self.Z_LATER[s] and k == 0:
+            for j in range(1, 4):
+                self.copy(s, g, d, 3 + j, at.line[j]).start()
+        self.copy(s, g, d, 11 + k, self.routes[s].second).start()
         self.copy(s, g, d, 19 + k, at.sibling).start()
 
     def from_second(self, s, k):
-        at, (g, x) = self.at, self.at.second_columns[k // 4]
+        at, (g, x) = self.at, self.routes[s].second_columns[k // 4]
         d = 2 * at.zs[k % 4] + x
         self.arrived(s, g, d)
         self.copy(s, g, d, 23 + k, at.sibling).start()
 
-    def from_sibling(self, s):
+    def group(self, i):
         at = self.at
-        for g in (at.sibling[1], at.diagonal[1]):
-
-            @pl.loop(0, self.shards)
-            def _(d):
-                self.arrived(s, g, d)
+        return 2 * (at.y + (i // 2) * (1 - 2 * at.y)) + at.core + (i % 2) * (1 - 2 * at.core)
+
+    def from_sibling(self, s, g):
+        @pl.loop(0, self.shards)
+        def _(d):
+            self.arrived(s, g, d)
 
     def keep(self, s):
         return pltpu.make_async_copy(self.w.at[s], self.kept.at[s], self.local.at[3 + s])
@@ -352,70 +399,50 @@
         return [self.bias_copy(k, peer) for k, peer in enumerate((at.sibling, across, at.diagonal))]
 
     def begin(self):
-        greet(self.at.peers)
-        self.along_z(0)
-        self.own_out(0)
+        signal(self.at.peers)
+        self.fill()
+        arrive(self.at.peers)
+        self.steps("begin")
         for copy in self.bias_copies():
             copy.start()
         self.biases[self.at.mp] = self.own_bias[...]
 
+    def near_heads(self):
+        self.steps("near")
+        for copy in self.bias_copies():
+            copy.wait_recv()
+        self.own_copy(0).wait()
+        self.from_sibling(0, self.group(1))
+
+    def far_heads(self):
+        self.steps("far")
+        self.from_sibling(0, self.group(3))
+        self.keep(0).start()
+
     def ready(self, section):
-        if section == 0:
-            self.from_z(0, 1)
-            self.from_z(0, 2)
-            self.from_z(0, 3)
-            self.along_z(1)
-            for k in range(4):
-                self.from_first(0, k)
-            self.own_out(1)
-            for k in range(8):
-                self.from_second(0, k)
-            for copy in self.bias_copies():
-                copy.wait_recv()
-            self.steps(0)
-            self.from_sibling(0)
-        elif section == 1:
+        if section == 1:
+            self.steps(8)
+        else:
             self.steps(9)
-            self.from_sibling(1)
-        else:
-            self.steps(10)
-            self.from_sibling(2)
+        self.from_sibling(section, self.group(1))
+        self.from_sibling(section, self.group(3))
         self.own_copy(section).wait()
         self.keep(section).start()
 
     def steps(self, step):
-        if step == 0:
-            for k in range(1, 4):
-                self.from_z(1, k)
-            self.along_z(2)
-        elif step == 2:
-            self.from_first(1, 0)
-            self.from_first(1, 1)
-        elif step == 3:
-            self.from_first(1, 2)
-            self.from_first(1, 3)
-        elif step == 4:
-            self.own_out(2)
-            for k in range(1, 4):
-                self.from_z(2, k)
-        elif step == 5:
-            for k in range(4):
-                self.from_second(1, k)
-        elif step == 6:
-            for k in range(4, 8):
-                self.from_second(1, k)
-        elif step == 7:
-            self.from_first(2, 0)
-            self.from_first(2, 1)
-        elif step == 9:
-            self.from_first(2, 2)
-            self.from_first(2, 3)
-        elif step == 10:
-            for k in range(8):
-                self.from_second(2, k)
+        actions = {
+            "along": lambda s, k: self.along_z(s),
+            "out": lambda s, k: self.own_out(s),
+            "z": self.from_z,
+            "first": self.from_first,
+            "second": self.from_second,
+        }
+        for name, s, *ks in GATHER_STEPS.get(step, ()):
+            for k in ks or (0,):
+                actions[name](s, k)
 
     def tick(self, step):
-        for k in range(2, 8):
+        for k in range(8):
             pl.when(step == k)(functools.partial(self.steps, k))
 
     def end(self):
@@ -470,21 +497,24 @@
     source.begin()
     fill_mask(sizes, me, lens, bias)
     load.wait()
-    source.ready(0)
-    project(sizes, me, x, w.at[0], biases, kv, q)
     save_kv = pltpu.make_async_copy(kv, kv_out, sems.at[1])
-    save_kv.start()
-    attend(sizes, me, kv, q, bias, lse, ctx, source.tick)
+    half = sizes.groups // 2
+    for span, ready in (((0, half), source.near_heads), ((half, sizes.groups), source.far_heads)):
+        ready()
+        project(sizes, me, source.group, span, x, w.at[0], biases, kv, q)
+        if span[1] == sizes.groups:
+            save_kv.start()
+        attend(sizes, me, source.group, span, source.tick, kv, q, bias, lse, ctx)
 
     own = pl.ds(sizes.own_offset(me), sizes.own)
-    hidden[...] = x[own, :].astype(F32) + b_out[...]
+    hidden[...] = x[own, :].astype(F32) + as_row(b_out)
     for g in range(sizes.groups):
         hidden[...] += dot(ctx[g], w[0, g, :, tile(4, 2)], 1, 1)
     normed, factor = norm_stats(hidden[...])
     n_1[...] = normed
     r_1[...] = factor
-    y_1 = normed * gain_1[...] + shift_1[...]
-    hidden[...] = y_1 + b_down[...]
+    y_1 = normed * as_row(gain_1) + as_row(shift_1)
+    hidden[...] = y_1 + as_row(b_down)
     encoded[...] = y_1.astype(BF16)
     source.ready(1)
 
@@ -508,7 +538,7 @@
     normed, factor = norm_stats(hidden[...])
     n_2[...] = normed
     r_2[...] = factor
-    y_2 = (normed * gain_2[...] + shift_2[...]).astype(BF16)
+    y_2 = (normed * as_row(gain_2) + as_row(shift_2)).astype(BF16)
     encoded[...] = y_2
     cls[...] = dot(start_rows(sizes, me, lens).astype(BF16), y_2)
     source.end()
@@ -523,10 +553,30 @@
     forward_math(sizes, source, lens, tokens, biases, *refs, w, bias, hidden, kv, z, slope, sems)
 
 
-def gathering_kernel(sizes, lens, tokens, packed, own_bias, *rest):
-    rows, (kept, *outs) = rest[:6], rest[6:]
-    *refs, w, bias, hidden, kv, z, slope, sems, biases, send, recv, local, bias_sems = outs
-    source = Gather(Place(), packed, own_bias, w, biases, kept, send, recv, local, bias_sems)
+def pack(w_key, w_value, w_query, w_out, w_down, b_value, b_query, b_up, packed, own_bias):
+    cols = w_key.shape[1]
+    for k, weight in enumerate((w_key, w_value, w_query)):
+        packed[0, :, k * cols : (k + 1) * cols] = weight[...]
+    packed[0, :, 3 * cols :] = w_out[...].astype(F32).T.astype(BF16)
+    packed[1] = w_down[...]
+    own_bias[...] = jnp.zeros_like(own_bias)
+    own_bias[:, cols : 2 * cols] = as_row(b_value)
+    own_bias[:, 2 * cols : 3 * cols] = as_row(b_query)
+    own_bias[:, 5 * LANES :] = as_row(b_up)
+
+
+def gathering_kernel(sizes, lens, tokens, *rest):
+    shards, rows, (kept, *outs) = rest[:9], rest[9:15], rest[15:]
+    *refs, w, bias, hidden, kv, z, slope, sems, packed, own_bias, biases, send, recv, local, bias_sems = outs
+    w_key, w_value, w_query, w_out, w_up, w_down, b_value, b_query, b_up = shards
+
+    def fill():
+        pack(w_key, w_value, w_query, w_out, w_down, b_value, b_query, b_up, packed, own_bias)
+
+    source = Gather(
+        Place(), (packed.at[0], w_up, packed.at[1]), own_bias, w, biases, kept, send, recv, local, bias_sems
+    )
+    source.fill = fill
     forward_math(
         sizes, source, lens, tokens, biases, *rows, *refs, w, bias, hidden, kv, z, slope, sems
     )
@@ -589,12 +639,12 @@
     dy = cot[...].astype(F32) + dot(picked, high, 0, 0) + dot(picked, low_part, 0, 0)
     small[0:1, :] = jnp.sum(dy * n_2[...], axis=0, keepdims=True)
     small[1:2, :] = jnp.sum(dy, axis=0, keepdims=True)
-    grad = norm_back(dy, n_2[...], r_2[...], gain_2[...])
+    grad = norm_back(dy, n_2[...], r_2[...], as_row(gain_2))
     small[2:3, :] = jnp.sum(grad, axis=0, keepdims=True)
     dh[...] = grad
     low[...] = grad.astype(BF16)
     turned[0] = grad.T.astype(BF16)
-    y_1 = n_1[...] * gain_1[...] + shift_1[...]
+    y_1 = n_1[...] * as_row(gain_1) + as_row(shift_1)
     other[...] = y_1.astype(BF16)
     turned[1] = y_1.T.astype(BF16)
     for load in loads:
@@ -624,7 +674,7 @@
     dy = dh[...]
     small[3:4, :] = jnp.sum(dy * n_1[...], axis=0, keepdims=True)
     small[4:5, :] = jnp.sum(dy, axis=0, keepdims=True)
-    grad = norm_back(dy, n_1[...], r_1[...], gain_1[...])
+    grad = norm_back(dy, n_1[...], r_1[...], as_row(gain_1))
     small[5:6, :] = jnp.sum(grad, axis=0, keepdims=True)
     small[6:8, :] = jnp.zeros_like(small[6:8, :])
     small[12:16, :] = jnp.zeros_like(small[12:16, :])
@@ -693,15 +743,41 @@
         self.own().wait()
 
 
+DURING = {
+    0: (("encoded", 0),),
+    1: (("second", 2),),
+    5: (("first", 2),),
+}
+BEFORE_LAST = (("second", 1),)
+AFTER_LAST = (
+    ("begin", 0),
+    ("chip", 0),
+    ("line", 2),
+    ("first", 1),
+    ("tokens", 0),
+    ("second", 0),
+    ("small", 0),
+    ("line", 1),
+    ("small", 1),
+    ("first", 0),
+    ("small", 2),
+    ("relay", 0),
+    ("line", 0),
+)
+
+
 class Scatter:
     STAGE = (0, 2, 0)
     HELD = (8, 6, 4)
+    ROUTES = ("by_core", "by_core", "by_core")
+    Z_EARLY = ((1,), (1,), (1,))
 
     def __init__(self, place, parts, inbox, by_second, by_first, by_line, shards, sems):
         self.at, self.parts, self.inbox, self.shards = place, parts, inbox, shards
         self.by_second, self.by_first, self.by_line = by_second, by_first, by_line
         self.core_sems, self.second_sems, self.first_sems, self.line_sems = sems
         self.rows = shards.shape[1]
+        self.routes = [getattr(place, name) for name in self.ROUTES]
 
     def shard(self, s, g, d):
         first = (self.HELD[s] + g // 2) * self.parts.shape[1] + d * self.rows
@@ -721,23 +797,23 @@
         )
 
     def to_second(self, s, k):
-        g, x = self.at.second_columns[1 - k // 4]
+        g, x = self.routes[s].second_columns[1 - k // 4]
         return remote(
             self.shard(s, g, 2 * (k % 4) + x),
             self.by_second.at[s, k],
             self.second_sems.at[0, s, k],
             self.second_sems.at[1, s, k],
-            self.at.second,
+            self.routes[s].second,
         )
 
     def to_first(self, s, k):
-        g, x = self.at.first_column
+        g, x = self.routes[s].first_column
         return remote(
             self.shard(s, g, 2 * k + x),
             self.by_first.at[s, k],
             self.first_sems.at[0, s, k],
             self.first_sems.at[1, s, k],
-            self.at.first,
+            self.routes[s].first,
         )
 
     def to_line(self, s, j):
@@ -763,15 +839,88 @@
         for k in range(8):
             self.to_second(s, k).start()
 
+    def other_line(self, s, j):
+        g, x = self.routes[s].first_column
+        return remote(
+            self.shard(s, g, 2 * self.at.zs[j] + x),
+            self.by_first.at[s, j],
+            self.first_sems.at[0, s, j],
+            self.first_sems.at[1, s, j],
+            self.at.line[j],
+        )
+
+    def last_cross(self, s):
+        g, x = self.routes[s].first_column
+        return remote(
+            self.shard(s, g, 2 * self.at.z + x),
+            self.by_first.at[s, 0],
+            self.first_sems.at[0, s, 0],
+            self.first_sems.at[1, s, 0],
+            self.routes[s].first,
+        )
+
+    def by_kind(self, s, early, late):
+        cores = self.Z_EARLY[s]
+        if len(cores) == 1:
+            pl.when(self.at.core == cores[0])(functools.partial(early, s))
+            pl.when(self.at.core != cores[0])(functools.partial(late, s))
+        else:
+            (early if cores else late)(s)
+
     def from_second(self, s):
-        g, x = self.at.first_column
+        self.by_kind(s, self.from_second_early, self.from_second_late)
+
+    def from_first(self, s):
+        self.by_kind(s, self.from_first_early, self.from_first_late)
+
+    def from_line(self, s):
+        self.by_kind(s, self.from_line_early, self.from_line_late)
+
+    def from_second_early(self, s):
+        at, (g, x) = self.at, self.routes[s].first_column
+        for k in range(8):
+            self.to_second(s, k).wait_recv()
+        for j in (3, 2, 1, 0):
+            z = at.zs[j]
+            mine = self.shard(s, g, 2 * z + x)
+            mine[...] = (mine[...].astype(F32) + self.by_second[s, z].astype(F32)).astype(BF16)
+            if j:
+                self.other_line(s, j).start()
+        for j in (3, 2, 1):
+            z = at.zs[j]
+            mine = self.shard(s, at.mp, 2 * z + at.x)
+            mine[...] = (mine[...].astype(F32) + self.by_second[s, 4 + z].astype(F32)).astype(BF16)
+            self.to_line(s, j).start()
+
+    def from_first_early(self, s):
+        g, x = self.routes[s].first_column
+        mine = self.shard(s, g, 2 * self.at.z + x)
+        total = mine[...].astype(F32)
+        for j in (1, 2, 3):
+            self.other_line(s, j).wait_recv()
+            total = total + self.by_first[s, j].astype(F32)
+        mine[...] = total.astype(BF16)
+        self.last_cross(s).start()
+
+    def from_line_early(self, s):
+        at = self.at
+        mine = self.shard(s, at.mp, 2 * at.z + at.x)
+        total = mine[...].astype(F32) + self.by_second[s, 4 + at.z].astype(F32)
+        for j in range(1, 4):
+            self.to_line(s, j).wait_recv()
+            total = total + self.by_line[s, j - 1].astype(F32)
+        self.last_cross(s).wait_recv()
+        self.shards[s] = total + self.by_first[s, 0].astype(F32)
+
+    def from_second_late(self, s):
+        g, x = self.routes[s].first_column
         for k in range(4):
             self.to_second(s, k).wait_recv()
             mine = self.shard(s, g, 2 * k + x)
             mine[...] = (mine[...].astype(F32) + self.by_second[s, k].astype(F32)).astype(BF16)
             self.to_first(s, k).start()
 
-    def from_first(self, s):
+    def from_first_late(self, s):
         at = self.at
         for k in range(4):
             self.to_second(s, 4 + k).wait_recv()
@@ -790,7 +939,7 @@
             else:
                 self.shards[s] = total
 
-    def from_line(self, s):
+    def from_line_late(self, s):
         for j in range(1, 4):
             self.to_line(s, j).wait_recv()
             self.shards[s] += self.by_line[s, j - 1].astype(F32)
@@ -813,7 +962,7 @@
     def __init__(self, place, sums, inbox, sems):
         self.at, self.sums, self.inbox, self.sems = place, sums, inbox, sems
         at = place
-        self.peers = [at.sibling, (2 * at.z + 1 - at.x, at.mp), (at.dp, at.across), *at.line[1:]]
+        self.peers = [at.sibling, at.x_peer, at.y_peer, *at.line[1:]]
 
     def copy(self, k):
         return remote(
@@ -899,11 +1048,11 @@
             self.mate(k).start()
 
     def start_gold(self):
-        columns = self.at.dp * self.passages.shape[0] + lax.broadcasted_iota(
-            jnp.int32, (self.gold.shape[0], self.passages.shape[0]), 1
-        )
-        target = jnp.where(self.gold[...] == columns, 1.0, 0.0).astype(BF16)
-        self.put(0, dot(target, self.passages[...]))
+        places = self.at.dp * self.passages.shape[0] + lax.broadcasted_iota(
+            jnp.int32, (self.passages.shape[0], self.gold.shape[0]), 0
+        )
+        target = jnp.where(as_row(self.gold) == places, 1.0, 0.0).astype(BF16)
+        self.put(0, dot(target, self.passages[...], 0, 0))
         for k in range(1, self.ways):
             self.back_copy(0, k).start()
 
@@ -1124,21 +1273,6 @@
         copy.start()
     kv_load(0).start()
 
-    def group_of(i):
-        return jnp.where(i < 2, 1 - at.core + 2 * i, at.core + 2 * (i - 2))
-
-    def ffn_loads(i):
-        slot, g = i % 2, group_of(i)
-        return [
-            pltpu.make_async_copy(weights.at[2, g], w.at[2 * slot], ffn_sems.at[slot, 0]),
-            pltpu.make_async_copy(weights.at[1, g], w.at[2 * slot + 1], ffn_sems.at[slot, 1]),
-            pltpu.make_async_copy(z_in.at[g], ffn.at[slot, 0], ffn_sems.at[slot, 2]),
-            pltpu.make_async_copy(slope_in.at[g], ffn.at[slot, 1], ffn_sems.at[slot, 3]),
-        ]
-
-    for copy in ffn_loads(0):
-        copy.start()
-
     scoring = Scoring(
         at,
         ways,
@@ -1150,7 +1284,27 @@
         (part, parts_in, firsts, first_rows, back_sent, back_got, stats, stats_got),
         (mp_sems, score_sems),
     )
-    greet([*scoring.mates, *scoring.others])
+    signal([*scoring.mates, *scoring.others])
+
+    def group_of(i):
+        return jnp.where(i < 2, 1 - at.core + 2 * i, at.core + 2 * (i - 2))
+
+    def z_load(i):
+        return pltpu.make_async_copy(z_in.at[group_of(i)], ffn.at[0, i % 2], ffn_sems.at[i % 2, 0])
+
+    def ffn_loads(i):
+        slot, g = i % 2, group_of(i)
+        return [
+            pltpu.make_async_copy(weights.at[2, g], w.at[2 * slot], ffn_sems.at[slot, 1]),
+            pltpu.make_async_copy(weights.at[1, g], w.at[2 * slot + 1], ffn_sems.at[slot, 2]),
+            pltpu.make_async_copy(slope_in.at[g], ffn.at[1, slot], ffn_sems.at[slot, 3]),
+        ]
+
+    z_load(0).start()
+    for copy in ffn_loads(0):
+        copy.start()
+
+    arrive([*scoring.mates, *scoring.others])
     scoring.start_cls()
     loads[0].wait()
     scoring.start_gold()
@@ -1159,7 +1313,7 @@
     fill_mask(sizes, me, lens, bias)
     picked = start_rows(sizes, me, lens).astype(BF16)
     loads[3].wait()
-    turned[1] = (n_1[...] * gain_1[...] + shift_1[...]).T.astype(BF16)
+    turned[1] = (n_1[...] * as_row(gain_1) + as_row(shift_1)).T.astype(BF16)
     scoring.start_back()
     loads[1].wait()
     loads[2].wait()
@@ -1170,50 +1324,57 @@
     mine = sums.at[0]
     mine[0:1, :] = jnp.sum(dy * work[1], axis=0, keepdims=True)
     mine[1:2, :] = jnp.sum(dy, axis=0, keepdims=True)
-    grad = norm_back(dy, work[1], r_2[...], gain_2[...])
+    grad = norm_back(dy, work[1], r_2[...], as_row(gain_2))
     mine[2:3, :] = jnp.sum(grad, axis=0, keepdims=True)
     work[0] = grad
     rows_low[...] = grad.astype(BF16)
     turned[0] = grad.T.astype(BF16)
 
-    for half in range(2):
-
-        @pl.loop(2 * half, 2 * half + 2)
-        def _(i):
-            slot, g = i % 2, group_of(i)
-            for copy in ffn_loads(i):
-                copy.wait()
-
-            @pl.when(i < 3)
-            def _():
-                for copy in ffn_loads(i + 1):
-                    copy.start()
-
-            k = i - 2 * half
-            into = [(Scatter.HELD if half else Scatter.STAGE)[s] + k for s in range(3)]
-            square(parts, into[2])[...] = dot(turned[0], ffn[slot, 0]).astype(BF16)
-            if not half:
-                scatter.to_sibling(2, k).start()
-            da = dot(rows_low[...], w[2 * slot]) * ffn[slot, 1].astype(F32)
-            mine[pl.ds(8 + g, 1), :] = jnp.sum(da, axis=0, keepdims=True)
-            da_low = da.astype(BF16)
-            square(parts, into[1])[...] = dot(turned[1], da_low).astype(BF16)
-            if not half:
-                scatter.to_sibling(1, k).start()
-            work[0] += dot(da_low, w[2 * slot + 1], 1, 1)
+    def into(s, i):
+        return jnp.where(i < 2, Scatter.STAGE[s] + i, Scatter.HELD[s] + i - 2)
+
+    @pl.loop(0, sizes.groups)
+    def _(i):
+        z_load(i).wait()
+
+        @pl.when(i < 3)
+        def _():
+            z_load(i + 1).start()
+
+        square(parts, into(2, i))[...] = dot(turned[0], ffn[0, i % 2]).astype(BF16)
+        pl.when(i < 2)(lambda: scatter.to_sibling(2, i).start())
+
+    scatter.chip_sum(2)
+
+    @pl.loop(0, sizes.groups)
+    def _(i):
+        slot, g = i % 2, group_of(i)
+        for copy in ffn_loads(i):
+            copy.wait()
+
+        @pl.when(i < 3)
+        def _():
+            for copy in ffn_loads(i + 1):
+                copy.start()
+
+        da = dot(rows_low[...], w[2 * slot]) * ffn[1, slot].astype(F32)
+        mine[pl.ds(8 + g, 1), :] = jnp.sum(da, axis=0, keepdims=True)
+        da_low = da.astype(BF16)
+        square(parts, into(1, i))[...] = dot(turned[1], da_low).astype(BF16)
+        pl.when(i < 2)(lambda: scatter.to_sibling(1, i).start())
+        work[0] += dot(da_low, w[2 * slot + 1], 1, 1)
 
     load_w = pltpu.make_async_copy(weights.at[0], w, load_sems.at[7])
     load_w.start()
     load_x = load(1, tokens.at[own_rows], row_in)
     load_x.start()
-    scatter.chip_sum(2)
     scatter.chip_sum(1)
     scatter.sent_to_sibling(2)
 
     dy = work[0]
     mine[3:4, :] = jnp.sum(dy * n_1[...], axis=0, keepdims=True)
     mine[4:5, :] = jnp.sum(dy, axis=0, keepdims=True)
-    grad = norm_back(dy, n_1[...], r_1[...], gain_1[...])
+    grad = norm_back(dy, n_1[...], r_1[...], as_row(gain_1))
     mine[5:6, :] = jnp.sum(grad, axis=0, keepdims=True)
     mine[6:8, :] = jnp.zeros((2, sizes.width), F32)
     mine[12:24, :] = jnp.zeros((12, sizes.width), F32)
@@ -1222,7 +1383,6 @@
     turned[0] = grad.T.astype(BF16)
     load_x.wait()
     turned[1] = row_in[...].astype(F32).T.astype(BF16)
-    spread.forward()
     load_w.wait()
     for copy in loads[4:]:
         copy.wait()
@@ -1231,19 +1391,25 @@
     def _(g):
         dctx[g] = dot(rows_low[...], w[g, :, tile(4, 2)]).astype(BF16)
 
-    def step(k):
-        if k == 2:
-            scatter.from_second(2)
-        elif k == 4:
-            scatter.from_first(2)
-        elif k == 5:
-            scatter.from_second(1)
-        elif k == 6:
-            scatter.from_line(2)
+    actions = {
+        "second": scatter.from_second,
+        "first": scatter.from_first,
+        "line": scatter.from_line,
+        "chip": scatter.chip_sum,
+        "small": small.step,
+        "begin": lambda s: small.begin(),
+        "tokens": lambda s: token_spread.begin(),
+        "relay": lambda s: token_spread.forward(),
+        "encoded": lambda s: spread.forward(),
+    }
+
+    def run(names):
+        for name, s in names:
+            actions[name](s)
 
     def tick(now):
-        for k in (2, 4, 5, 6):
-            pl.when(now == k)(functools.partial(step, k))
+        for k, names in DURING.items():
+            pl.when(now == k)(functools.partial(run, names))
 
     def finalize(g):
         slot = g % 2
@@ -1293,20 +1459,10 @@
         def _():
             finalize(g - 1)
 
-    scatter.from_first(1)
+    run(BEFORE_LAST)
     finalize(sizes.groups - 1)
-    small.begin()
     rows_low[...] = work[1].astype(BF16)
-    scatter.chip_sum(0)
-    token_spread.begin()
-    small.step(0)
-    scatter.from_line(1)
-    scatter.from_second(0)
-    small.step(1)
-    scatter.from_first(0)
-    small.step(2)
-    token_spread.forward()
-    scatter.from_line(0)
+    run(AFTER_LAST)
     small.end(small_out)
     scatter.sent_to_sibling(1)
     scatter.sent_to_sibling(0)
@@ -1341,7 +1497,7 @@
     return pltpu.CompilerParams(vmem_limit_bytes=63 * 2**20, **more)
 
 
-def run_forward(sizes, lengths, tokens, weights, biases, rows, gathers):
+def run_forward(sizes, lengths, tokens, weights, rows, gathers):
     own, width, groups = sizes.own, sizes.width, sizes.groups
     docs = lengths.shape[1]
     shape = jax.ShapeDtypeStruct
@@ -1374,7 +1530,9 @@
         outs.insert(0, shape((3, groups, width, width), BF16))
         spaces.insert(0, ANY)
         scratch += [
-            pltpu.VMEM((groups, 1, biases.shape[1]), F32),
+            pltpu.VMEM((2, weights[0].shape[0], width), BF16),
+            pltpu.VMEM((1, 5 * LANES + weights[8].shape[0]), F32),
+            pltpu.VMEM((groups, 1, 5 * LANES + weights[8].shape[0]), F32),
             pltpu.SemaphoreType.DMA((3, 31)),
             pltpu.SemaphoreType.DMA((3, 32)),
             pltpu.SemaphoreType.DMA((6,)),
@@ -1387,12 +1545,12 @@
     return pl.pallas_call(
         functools.partial(kernel, sizes),
         out_shape=outs,
-        in_specs=specs(SMEM, ANY, VMEM if gathers else ANY, *[VMEM] * 7),
+        in_specs=specs(SMEM, ANY, *([VMEM] * 15 if gathers else [ANY, *[VMEM] * 7])),
         out_specs=specs(*spaces),
         scratch_shapes=scratch,
         compiler_params=params(**more),
         name="forward",
-    )(lengths, tokens, weights, biases, *rows)
+    )(lengths, tokens, *weights, *rows)
 
 
 def run_backward(sizes, lengths, cotangent, dcls, weights, gain_1, shift_1, gain_2, saved):
@@ -1551,11 +1709,18 @@
     return table, lse, summed_on_arrival(grad.astype(BF16), "dp", 0)
 
 
-def plain_layer(sizes, tokens, cotangent, lengths, gold, passages, packed, own_bias, rows):
+def plain_layer(sizes, tokens, cotangent, lengths, gold, passages, shards, rows):
     me, groups = lax.axis_index("mp"), sizes.groups
+    w_key, w_value, w_query, w_out, w_up, w_down, b_value, b_query, b_up = shards
+    packed = jnp.stack(
+        [jnp.concatenate([w_key, w_value, w_query, w_out.T], axis=1), w_up, w_down]
+    )
+    c = w_key.shape[1]
+    zeros = jnp.zeros((c,), F32)
+    own_bias = jnp.concatenate([zeros, b_value, b_query, zeros[:HEAD], b_up])[None]
     whole = lax.all_gather(lax.all_gather(packed, "dp", axis=1, tiled=True), "mp", axis=1)
     biases = lax.all_gather(own_bias, "mp", axis=0)
-    encoded, cls, *saved = run_forward(sizes, lengths, tokens, whole, biases, rows, False)
+    encoded, cls, *saved = run_forward(sizes, lengths, tokens, (whole, biases), rows, False)
     cls = lax.psum(cls, "mp").astype(BF16)
     table, lse, dcls = score(cls, passages, gold)
     n_1, r_1, n_2, r_2, z, slope, kv, q, logs, ctx = saved
@@ -1581,7 +1746,119 @@
     grads = summed_on_arrival(grads, "mp", 1)[:, 0].astype(BF16)
     grads = summed_on_arrival(grads, "dp", 1)
     small, small_attn = lax.psum((small, small_attn), ("dp", "mp"))
-    return table, lse, encoded, token_grad, grads, small, small_attn[:, 0]
+    mine = lax.dynamic_index_in_dim(small_attn[:, 0], me, 0, keepdims=False)
+    up_bias = lax.dynamic_index_in_dim(small, 8 + me, 0, keepdims=False)
+    return (
+        table,
+        lse,
+        encoded,
+        token_grad,
+        grads[0, :, 2 * c : 3 * c],
+        grads[0, :, :c],
+        grads[0, :, c : 2 * c],
+        mine[2 * c : 3 * c],
+        mine[c : 2 * c],
+        grads[0, :, 3 * c :].T,
+        small[5],
+        small[3],
+        small[4],
+        grads[1],
+        up_bias,
+        grads[2].T,
+        small[2],
+        small[0],
+        small[1],
+    )
+
+
+def outputs_kernel(cols, table, lse, small, shards, encoded, tokens, *outs):
+    *outs, got, wide, sems = outs
+    (
+        table_out,
+        lse_out,
+        encoded_out,
+        tokens_out,
+        g_query,
+        g_key,
+        g_value,
+        gb_query,
+        gb_value,
+        g_out,
+        gb_out,
+        g_gain_1,
+        g_shift_1,
+        g_up,
+        gb_up,
+        g_down,
+        gb_down,
+        g_gain_2,
+        g_shift_2,
+    ) = outs
+    steps = got.shape[0]
+    rows = [pl.ds(k * got.shape[1], got.shape[1]) for k in range(steps)]
+    copies = [pltpu.make_async_copy(tokens.at[rows[k]], got.at[k], sems.at[0, k]) for k in range(steps)]
+    writes = [pltpu.make_async_copy(wide.at[k], tokens_out.at[rows[k]], sems.at[1, k]) for k in range(steps)]
+    spare = pltpu.make_async_copy(encoded, encoded_out, sems.at[2, 0])
+    for copy in copies:
+        copy.start()
+    spare.start()
+    for k in range(steps):
+        copies[k].wait()
+        wide[k] = got[k].astype(F32)
+        writes[k].start()
+    me = lax.axis_index("mp")
+    table_out[...] = table[...]
+    lse_out[...] = lse[...].T.reshape(lse_out.shape)
+    for k, target in enumerate((g_key, g_value, g_query)):
+        target[...] = shards[0, :, k * cols : (k + 1) * cols]
+    g_out[...] = shards[0, :, 3 * cols :].T
+    g_up[...] = shards[1]
+    g_down[...] = shards[2]
+    heads = small[pl.ds(16 + me, 1), :]
+    gb_value[...] = heads[:, cols : 2 * cols].reshape(gb_value.shape)
+    gb_query[...] = heads[:, 2 * cols : 3 * cols].reshape(gb_query.shape)
+    gb_up[...] = small[pl.ds(8 + me, 1), :].reshape(gb_up.shape)
+    for k, target in enumerate((g_gain_2, g_shift_2, gb_down, g_gain_1, g_shift_1, gb_out)):
+        target[...] = small[k : k + 1, :].reshape(target.shape)
+    for write in writes:
+        write.wait()
+    spare.wait()
+
+
+def run_outputs(made, cols):
+    table, lse, small, shards, encoded, tokens = made
+    rows, width = shards.shape[1:]
+    shape = jax.ShapeDtypeStruct
+    vector = shape((width,), F32)
+    outs = (
+        shape(table.shape, F32),
+        shape((lse.shape[0],), F32),
+        shape(encoded.shape, BF16),
+        shape(tokens.shape, F32),
+        *[shape((rows, cols), F32)] * 3,
+        *[shape((cols,), F32)] * 2,
+        shape((cols, rows), F32),
+        *[vector] * 3,
+        shape((rows, width), F32),
+        vector,
+        shape((rows, width), F32),
+        *[vector] * 3,
+    )
+    steps = 8
+    span = tokens.shape[0] // steps
+    return pl.pallas_call(
+        functools.partial(outputs_kernel, cols),
+        out_shape=outs,
+        in_specs=specs(*[VMEM] * 4, ANY, ANY),
+        out_specs=specs(*[ANY if k in (2, 3) else VMEM for k in range(len(outs))]),
+        scratch_shapes=[
+            pltpu.VMEM((steps, span, width), BF16),
+            pltpu.VMEM((steps, span, width), F32),
+            pltpu.SemaphoreType.DMA((3, steps)),
+        ],
+        compiler_params=params(),
+        name="outputs",
+    )(*made)
 
 
 def body(
@@ -1608,52 +1885,21 @@
 ):
     groups = lax.axis_size("mp")
     sizes = Sizes(tokens.shape[0], tokens.shape[1], groups)
-    me = lax.axis_index("mp")
-    head_cols = w_query.shape[1]
-    packed = jnp.stack(
-        [jnp.concatenate([w_key, w_value, w_query, w_out.T], axis=1), w_up, w_down.T]
-    )
-    zeros = jnp.zeros((head_cols,), F32)
-    own_bias = jnp.concatenate([zeros, b_value, b_query, zeros[:HEAD], b_up])[None]
-    rows = [r[None] for r in (b_out, gain_attn, shift_attn, b_down, gain_ffn, shift_ffn)]
-    c = head_cols
+    rows = (b_out, gain_attn, shift_attn, b_down, gain_ffn, shift_ffn)
+    shards = (w_key, w_value, w_query, w_out, w_up, w_down.T, b_value, b_query, b_up)
     if lax.axis_size("dp") == 8 and groups == 4:
         whole, encoded, cls, n_1, r_1, n_2, r_2, z, slope, kv, q, logs, ctx = run_forward(
-            sizes, lengths, tokens, packed, own_bias, rows, True
-        )
-        table, lse, small, grads, encoded, token_part = run_finish(
+            sizes, lengths, tokens, shards, rows, True
+        )
+        made = run_finish(
             sizes,
-            (lengths, cls, gold[:, None], rows[1], rows[2], rows[4], r_1, r_2, logs),
+            (lengths, cls, gold, gain_attn, shift_attn, gain_ffn, r_1, r_2, logs),
             (tokens, cotangent, passages, encoded, whole, n_1, n_2, z, slope, kv, q, ctx),
         )
-        lse, token_grad, small_attn = lse[:, 0], token_part.astype(F32), small[16:20]
-    else:
-        table, lse, encoded, token_grad, grads, small, small_attn = plain_layer(
-            sizes, tokens, cotangent, lengths, gold, passages, packed, own_bias, rows
-        )
-    mine = lax.dynamic_index_in_dim(small_attn, me, 0, keepdims=False)
-    up_bias = lax.dynamic_index_in_dim(small, 8 + me, 0, keepdims=False)
-    return (
-        table,
-        lse,
-        encoded,
-        token_grad,
-        grads[0, :, 2 * c : 3 * c],
-        grads[0, :, :c],
-        grads[0, :, c : 2 * c],
-        mine[2 * c : 3 * c],
-        mine[c : 2 * c],
-        grads[0, :, 3 * c :].T,
-        small[5],
-        small[3],
-        small[4],
-        grads[1],
-        up_bias,
-        grads[2].T,
-        small[2],
-        small[0],
-        small[1],
-    )
+        outs = list(run_outputs(made, w_key.shape[1]))
+        outs[15] = outs[15].T
+        return tuple(outs)
+    return plain_layer(sizes, tokens, cotangent, lengths, gold, passages, shards, rows)
 
 
 def solution(mesh):

time: 258 us -> 313 us (1.21)
  Pallas kernels: 228 us -> 312 us
  local copies, waits for them, and re-layouts: 18.3 us -> 0 us
  other arithmetic: 8.6 us -> 0 us
    pallas_call x0 -> x1, Pallas kernels: none -> 98.9 us  [run_outputs(): pl.pallas_call(functools.partial(outputs_kernel, cols), out_shape=outs, i...]
    pallas_call x1, Pallas kernels: 143 us -> 129 us  [run_finish(): pl.pallas_call(functools.partial(finish_kernel, sizes), out_shape=outs, i...]
    broadcast_in_dim x9 -> x0, local copies, waits for them, and re-layouts: 8.92 us -> none  [the longest x6 7.6 us: body(): r[None]]
    convert_element_type x1 -> x0, other arithmetic: 5.23 us -> none  [body(): token_part.astype(F32)]
    unnamed x14 -> x0, local copies, waits for them, and re-layouts: 4.01 us -> none
where the time goes in v4:
time: 313 us
  Pallas kernels  312 us (100%)
    pallas_call x1, Pallas kernels, run_finish(): pl.pallas_call(functools.partial(finish_kernel, sizes), out_shape=outs, i...  129 us
    pallas_call x1, Pallas kernels, run_outputs(): pl.pallas_call(functools.partial(outputs_kernel, cols), out_shape=outs, i...  98.9 us
    pallas_call x1, Pallas kernels, run_forward(): pl.pallas_call(functools.partial(kernel, sizes), out_shape=outs, in_specs...  84.3 us

profile of v4, /device:TPU:1, one launch (start us, length us, event | category | flops | bytes accessed | tf_op | source)
XLA Modules:
  0.0 313.0 jit_solution(13778571176070270063)
XLA Ops:
  0.7 84.3 %forward.1 = (bf16[3,4,768,768]{3,2,1,0:T(8,128)(2,1)}, bf16[512,768]{1,0:T(8,128)(2,1)}, f32[8,768]{1,0:T(8,128)}, f32[512,768]{1,0:T(8,128)}, f32[512,1]{1,0:T...) custom-call(s32[1,8]{1,0:T(1,128)} %lens.3, ...), custom_call_target="tpu_custom_call" | custom-call | tf_op jit(solution)/shard_map/forward/pallas_call | solution.py:1545
  84.9 128.9 %finish.1 = (f32[64,1024]{1,0:T(8,128)}, f32[8,1]{1,0:T(8,128)}, f32[24,768]{1,0:T(8,128)}, f32[3,96,768]{2,1,0:T(8,128)}, bf16[2048,768]{1,0:T(8,128)(2,1)}, /*index=5*/bf16[2048,768]{1,0:T(8,128)(2,1)}) custom-call(s32[1,8]{1,0:T(1,128)} %lens.3, f32[8,768]{1,0:T(8,128)} %get-tuple-element.57.cls, s32[64]{0:T(128)} %gold.1, f32[768]{0:T(1024)} %gain_1.1, ...), custom_call_target="tpu_custom_call" | custom-call | tf_op jit(solution)/shard_map/finish/pallas_call | solution.py:1675
  213.8 98.9 %outputs.1 = (f32[64,1024]{1,0:T(8,128)}, f32[8]{0:T(128)}, bf16[2048,768]{1,0:T(8,128)(2,1)}, f32[2048,768]{1,0:T(8,128)}, f32[96,192]{1,0:T(8,128)}, /*index=5...) custom-call(f32[64,1024]{1,0:T(8,128)} %get-tuple-element.70.table, ...), custom_call_target="tpu_custom_call" | custom-call | tf_op jit(solution)/shard_map/outputs/pallas_call | solution.py:1849

commit v5 on v4

--- a/solution.py
+++ b/solution.py
@@ -1772,7 +1772,7 @@
 
 
 def outputs_kernel(cols, table, lse, small, shards, encoded, tokens, *outs):
-    *outs, got, wide, sems = outs
+    *outs, got, wide, passed, sems = outs
     (
         table_out,
         lse_out,
@@ -1798,14 +1798,17 @@
     rows = [pl.ds(k * got.shape[1], got.shape[1]) for k in range(steps)]
     copies = [pltpu.make_async_copy(tokens.at[rows[k]], got.at[k], sems.at[0, k]) for k in range(steps)]
     writes = [pltpu.make_async_copy(wide.at[k], tokens_out.at[rows[k]], sems.at[1, k]) for k in range(steps)]
-    spare = pltpu.make_async_copy(encoded, encoded_out, sems.at[2, 0])
-    for copy in copies:
-        copy.start()
-    spare.start()
+    takes = [pltpu.make_async_copy(encoded.at[rows[k]], passed.at[k], sems.at[2, k]) for k in range(steps)]
+    gives = [pltpu.make_async_copy(passed.at[k], encoded_out.at[rows[k]], sems.at[3, k]) for k in range(steps)]
+    for k in range(steps):
+        copies[k].start()
+        takes[k].start()
     for k in range(steps):
         copies[k].wait()
         wide[k] = got[k].astype(F32)
         writes[k].start()
+        takes[k].wait()
+        gives[k].start()
     me = lax.axis_index("mp")
     table_out[...] = table[...]
     lse_out[...] = lse[...].T.reshape(lse_out.shape)
@@ -1820,9 +1823,9 @@
     gb_up[...] = small[pl.ds(8 + me, 1), :].reshape(gb_up.shape)
     for k, target in enumerate((g_gain_2, g_shift_2, gb_down, g_gain_1, g_shift_1, gb_out)):
         target[...] = small[k : k + 1, :].reshape(target.shape)
-    for write in writes:
-        write.wait()
-    spare.wait()
+    for k in range(steps):
+        writes[k].wait()
+        gives[k].wait()
 
 
 def run_outputs(made, cols):
@@ -1854,7 +1857,8 @@
         scratch_shapes=[
             pltpu.VMEM((steps, span, width), BF16),
             pltpu.VMEM((steps, span, width), F32),
-            pltpu.SemaphoreType.DMA((3, steps)),
+            pltpu.VMEM((steps, span, width), BF16),
+            pltpu.SemaphoreType.DMA((4, steps)),
         ],
         compiler_params=params(),
         name="outputs",

time: 313 us -> 222 us (0.71)
  Pallas kernels: 312 us -> 221 us
    pallas_call x1, Pallas kernels: 98.9 us -> 8.14 us  [run_outputs(): pl.pallas_call(functools.partial(outputs_kernel, cols), out_shape=outs, i...]
where the time goes in v5:
time: 222 us
  Pallas kernels  221 us (100%)
    pallas_call x1, Pallas kernels, run_finish(): pl.pallas_call(functools.partial(finish_kernel, sizes), out_shape=outs, i...  129 us
    pallas_call x1, Pallas kernels, run_forward(): pl.pallas_call(functools.partial(kernel, sizes), out_shape=outs, in_specs...  84.3 us
    pallas_call x1, Pallas kernels, run_outputs(): pl.pallas_call(functools.partial(outputs_kernel, cols), out_shape=outs, i...  8.14 us

profile of v5, /device:TPU:1, one launch (start us, length us, event | category | flops | bytes accessed | tf_op | source)
XLA Modules:
  0.0 222.2 jit_solution(9945446681757918053)
XLA Ops:
  0.7 84.3 %forward.1 = (bf16[3,4,768,768]{3,2,1,0:T(8,128)(2,1)}, bf16[512,768]{1,0:T(8,128)(2,1)}, f32[8,768]{1,0:T(8,128)}, f32[512,768]{1,0:T(8,128)}, f32[512,1]{1,0:T...) custom-call(s32[1,8]{1,0:T(1,128)} %lens.3, ...), custom_call_target="tpu_custom_call" | custom-call | tf_op jit(solution)/shard_map/forward/pallas_call | solution.py:1545
  84.9 128.9 %finish.1 = (f32[64,1024]{1,0:T(8,128)}, f32[8,1]{1,0:T(8,128)}, f32[24,768]{1,0:T(8,128)}, f32[3,96,768]{2,1,0:T(8,128)}, bf16[2048,768]{1,0:T(8,128)(2,1)}, /*index=5*/bf16[2048,768]{1,0:T(8,128)(2,1)}) custom-call(s32[1,8]{1,0:T(1,128)} %lens.3, f32[8,768]{1,0:T(8,128)} %get-tuple-element.57.cls, s32[64]{0:T(128)} %gold.1, f32[768]{0:T(1024)} %gain_1.1, ...), custom_call_target="tpu_custom_call" | custom-call | tf_op jit(solution)/shard_map/finish/pallas_call | solution.py:1675
  213.8 8.1 %outputs.1 = (f32[64,1024]{1,0:T(8,128)}, f32[8]{0:T(128)}, bf16[2048,768]{1,0:T(8,128)(2,1)}, f32[2048,768]{1,0:T(8,128)}, f32[96,192]{1,0:T(8,128)}, /*index=5...) custom-call(f32[64,1024]{1,0:T(8,128)} %get-tuple-element.70.table, ...), custom_call_target="tpu_custom_call" | custom-call | tf_op jit(solution)/shard_map/outputs/pallas_call | solution.py:1852

commit v6 on v5

--- a/solution.py
+++ b/solution.py
@@ -234,6 +234,12 @@
     def ready(self, section):
         self.copies[section].wait()
 
+    def group_ready(self, section, i):
+        pass
+
+    def done(self, section):
+        pass
+
     def tick(self, step):
         pass
 
@@ -420,13 +426,20 @@
         self.keep(0).start()
 
     def ready(self, section):
+        self.steps(7 + section)
+        self.own_copy(section).wait()
         if section == 1:
-            self.steps(8)
+            for i in (1, 3):
+                self.group_ready(1, i)
+            self.done(1)
+
+    def group_ready(self, section, i):
+        if isinstance(i, int):
+            self.from_sibling(section, self.group(i))
         else:
-            self.steps(9)
-        self.from_sibling(section, self.group(1))
-        self.from_sibling(section, self.group(3))
-        self.own_copy(section).wait()
+            pl.when(i % 2 == 1)(lambda: self.from_sibling(section, self.group(i)))
+
+    def done(self, section):
         self.keep(section).start()
 
     def steps(self, step):
@@ -532,8 +545,12 @@
     source.ready(2)
 
     @pl.loop(0, sizes.groups)
-    def _(g):
+    def _(i):
+        g = source.group(i)
+        source.group_ready(2, i)
         hidden[...] += dot(z[g], w[2, g], 1, 1)
+
+    source.done(2)
 
     normed, factor = norm_stats(hidden[...])
     n_2[...] = normed
@@ -745,22 +762,22 @@
 
 DURING = {
     0: (("encoded", 0),),
-    1: (("second", 2),),
+    2: (("second", 2),),
     5: (("first", 2),),
+    7: (("second", 1),),
 }
-BEFORE_LAST = (("second", 1),)
+BEFORE_LAST = (("line", 2),)
 AFTER_LAST = (
     ("begin", 0),
     ("chip", 0),
-    ("line", 2),
+    ("small", 0),
     ("first", 1),
+    ("small", 1),
     ("tokens", 0),
     ("second", 0),
-    ("small", 0),
+    ("small", 2),
     ("line", 1),
-    ("small", 1),
     ("first", 0),
-    ("small", 2),
     ("relay", 0),
     ("line", 0),
 )
@@ -799,7 +816,7 @@
     def to_second(self, s, k):
         g, x = self.routes[s].second_columns[1 - k // 4]
         return remote(
-            self.shard(s, g, 2 * (k % 4) + x),
+            self.shard(s, g, 2 * self.at.zs[3 - k % 4] + x),
             self.by_second.at[s, k],
             self.second_sems.at[0, s, k],
             self.second_sems.at[1, s, k],
@@ -809,7 +826,7 @@
     def to_first(self, s, k):
         g, x = self.routes[s].first_column
         return remote(
-            self.shard(s, g, 2 * k + x),
+            self.shard(s, g, 2 * self.at.zs[3 - k] + x),
             self.by_first.at[s, k],
             self.first_sems.at[0, s, k],
             self.first_sems.at[1, s, k],
@@ -826,18 +843,23 @@
             at.line[j],
         )
 
+    def chip_shard(self, s, g, z, x):
+        d = 2 * z + x
+        rows = pl.ds(pl.multiple_of(d * self.rows, 16), self.rows)
+        self.shard(s, g, d)[...] += self.inbox[self.STAGE[s] + g // 2, rows]
+
     def chip_sum(self, s):
         for k in range(2):
             self.to_sibling(s, k).wait_recv()
-            held, more = self.part(self.HELD[s] + k), self.inbox.at[self.STAGE[s] + k]
-
-            @pl.loop(0, held.shape[0] // self.rows)
-            def _(d):
-                rows = pl.ds(pl.multiple_of(d * self.rows, 16), self.rows)
-                held[rows, :] = (held[rows, :].astype(F32) + more[rows, :].astype(F32)).astype(BF16)
-
         for k in range(8):
+            g, x = self.routes[s].second_columns[1 - k // 4]
+            self.chip_shard(s, g, self.at.zs[3 - k % 4], x)
             self.to_second(s, k).start()
+        for g, x in (self.routes[s].first_column, self.at.own_column):
+
+            @pl.loop(0, 4)
+            def _(z):
+                self.chip_shard(s, g, z, x)
 
     def other_line(self, s, j):
         g, x = self.routes[s].first_column
@@ -880,17 +902,12 @@
         at, (g, x) = self.at, self.routes[s].first_column
         for k in range(8):
             self.to_second(s, k).wait_recv()
-        for j in (3, 2, 1, 0):
-            z = at.zs[j]
-            mine = self.shard(s, g, 2 * z + x)
-            mine[...] = (mine[...].astype(F32) + self.by_second[s, z].astype(F32)).astype(BF16)
+            j = 3 - k % 4
+            mine = self.shard(s, g, 2 * at.zs[j] + x) if k < 4 else self.shard(s, at.mp, 2 * at.zs[j] + at.x)
+            if k < 7:
+                mine[...] += self.by_second[s, k]
             if j:
-                self.other_line(s, j).start()
-        for j in (3, 2, 1):
-            z = at.zs[j]
-            mine = self.shard(s, at.mp, 2 * z + at.x)
-            mine[...] = (mine[...].astype(F32) + self.by_second[s, 4 + z].astype(F32)).astype(BF16)
-            self.to_line(s, j).start()
+                (self.other_line if k < 4 else self.to_line)(s, j).start()
 
     def from_first_early(self, s):
         g, x = self.routes[s].first_column
@@ -905,7 +922,7 @@
     def from_line_early(self, s):
         at = self.at
         mine = self.shard(s, at.mp, 2 * at.z + at.x)
-        total = mine[...].astype(F32) + self.by_second[s, 4 + at.z].astype(F32)
+        total = mine[...].astype(F32) + self.by_second[s, 7].astype(F32)
         for j in range(1, 4):
             self.to_line(s, j).wait_recv()
             total = total + self.by_line[s, j - 1].astype(F32)
@@ -916,8 +933,7 @@
         g, x = self.routes[s].first_column
         for k in range(4):
             self.to_second(s, k).wait_recv()
-            mine = self.shard(s, g, 2 * k + x)
-            mine[...] = (mine[...].astype(F32) + self.by_second[s, k].astype(F32)).astype(BF16)
+            self.shard(s, g, 2 * self.at.zs[3 - k] + x)[...] += self.by_second[s, k]
             self.to_first(s, k).start()
 
     def from_first_late(self, s):
@@ -925,17 +941,15 @@
         for k in range(4):
             self.to_second(s, 4 + k).wait_recv()
             self.to_first(s, k).wait_recv()
-        for j in (3, 2, 1, 0):
-            z = at.zs[j]
-            mine = self.shard(s, at.mp, 2 * z + at.x)
+            mine = self.shard(s, at.mp, 2 * at.zs[3 - k] + at.x)
             total = (
                 mine[...].astype(F32)
-                + self.by_second[s, 4 + z].astype(F32)
-                + self.by_first[s, z].astype(F32)
+                + self.by_second[s, 4 + k].astype(F32)
+                + self.by_first[s, k].astype(F32)
             )
-            if j:
+            if k < 3:
                 mine[...] = total.astype(BF16)
-                self.to_line(s, j).start()
+                self.to_line(s, 3 - k).start()
             else:
                 self.shards[s] = total
 

time: 222 us -> 217 us (0.977)
  Pallas kernels: 221 us -> 216 us
    pallas_call x1, Pallas kernels: 129 us -> 125 us  [run_finish(): pl.pallas_call(functools.partial(finish_kernel, sizes), out_shape=outs, i...]
where the time goes in v6:
time: 217 us
  Pallas kernels  216 us (100%)
    pallas_call x1, Pallas kernels, run_finish(): pl.pallas_call(functools.partial(finish_kernel, sizes), out_shape=outs, i...  125 us
    pallas_call x1, Pallas kernels, run_forward(): pl.pallas_call(functools.partial(kernel, sizes), out_shape=outs, in_specs...  82.5 us
    pallas_call x1, Pallas kernels, run_outputs(): pl.pallas_call(functools.partial(outputs_kernel, cols), out_shape=outs, i...  8.14 us

profile of v6, /device:TPU:1, one launch (start us, length us, event | category | flops | bytes accessed | tf_op | source)
XLA Modules:
  0.0 216.6 jit_solution(14347120619403115258)
XLA Ops:
  0.7 82.5 %forward.1 = (bf16[3,4,768,768]{3,2,1,0:T(8,128)(2,1)}, bf16[512,768]{1,0:T(8,128)(2,1)}, f32[8,768]{1,0:T(8,128)}, f32[512,768]{1,0:T(8,128)}, f32[512,1]{1,0:T...) custom-call(s32[1,8]{1,0:T(1,128)} %lens.3, ...), custom_call_target="tpu_custom_call" | custom-call | tf_op jit(solution)/shard_map/forward/pallas_call | solution.py:1559
  83.2 125.1 %finish.1 = (f32[64,1024]{1,0:T(8,128)}, f32[8,1]{1,0:T(8,128)}, f32[24,768]{1,0:T(8,128)}, f32[3,96,768]{2,1,0:T(8,128)}, bf16[2048,768]{1,0:T(8,128)(2,1)}, /*index=5*/bf16[2048,768]{1,0:T(8,128)(2,1)}) custom-call(s32[1,8]{1,0:T(1,128)} %lens.3, f32[8,768]{1,0:T(8,128)} %get-tuple-element.57.cls, s32[64]{0:T(128)} %gold.1, f32[768]{0:T(1024)} %gain_1.1, ...), custom_call_target="tpu_custom_call" | custom-call | tf_op jit(solution)/shard_map/finish/pallas_call | solution.py:1689
  208.3 8.1 %outputs.1 = (f32[64,1024]{1,0:T(8,128)}, f32[8]{0:T(128)}, bf16[2048,768]{1,0:T(8,128)(2,1)}, f32[2048,768]{1,0:T(8,128)}, f32[96,192]{1,0:T(8,128)}, /*index=5...) custom-call(f32[64,1024]{1,0:T(8,128)} %get-tuple-element.70.table, ...), custom_call_target="tpu_custom_call" | custom-call | tf_op jit(solution)/shard_map/outputs/pallas_call | solution.py:1866

commit v7 on v6

--- a/solution.py
+++ b/solution.py
@@ -87,6 +87,11 @@
         return pl.multiple_of(self.key_start(me, block) - self.window_start(me), 16)
 
 
+def square(parts, index):
+    side = parts.shape[1]
+    return parts.at[pl.ds(pl.multiple_of(index * side, side), side)]
+
+
 def document_bounds(lens, places):
     start = jnp.zeros_like(places)
     end = jnp.zeros_like(places)
@@ -125,7 +130,7 @@
     return picked
 
 
-def project(sizes, me, group, span, tokens, w_attn, biases, kv, q):
+def project(sizes, me, group, slot, span, tokens, weight, biases, kv, q):
     cut = sizes.window // 2
     own = pl.ds(sizes.own_offset(me), sizes.own)
 
@@ -134,13 +139,13 @@
         g = group(i)
         for part in range(2):
             rows = pl.ds(part * cut, cut)
-            made = dot(tokens[rows, :], w_attn[g, :, tile(0, 3)]) + biases[g, :, tile(0, 3)]
-            kv[g, rows, :] = made.astype(BF16)
-        made = dot(tokens[own, :], w_attn[g, :, tile(3, 2)]) + biases[g, :, tile(3, 2)]
+            made = dot(tokens[rows, :], weight(0, g)[:, tile(0, 3)]) + biases[g, :, tile(0, 3)]
+            kv[slot(i), rows, :] = made.astype(BF16)
+        made = dot(tokens[own, :], weight(0, g)[:, tile(3, 2)]) + biases[g, :, tile(3, 2)]
         q[g] = made.astype(BF16) * jnp.asarray(HEAD**-0.5, BF16)
 
 
-def attend(sizes, me, group, span, tick, kv, q, bias, lse, ctx):
+def attend(sizes, me, group, slot, span, tick, kv, q, bias, lse, ctx):
     @pl.loop(*span)
     def _(i):
         g = group(i)
@@ -157,11 +162,11 @@
                 vt, vh = VALUE_AT[j]
                 qt, _ = QUERY_AT[j]
                 query = q[g, rows, tile(qt)] * half_mask(kh, BF16)
-                s = dot(kv[g, keys, tile(kt)], query, 1, 1) + bias[b]
+                s = dot(kv[slot(i), keys, tile(kt)], query, 1, 1) + bias[b]
                 peak = jnp.max(s, axis=0, keepdims=True)
                 e = jnp.exp(s - peak)
                 total = jnp.sum(e, axis=0, keepdims=True)
-                mixed = dot(kv[g, keys, tile(vt)], e.astype(BF16), 0, 0)
+                mixed = dot(kv[slot(i), keys, tile(vt)], e.astype(BF16), 0, 0)
                 made.append(mixed[vh * HEAD : (vh + 1) * HEAD] / total)
                 logs.append(peak + jnp.log(total))
             ctx[g, rows, :] = jnp.concatenate(made, axis=0).T.astype(BF16)
@@ -225,6 +230,9 @@
     def group(self, i):
         return i
 
+    def slot(self, i):
+        return i
+
     def near_heads(self):
         self.copies[0].wait()
 
@@ -235,9 +243,6 @@
         self.copies[section].wait()
 
     def group_ready(self, section, i):
-        pass
-
-    def done(self, section):
         pass
 
     def tick(self, step):
@@ -276,7 +281,9 @@
         self.by_core = Route(self, self.core)
         self.x_first, self.y_first = Route(self, 0), Route(self, 1)
         self.own_column = (self.mp, self.x)
-        self.peers = [*self.line[1:], self.x_peer, self.y_peer, self.sibling, self.diagonal]
+        self.mates = (self.sibling, self.y_peer, self.diagonal)
+        self.others = [(lax.rem(self.dp + k, 8), self.mp) for k in range(1, 8)]
+        self.peers = [*self.mates, *self.others]
 
 
 def signal(peers):
@@ -314,11 +321,12 @@
         self.own_bias, self.biases = own_bias, biases
         self.send_sems, self.recv_sems, self.local, self.bias_sems = send, recv, local, bias_sems
         self.rows = packed[1].shape[0]
-        self.shards = w.shape[2] // self.rows
+        self.shards = w.shape[1] // self.rows
         self.routes = [getattr(place, name) for name in self.ROUTES]
 
     def shard(self, s, g, d):
-        return self.w.at[s, g, pl.ds(pl.multiple_of(d * self.rows, 16), self.rows)]
+        first = (4 * s + g) * self.w.shape[1] + d * self.rows
+        return self.w.at[pl.ds(pl.multiple_of(first, 16), self.rows)]
 
     def copy(self, s, g, d, slot, peer, source=None):
         here = self.shard(s, g, d)
@@ -381,13 +389,19 @@
         at = self.at
         return 2 * (at.y + (i // 2) * (1 - 2 * at.y)) + at.core + (i % 2) * (1 - 2 * at.core)
 
+    def slot(self, i):
+        return i % 2
+
     def from_sibling(self, s, g):
         @pl.loop(0, self.shards)
         def _(d):
             self.arrived(s, g, d)
 
-    def keep(self, s):
-        return pltpu.make_async_copy(self.w.at[s], self.kept.at[s], self.local.at[3 + s])
+    def keep(self, s, i):
+        index = 4 * s + self.group(i)
+        return pltpu.make_async_copy(
+            square(self.w, index), square(self.kept, index), self.local.at[3 + 4 * s + i]
+        )
 
     def bias_copy(self, k, peer):
         return pltpu.make_async_remote_copy(
@@ -419,28 +433,33 @@
             copy.wait_recv()
         self.own_copy(0).wait()
         self.from_sibling(0, self.group(1))
+        self.keep(0, 0).start()
+        self.keep(0, 1).start()
 
     def far_heads(self):
         self.steps("far")
         self.from_sibling(0, self.group(3))
-        self.keep(0).start()
+        self.keep(0, 2).start()
+        self.keep(0, 3).start()
 
     def ready(self, section):
         self.steps(7 + section)
         self.own_copy(section).wait()
+        for i in (0, 2):
+            self.keep(section, i).start()
         if section == 1:
             for i in (1, 3):
                 self.group_ready(1, i)
-            self.done(1)
 
     def group_ready(self, section, i):
+        def take():
+            self.from_sibling(section, self.group(i))
+            self.keep(section, i).start()
+
         if isinstance(i, int):
-            self.from_sibling(section, self.group(i))
+            take()
         else:
-            pl.when(i % 2 == 1)(lambda: self.from_sibling(section, self.group(i)))
-
-    def done(self, section):
-        self.keep(section).start()
+            pl.when(i % 2 == 1)(take)
 
     def steps(self, step):
         actions = {
@@ -467,7 +486,8 @@
             def _(slot):
                 self.copy(s, 0, 0, slot, self.at.sibling).wait_send()
 
-            self.keep(s).wait()
+            for i in range(4):
+                self.keep(s, i).wait()
 
 
 def forward_math(
@@ -495,7 +515,7 @@
     lse,
     ctx,
     x,
-    w,
+    weight,
     bias,
     hidden,
     kv,
@@ -510,19 +530,26 @@
     source.begin()
     fill_mask(sizes, me, lens, bias)
     load.wait()
-    save_kv = pltpu.make_async_copy(kv, kv_out, sems.at[1])
     half = sizes.groups // 2
+
+    def save_kv(i):
+        return pltpu.make_async_copy(
+            kv.at[source.slot(i)], kv_out.at[source.group(i)], sems.at[4 + i]
+        )
+
     for span, ready in (((0, half), source.near_heads), ((half, sizes.groups), source.far_heads)):
         ready()
-        project(sizes, me, source.group, span, x, w.at[0], biases, kv, q)
-        if span[1] == sizes.groups:
-            save_kv.start()
-        attend(sizes, me, source.group, span, source.tick, kv, q, bias, lse, ctx)
+        project(sizes, me, source.group, source.slot, span, x, weight, biases, kv, q)
+        for i in range(*span):
+            save_kv(i).start()
+        attend(sizes, me, source.group, source.slot, span, source.tick, kv, q, bias, lse, ctx)
+        for i in range(*span):
+            save_kv(i).wait()
 
     own = pl.ds(sizes.own_offset(me), sizes.own)
     hidden[...] = x[own, :].astype(F32) + as_row(b_out)
     for g in range(sizes.groups):
-        hidden[...] += dot(ctx[g], w[0, g, :, tile(4, 2)], 1, 1)
+        hidden[...] += dot(ctx[g], weight(0, g)[:, tile(4, 2)], 1, 1)
     normed, factor = norm_stats(hidden[...])
     n_1[...] = normed
     r_1[...] = factor
@@ -533,7 +560,7 @@
 
     @pl.loop(0, sizes.groups)
     def _(g):
-        a = dot(encoded[...], w[1, g]) + biases[g, :, 5 * LANES :]
+        a = dot(encoded[...], weight(1, g)[...]) + biases[g, :, 5 * LANES :]
         out, grad = gelu_and_slope(a)
         z[g] = out.astype(BF16)
         slope[g] = grad.astype(BF16)
@@ -548,9 +575,7 @@
     def _(i):
         g = source.group(i)
         source.group_ready(2, i)
-        hidden[...] += dot(z[g], w[2, g], 1, 1)
-
-    source.done(2)
+        hidden[...] += dot(z[g], weight(2, g)[...], 1, 1)
 
     normed, factor = norm_stats(hidden[...])
     n_2[...] = normed
@@ -559,7 +584,6 @@
     encoded[...] = y_2
     cls[...] = dot(start_rows(sizes, me, lens).astype(BF16), y_2)
     source.end()
-    save_kv.wait()
     save_z.wait()
     save_slope.wait()
 
@@ -567,7 +591,13 @@
 def forward_kernel(sizes, lens, tokens, weights, biases, *rest):
     *refs, w, bias, hidden, kv, z, slope, sems, loads = rest
     source = Loads(weights, w, loads)
-    forward_math(sizes, source, lens, tokens, biases, *refs, w, bias, hidden, kv, z, slope, sems)
+
+    def weight(section, g):
+        return w.at[section, g]
+
+    forward_math(
+        sizes, source, lens, tokens, biases, *refs, weight, bias, hidden, kv, z, slope, sems
+    )
 
 
 def pack(w_key, w_value, w_query, w_out, w_down, b_value, b_query, b_up, packed, own_bias):
@@ -580,23 +610,6 @@
     own_bias[:, cols : 2 * cols] = as_row(b_value)
     own_bias[:, 2 * cols : 3 * cols] = as_row(b_query)
     own_bias[:, 5 * LANES :] = as_row(b_up)
-
-
-def gathering_kernel(sizes, lens, tokens, *rest):
-    shards, rows, (kept, *outs) = rest[:9], rest[9:15], rest[15:]
-    *refs, w, bias, hidden, kv, z, slope, sems, packed, own_bias, biases, send, recv, local, bias_sems = outs
-    w_key, w_value, w_query, w_out, w_up, w_down, b_value, b_query, b_up = shards
-
-    def fill():
-        pack(w_key, w_value, w_query, w_out, w_down, b_value, b_query, b_up, packed, own_bias)
-
-    source = Gather(
-        Place(), (packed.at[0], w_up, packed.at[1]), own_bias, w, biases, kept, send, recv, local, bias_sems
-    )
-    source.fill = fill
-    forward_math(
-        sizes, source, lens, tokens, biases, *rows, *refs, w, bias, hidden, kv, z, slope, sems
-    )
 
 
 def backward_kernel(
@@ -720,11 +733,6 @@
     )
 
 
-def square(parts, index):
-    side = parts.shape[1]
-    return parts.at[pl.ds(pl.multiple_of(index * side, side), side)]
-
-
 class Spread:
     def __init__(self, place, source, whole, send, recv, local):
         self.at, self.source, self.whole = place, source, whole
@@ -762,16 +770,16 @@
 
 DURING = {
     0: (("encoded", 0),),
-    2: (("second", 2),),
+    1: (("second", 2),),
     5: (("first", 2),),
-    7: (("second", 1),),
+    6: (("second", 1),),
 }
 BEFORE_LAST = (("line", 2),)
 AFTER_LAST = (
     ("begin", 0),
+    ("first", 1),
     ("chip", 0),
     ("small", 0),
-    ("first", 1),
     ("small", 1),
     ("tokens", 0),
     ("second", 0),
@@ -1159,14 +1167,16 @@
                 self.sent[g % 2, side] = self.dkv[rows, :].astype(BF16)
                 self.copy(g, side).start()
 
-    def add(self, g, own):
+    def add(self, g, own, total):
         for side in range(2):
 
             @pl.when(self.has[1 - side])
             def _():
                 self.copy(g, side).wait_recv()
                 rows = pl.ds(self.into[side], LONGEST)
-                own[rows, :] += self.got[g, side].astype(F32)
+                more = self.got[g, side].astype(F32)
+                total[:, tile(0, 3)] += jnp.sum(more, axis=0, keepdims=True)
+                own[rows, tile(0, 3)] = (own[rows, tile(0, 3)].astype(F32) + more).astype(BF16)
 
     def end(self):
         for side in range(2):
@@ -1177,82 +1187,51 @@
                 self.copy(3, side).wait_send()
 
 
-def finish_kernel(
+def finish_math(
     sizes,
+    at,
     lens,
-    cls,
+    cotangent,
+    tokens,
+    passages,
     gold,
     gain_1,
     shift_1,
     gain_2,
-    r_1,
-    r_2,
-    lse,
-    tokens,
-    cotangent,
-    passages,
-    encoded,
-    weights,
-    n_1_in,
-    n_2_in,
-    z_in,
-    slope_in,
-    kv_in,
-    q_in,
-    ctx_in,
-    scores,
-    query_lse,
-    small_out,
-    shards,
-    encoded_whole,
-    token_whole,
-    w,
+    held,
+    kept,
+    outs,
+    landing,
+    sems,
     ffn,
-    parts,
-    inbox,
-    by_second,
-    by_first,
-    by_line,
     kv,
-    q,
-    ctx,
     dctx,
     dkv,
-    own_kv,
     halo_sent,
-    halo_got,
-    n_1,
-    work,
     rows_low,
-    row_in,
     turned,
     low,
-    bias,
     delta,
-    sums,
-    sums_in,
-    part,
-    parts_in,
-    firsts,
-    first_rows,
-    back_sent,
-    back_got,
-    stats,
-    stats_got,
-    load_sems,
-    kv_sems,
-    ffn_sems,
-    spread_sems,
-    core_sems,
-    second_sems,
-    first_sems,
-    line_sems,
-    halo_sems,
-    small_sems,
-    mp_sems,
-    score_sems,
 ):
-    at = Place()
+    parts, cls, r_1, r_2, lse, q, ctx, encoded, n_1, work, bias = held
+    weights, z_in, slope_in, kv_in = kept
+    scores, query_lse, small_out, shards, encoded_whole, token_whole = outs
+    inbox, by_second, by_first, by_line, halo_got, sums, sums_in, *scored = landing
+    part, parts_in, firsts, first_rows, back_sent, back_got, stats, stats_got = scored
+    (
+        load_sems,
+        kv_sems,
+        ffn_sems,
+        spread_sems,
+        core_sems,
+        second_sems,
+        first_sems,
+        line_sems,
+        halo_sems,
+        small_sems,
+        mp_sems,
+        score_sems,
+    ) = sems
     me = at.mp
     own_rows = pl.ds(pl.multiple_of(sizes.own * me, 16), sizes.own)
     ways = firsts.shape[0]
@@ -1273,19 +1252,15 @@
 
     loads = [
         load(0, passages, table),
-        load(1, cotangent.at[own_rows], row_in),
-        load(2, n_2_in, work.at[1]),
-        load(3, n_1_in, n_1),
-        load(5, q_in, q),
-        load(6, ctx_in, ctx),
+        load(1, cotangent.at[own_rows], ffn.at[1]),
     ]
+    weight_slots = 10
 
     def kv_load(g):
-        return pltpu.make_async_copy(kv_in.at[g], kv.at[g % 2], kv_sems.at[g % 2])
+        return pltpu.make_async_copy(kv_in.at[g], kv, kv_sems.at[0])
 
     for copy in loads:
         copy.start()
-    kv_load(0).start()
 
     scoring = Scoring(
         at,
@@ -1298,43 +1273,42 @@
         (part, parts_in, firsts, first_rows, back_sent, back_got, stats, stats_got),
         (mp_sems, score_sems),
     )
-    signal([*scoring.mates, *scoring.others])
+    scoring.start_cls()
+    kv_load(0).start()
 
     def group_of(i):
         return jnp.where(i < 2, 1 - at.core + 2 * i, at.core + 2 * (i - 2))
 
+    def wide(k):
+        return square(parts, weight_slots + k)
+
     def z_load(i):
-        return pltpu.make_async_copy(z_in.at[group_of(i)], ffn.at[0, i % 2], ffn_sems.at[i % 2, 0])
+        return pltpu.make_async_copy(z_in.at[group_of(i)], ffn.at[i % 2], ffn_sems.at[i % 2, 0])
 
     def ffn_loads(i):
         slot, g = i % 2, group_of(i)
         return [
-            pltpu.make_async_copy(weights.at[2, g], w.at[2 * slot], ffn_sems.at[slot, 1]),
-            pltpu.make_async_copy(weights.at[1, g], w.at[2 * slot + 1], ffn_sems.at[slot, 2]),
-            pltpu.make_async_copy(slope_in.at[g], ffn.at[1, slot], ffn_sems.at[slot, 3]),
+            pltpu.make_async_copy(square(weights, 8 + g), wide(2 * slot), ffn_sems.at[slot, 1]),
+            pltpu.make_async_copy(square(weights, 4 + g), wide(2 * slot + 1), ffn_sems.at[slot, 2]),
+            pltpu.make_async_copy(slope_in.at[g], ffn.at[2 - 2 * slot], ffn_sems.at[slot, 3]),
         ]
 
     z_load(0).start()
     for copy in ffn_loads(0):
         copy.start()
 
-    arrive([*scoring.mates, *scoring.others])
-    scoring.start_cls()
     loads[0].wait()
     scoring.start_gold()
     scoring.start_firsts()
     spread.begin()
-    fill_mask(sizes, me, lens, bias)
     picked = start_rows(sizes, me, lens).astype(BF16)
-    loads[3].wait()
     turned[1] = (n_1[...] * as_row(gain_1) + as_row(shift_1)).T.astype(BF16)
     scoring.start_back()
     loads[1].wait()
-    loads[2].wait()
     dcls = scoring.result()
     high = dcls.astype(BF16)
     rest = (dcls - high.astype(F32)).astype(BF16)
-    dy = row_in[...].astype(F32) + dot(picked, high, 0, 0) + dot(picked, rest, 0, 0)
+    dy = ffn[1].astype(F32) + dot(picked, high, 0, 0) + dot(picked, rest, 0, 0)
     mine = sums.at[0]
     mine[0:1, :] = jnp.sum(dy * work[1], axis=0, keepdims=True)
     mine[1:2, :] = jnp.sum(dy, axis=0, keepdims=True)
@@ -1355,7 +1329,7 @@
         def _():
             z_load(i + 1).start()
 
-        square(parts, into(2, i))[...] = dot(turned[0], ffn[0, i % 2]).astype(BF16)
+        square(parts, into(2, i))[...] = dot(turned[0], ffn[i % 2]).astype(BF16)
         pl.when(i < 2)(lambda: scatter.to_sibling(2, i).start())
 
     scatter.chip_sum(2)
@@ -1371,16 +1345,20 @@
             for copy in ffn_loads(i + 1):
                 copy.start()
 
-        da = dot(rows_low[...], w[2 * slot]) * ffn[1, slot].astype(F32)
+        da = dot(rows_low[...], wide(2 * slot)[...]) * ffn[2 - 2 * slot].astype(F32)
         mine[pl.ds(8 + g, 1), :] = jnp.sum(da, axis=0, keepdims=True)
         da_low = da.astype(BF16)
         square(parts, into(1, i))[...] = dot(turned[1], da_low).astype(BF16)
         pl.when(i < 2)(lambda: scatter.to_sibling(1, i).start())
-        work[0] += dot(da_low, w[2 * slot + 1], 1, 1)
-
-    load_w = pltpu.make_async_copy(weights.at[0], w, load_sems.at[7])
+        work[0] += dot(da_low, wide(2 * slot + 1)[...], 1, 1)
+
+    load_w = pltpu.make_async_copy(
+        weights.at[pl.ds(0, 4 * sizes.width)],
+        parts.at[pl.ds(weight_slots * sizes.width, 4 * sizes.width)],
+        load_sems.at[7],
+    )
     load_w.start()
-    load_x = load(1, tokens.at[own_rows], row_in)
+    load_x = load(1, tokens.at[own_rows], ffn.at[0])
     load_x.start()
     scatter.chip_sum(1)
     scatter.sent_to_sibling(2)
@@ -1396,14 +1374,12 @@
     rows_low[...] = grad.astype(BF16)
     turned[0] = grad.T.astype(BF16)
     load_x.wait()
-    turned[1] = row_in[...].astype(F32).T.astype(BF16)
+    turned[1] = ffn[0].astype(F32).T.astype(BF16)
     load_w.wait()
-    for copy in loads[4:]:
-        copy.wait()
 
     @pl.loop(0, sizes.groups)
     def _(g):
-        dctx[g] = dot(rows_low[...], w[g, :, tile(4, 2)]).astype(BF16)
+        dctx[g] = dot(rows_low[...], wide(g)[:, tile(4, 2)]).astype(BF16)
 
     actions = {
         "second": scatter.from_second,
@@ -1427,11 +1403,8 @@
 
     def finalize(g):
         slot = g % 2
-        halo.add(g, own_kv.at[slot])
-        dkv_own = own_kv[slot]
-        mine[pl.ds(16 + g, 1), tile(0, 3)] = jnp.sum(dkv_own, axis=0, keepdims=True)
-        low[slot, :, tile(0, 3)] = dkv_own.astype(BF16)
-        work[1] += dot(low[slot], w[g, :, tile(0, 5)], 1, 1)
+        halo.add(g, low.at[slot], mine.at[pl.ds(16 + g, 1)])
+        work[1] += dot(low[slot], wide(g)[:, tile(0, 5)], 1, 1)
         into = jnp.where(g % 2 == at.core, Scatter.HELD[0], Scatter.STAGE[0]) + g // 2
         made = dot(turned[1], low[slot])
         more = dot(turned[0], ctx[g])
@@ -1450,24 +1423,25 @@
     def _(g):
         slot = g % 2
         kv_load(g).wait()
-
-        @pl.when(g < sizes.groups - 1)
-        def _():
-            kv_load(g + 1).start()
-
         delta[...] = delta_rows(dctx[g], ctx[g])
         dkv[...] = jnp.zeros_like(dkv)
         for b in range(sizes.blocks):
             tick(g * sizes.blocks + b)
             rows = slice(b * sizes.block, (b + 1) * sizes.block)
             dq = attend_back_block(
-                sizes, me, g, b, kv.at[slot], q, bias, lse, dctx, delta, dkv
+                sizes, me, g, b, kv, q, bias, lse, dctx, delta, dkv
             )
             total = jnp.sum(dq, axis=0, keepdims=True)
             mine[pl.ds(16 + g, 1), tile(3, 2)] += total
             low[slot, rows, tile(3, 2)] = dq.astype(BF16)
+
+        @pl.when(g < sizes.groups - 1)
+        def _():
+            kv_load(g + 1).start()
+
         halo.start(g)
-        own_kv[slot] = dkv[own, :]
+        mine[pl.ds(16 + g, 1), tile(0, 3)] = jnp.sum(dkv[own, :], axis=0, keepdims=True)
+        low[slot, :, tile(0, 3)] = dkv[own, :].astype(BF16)
 
         @pl.when(g > 0)
         def _():
@@ -1485,6 +1459,56 @@
     scoring.end()
     spread.end()
     token_spread.end()
+
+
+def layer_kernel(sizes, lens, tokens, cotangent, passages, gold, *rest):
+    weights, rows, outs, kept = rest[:9], rest[9:15], rest[15:21], rest[21:25]
+    w, cls, r_1, r_2, lse, q, ctx, encoded, n_1, work, bias, packed, own_bias, biases = rest[25:39]
+    landing, sems = rest[39:54], rest[54:]
+    w_key, w_value, w_query, w_out, w_up, w_down, b_value, b_query, b_up = weights
+    own, width, groups = sizes.own, sizes.width, sizes.groups
+    at = Place()
+    source = Gather(at, (packed.at[0], w_up, packed.at[1]), own_bias, w, biases, kept[0], *sems[:4])
+
+    def fill():
+        pack(w_key, w_value, w_query, w_out, w_down, b_value, b_query, b_up, packed, own_bias)
+
+    source.fill = fill
+
+    def weight(section, g):
+        return square(w, 4 * section + g)
+
+    def forward(x, kv, z, slope):
+        forward_math(
+            sizes, source, lens, tokens, biases, *rows, encoded, cls, n_1, r_1, work.at[1], r_2,
+            *kept[1:], q, lse, ctx, x, weight, bias, work.at[0], kv, z, slope, sems[4],
+        )
+
+    pl.run_scoped(
+        forward,
+        pltpu.VMEM((sizes.window, width), BF16),
+        pltpu.VMEM((2, sizes.window, 3 * LANES), BF16),
+        pltpu.VMEM((groups, own, width), BF16),
+        pltpu.VMEM((groups, own, width), BF16),
+    )
+    held = (w, cls, r_1, r_2, lse, q, ctx, encoded, n_1, work, bias)
+    z_kept, slope_kept, kv_kept = kept[1:]
+    finish = functools.partial(
+        finish_math, sizes, at, lens, cotangent, tokens, passages, gold, rows[1], rows[2], rows[4],
+        held, (kept[0], z_kept, slope_kept, kv_kept), outs, landing, sems[5:],
+    )
+    pl.run_scoped(
+        finish,
+        pltpu.VMEM((3, own, width), BF16),
+        pltpu.VMEM((sizes.window, 3 * LANES), BF16),
+        pltpu.VMEM((groups, own, 2 * LANES), BF16),
+        pltpu.VMEM((sizes.window, 3 * LANES), F32),
+        pltpu.VMEM((2, 2, LONGEST, 3 * LANES), BF16),
+        pltpu.VMEM((own, width), BF16),
+        pltpu.VMEM((2, width, own), BF16),
+        pltpu.VMEM((2, own, 5 * LANES), BF16),
+        pltpu.VMEM((8, own), F32),
+    )
 
 
 def input_kernel(sizes, tokens, weights, dkv, dq, dh_1, grads_out, token_grad, grads, small, turned, low):
@@ -1508,10 +1532,10 @@
 
 
 def params(**more):
-    return pltpu.CompilerParams(vmem_limit_bytes=63 * 2**20, **more)
-
-
-def run_forward(sizes, lengths, tokens, weights, rows, gathers):
+    return pltpu.CompilerParams(vmem_limit_bytes=64 * 2**20, **more)
+
+
+def run_forward(sizes, lengths, tokens, weights, rows):
     own, width, groups = sizes.own, sizes.width, sizes.groups
     docs = lengths.shape[1]
     shape = jax.ShapeDtypeStruct
@@ -1538,31 +1562,16 @@
         pltpu.VMEM((groups, sizes.window, 3 * LANES), BF16),
         pltpu.VMEM((groups, own, width), BF16),
         pltpu.VMEM((groups, own, width), BF16),
-        pltpu.SemaphoreType.DMA((4,)),
+        pltpu.SemaphoreType.DMA((4 + groups,)),
     ]
-    if gathers:
-        outs.insert(0, shape((3, groups, width, width), BF16))
-        spaces.insert(0, ANY)
-        scratch += [
-            pltpu.VMEM((2, weights[0].shape[0], width), BF16),
-            pltpu.VMEM((1, 5 * LANES + weights[8].shape[0]), F32),
-            pltpu.VMEM((groups, 1, 5 * LANES + weights[8].shape[0]), F32),
-            pltpu.SemaphoreType.DMA((3, 31)),
-            pltpu.SemaphoreType.DMA((3, 32)),
-            pltpu.SemaphoreType.DMA((6,)),
-            pltpu.SemaphoreType.DMA((2, 3)),
-        ]
-        kernel, more = gathering_kernel, {"collective_id": 0, "has_side_effects": True}
-    else:
-        scratch.append(pltpu.SemaphoreType.DMA((3,)))
-        kernel, more = forward_kernel, {}
+    scratch.append(pltpu.SemaphoreType.DMA((3,)))
     return pl.pallas_call(
-        functools.partial(kernel, sizes),
+        functools.partial(forward_kernel, sizes),
         out_shape=outs,
-        in_specs=specs(SMEM, ANY, *([VMEM] * 15 if gathers else [ANY, *[VMEM] * 7])),
+        in_specs=specs(SMEM, ANY, ANY, *[VMEM] * 7),
         out_specs=specs(*spaces),
         scratch_shapes=scratch,
-        compiler_params=params(**more),
+        compiler_params=params(),
         name="forward",
     )(lengths, tokens, *weights, *rows)
 
@@ -1623,58 +1632,62 @@
     )(own_tokens, w_attn, dkv, dq, dh_1, grads_out)
 
 
-def run_finish(sizes, small_in, large_in):
+def run_layer(sizes, lengths, tokens, cotangent, passages, gold, weights, rows):
     own, width, groups = sizes.own, sizes.width, sizes.groups
-    tokens, passages = large_in[0], large_in[2]
-    queries = small_in[2].shape[0]
-    ways = queries // 8
-    shard = width // ways
-    shape = jax.ShapeDtypeStruct
+    queries, docs = gold.shape[0], lengths.shape[1]
+    ways = queries // docs
+    shard, half = width // ways, width // 2
+    shape, vmem, dma = jax.ShapeDtypeStruct, pltpu.VMEM, pltpu.SemaphoreType.DMA
     outs = (
         shape((queries, passages.shape[0]), F32),
-        shape((8, 1), F32),
+        shape((docs, 1), F32),
         shape((24, width), F32),
         shape((3, shard, width), F32),
         shape(tokens.shape, BF16),
         shape(tokens.shape, BF16),
-    )
-    dma = pltpu.SemaphoreType.DMA
+        shape((12 * width, width), BF16),
+        shape((groups, own, width), BF16),
+        shape((groups, own, width), BF16),
+        shape((groups, sizes.window, 3 * LANES), BF16),
+    )
+    bias_width = 5 * LANES + weights[8].shape[0]
     scratch = [
-        pltpu.VMEM((groups, width, width), BF16),
-        pltpu.VMEM((2, 2, own, width), BF16),
-        pltpu.VMEM((10 * width, width), BF16),
-        pltpu.VMEM((4, width, width), BF16),
-        pltpu.VMEM((3, 8, shard, width), BF16),
-        pltpu.VMEM((3, 4, shard, width), BF16),
-        pltpu.VMEM((3, 3, shard, width), BF16),
-        pltpu.VMEM((2, sizes.window, 3 * LANES), BF16),
-        pltpu.VMEM((groups, own, 2 * LANES), BF16),
-        pltpu.VMEM((groups, own, 2 * LANES), BF16),
-        pltpu.VMEM((groups, own, 2 * LANES), BF16),
-        pltpu.VMEM((sizes.window, 3 * LANES), F32),
-        pltpu.VMEM((2, own, 3 * LANES), F32),
-        pltpu.VMEM((2, 2, LONGEST, 3 * LANES), BF16),
-        pltpu.VMEM((groups, 2, LONGEST, 3 * LANES), BF16),
-        pltpu.VMEM((own, width), F32),
-        pltpu.VMEM((2, own, width), F32),
-        pltpu.VMEM((own, width), BF16),
-        pltpu.VMEM((own, width), BF16),
-        pltpu.VMEM((2, width, own), BF16),
-        pltpu.VMEM((2, own, 5 * LANES), BF16),
-        pltpu.VMEM((sizes.blocks, sizes.keys, sizes.block), F32),
-        pltpu.VMEM((8, own), F32),
-        pltpu.VMEM((4, 24, width), F32),
-        pltpu.VMEM((6, 24, width), F32),
-        pltpu.VMEM((16, width // 2), BF16),
-        pltpu.VMEM((3, 16, width // 2), BF16),
-        pltpu.VMEM((ways, 16, width // 2), BF16),
-        pltpu.VMEM((queries, width), F32),
-        pltpu.VMEM((2, ways, 16, width // 2), BF16),
-        pltpu.VMEM((2, ways, 16, width // 2), BF16),
-        pltpu.VMEM((ways, 8, LANES), F32),
-        pltpu.VMEM((ways, 8, LANES), F32),
+        vmem((14 * width, width), BF16),
+        vmem((docs, width), F32),
+        vmem((own, 1), F32),
+        vmem((own, 1), F32),
+        vmem((groups, sizes.blocks, 8, sizes.block), F32),
+        vmem((groups, own, 2 * LANES), BF16),
+        vmem((groups, own, 2 * LANES), BF16),
+        vmem((own, width), BF16),
+        vmem((own, width), F32),
+        vmem((2, own, width), F32),
+        vmem((sizes.blocks, sizes.keys, sizes.block), F32),
+        vmem((2, shard, width), BF16),
+        vmem((1, bias_width), F32),
+        vmem((groups, 1, bias_width), F32),
+        vmem((4, width, width), BF16),
+        vmem((3, 8, shard, width), BF16),
+        vmem((3, 4, shard, width), BF16),
+        vmem((3, 3, shard, width), BF16),
+        vmem((groups, 2, LONGEST, 3 * LANES), BF16),
+        vmem((4, 24, width), F32),
+        vmem((6, 24, width), F32),
+        vmem((16, half), BF16),
+        vmem((3, 16, half), BF16),
+        vmem((ways, 16, half), BF16),
+        vmem((queries, width), F32),
+        vmem((2, ways, 16, half), BF16),
+        vmem((2, ways, 16, half), BF16),
+        vmem((ways, 8, LANES), F32),
+        vmem((ways, 8, LANES), F32),
+        dma((3, 31)),
+        dma((3, 32)),
+        dma((15,)),
+        dma((2, 3)),
+        dma((4 + groups,)),
         dma((10,)),
-        dma((2,)),
+        dma((1,)),
         dma((2, 4)),
         dma((2, 2, 3)),
         dma((2, 3, 2)),
@@ -1687,14 +1700,14 @@
         dma((4, 2, ways - 1)),
     ]
     return pl.pallas_call(
-        functools.partial(finish_kernel, sizes),
+        functools.partial(layer_kernel, sizes),
         out_shape=outs,
-        in_specs=specs(SMEM, *[VMEM] * (len(small_in) - 1), *[ANY] * len(large_in)),
-        out_specs=specs(*[VMEM] * 4, ANY, ANY),
+        in_specs=specs(SMEM, ANY, ANY, ANY, *[VMEM] * (1 + len(weights) + len(rows))),
+        out_specs=specs(*[VMEM] * 4, *[ANY] * 6),
         scratch_shapes=scratch,
-        compiler_params=params(collective_id=1, has_side_effects=True),
-        name="finish",
-    )(*small_in, *large_in)
+        compiler_params=params(collective_id=0, has_side_effects=True),
+        name="layer",
+    )(lengths, tokens, cotangent, passages, gold, *weights, *rows)[:6]
 
 
 def cut_along(array, dim, devices):
@@ -1734,7 +1747,7 @@
     own_bias = jnp.concatenate([zeros, b_value, b_query, zeros[:HEAD], b_up])[None]
     whole = lax.all_gather(lax.all_gather(packed, "dp", axis=1, tiled=True), "mp", axis=1)
     biases = lax.all_gather(own_bias, "mp", axis=0)
-    encoded, cls, *saved = run_forward(sizes, lengths, tokens, (whole, biases), rows, False)
+    encoded, cls, *saved = run_forward(sizes, lengths, tokens, (whole, biases), rows)
     cls = lax.psum(cls, "mp").astype(BF16)
     table, lse, dcls = score(cls, passages, gold)
     n_1, r_1, n_2, r_2, z, slope, kv, q, logs, ctx = saved
@@ -1906,14 +1919,7 @@
     rows = (b_out, gain_attn, shift_attn, b_down, gain_ffn, shift_ffn)
     shards = (w_key, w_value, w_query, w_out, w_up, w_down.T, b_value, b_query, b_up)
     if lax.axis_size("dp") == 8 and groups == 4:
-        whole, encoded, cls, n_1, r_1, n_2, r_2, z, slope, kv, q, logs, ctx = run_forward(
-            sizes, lengths, tokens, shards, rows, True
-        )
-        made = run_finish(
-            sizes,
-            (lengths, cls, gold, gain_attn, shift_attn, gain_ffn, r_1, r_2, logs),
-            (tokens, cotangent, passages, encoded, whole, n_1, n_2, z, slope, kv, q, ctx),
-        )
+        made = run_layer(sizes, lengths, tokens, cotangent, passages, gold, shards, rows)
         outs = list(run_outputs(made, w_key.shape[1]))
         outs[15] = outs[15].T
         return tuple(outs)

time: 217 us -> 211 us (0.972)
  Pallas kernels: 216 us -> 210 us
    pallas_call x2 -> x1, Pallas kernels: 208 us -> 202 us  [run_layer(): pl.pallas_call(functools.partial(layer_kernel, sizes), out_shape=outs, in...]
where the time goes in v7:
time: 211 us
  Pallas kernels  210 us (100%)
    pallas_call x1, Pallas kernels, run_layer(): pl.pallas_call(functools.partial(layer_kernel, sizes), out_shape=outs, in...  202 us
    pallas_call x1, Pallas kernels, run_outputs(): pl.pallas_call(functools.partial(outputs_kernel, cols), out_shape=outs, i...  8.14 us

profile of v7, /device:TPU:1, one launch (start us, length us, event | category | flops | bytes accessed | tf_op | source)
XLA Modules:
  0.0 210.8 jit_solution(13555179381719469555)
XLA Ops:
  0.7 201.8 %layer.1 = (f32[64,1024]{1,0:T(8,128)}, f32[8,1]{1,0:T(8,128)}, f32[24,768]{1,0:T(8,128)}, f32[3,96,768]{2,1,0:T(8,128)}, bf16[2048,768]{1,0:T(8,128)(2,1)}, /*i...) custom-call(s32[1,8]{1,0:T(1,128)} %lens.1, ...), custom_call_target="tpu_custom_call" | custom-call | tf_op jit(solution)/shard_map/layer/pallas_call | solution.py:1702
  202.4 8.1 %outputs.1 = (f32[64,1024]{1,0:T(8,128)}, f32[8]{0:T(128)}, bf16[2048,768]{1,0:T(8,128)(2,1)}, f32[2048,768]{1,0:T(8,128)}, f32[96,192]{1,0:T(8,128)}, /*index=5...) custom-call(f32[64,1024]{1,0:T(8,128)} %get-tuple-element.44.table, ...), custom_call_target="tpu_custom_call" | custom-call | tf_op jit(solution)/shard_map/outputs/pallas_call | solution.py:1879

commit v8 on v7

--- a/solution.py
+++ b/solution.py
@@ -299,16 +299,16 @@
 GATHER_STEPS = {
     "begin": (("along", 0), ("out", 0), ("out", 1), ("out", 2)),
     "near": (("z", 0, 1, 2, 3), ("along", 1), ("first", 0, 0, 1, 2, 3)),
-    0: (("z", 1, 1, 2, 3), ("along", 2)),
-    1: (("second", 0, 0, 1, 2, 3),),
-    2: (("first", 1, 0, 1), ("second", 0, 4, 5)),
-    3: (("first", 1, 2, 3), ("second", 0, 6, 7)),
-    4: (("z", 2, 1, 2, 3),),
-    5: (("second", 1, 0, 1, 2, 3),),
-    6: (("second", 1, 4, 5, 6, 7),),
-    7: (("first", 2, 0, 1),),
-    8: (("first", 2, 2, 3),),
-    9: (("second", 2, 0, 1, 2, 3, 4, 5, 6, 7),),
+    0: (("z", 1, 1, 2, 3), ("along", 2), ("second", 0, 0, 1, 2, 3)),
+    1: (("second", 0, 4, 5, 6, 7),),
+    2: (("first", 1, 0, 1),),
+    3: (("first", 1, 2, 3),),
+    4: (("z", 2, 1, 2, 3), ("second", 1, 0, 1)),
+    5: (("second", 1, 2, 3, 4, 5),),
+    6: (("second", 1, 6, 7), ("first", 2, 0)),
+    7: (("first", 2, 1, 2),),
+    8: (("first", 2, 3), ("second", 2, 0, 1, 2, 3)),
+    9: (("second", 2, 4, 5, 6, 7),),
 }
 
 
@@ -1874,7 +1874,7 @@
         shape((rows, width), F32),
         *[vector] * 3,
     )
-    steps = 8
+    steps = 4
     span = tokens.shape[0] // steps
     return pl.pallas_call(
         functools.partial(outputs_kernel, cols),

time: 211 us -> 210 us (level)
  no operation moved by 1% of the time
where the time goes in v8:
time: 210 us
  Pallas kernels  209 us (100%)
    pallas_call x1, Pallas kernels, run_layer(): pl.pallas_call(functools.partial(layer_kernel, sizes), out_shape=outs, in...  201 us
    pallas_call x1, Pallas kernels, run_outputs(): pl.pallas_call(functools.partial(outputs_kernel, cols), out_shape=outs, i...  7.72 us

profile of v8, /device:TPU:1, one launch (start us, length us, event | category | flops | bytes accessed | tf_op | source)
XLA Modules:
  0.0 209.7 jit_solution(555725493645011573)
XLA Ops:
  0.7 201.1 %layer.1 = (f32[64,1024]{1,0:T(8,128)}, f32[8,1]{1,0:T(8,128)}, f32[24,768]{1,0:T(8,128)}, f32[3,96,768]{2,1,0:T(8,128)}, bf16[2048,768]{1,0:T(8,128)(2,1)}, /*i...) custom-call(s32[1,8]{1,0:T(1,128)} %lens.1, ...), custom_call_target="tpu_custom_call" | custom-call | tf_op jit(solution)/shard_map/layer/pallas_call | solution.py:1702
  201.8 7.7 %outputs.1 = (f32[64,1024]{1,0:T(8,128)}, f32[8]{0:T(128)}, bf16[2048,768]{1,0:T(8,128)(2,1)}, f32[2048,768]{1,0:T(8,128)}, f32[96,192]{1,0:T(8,128)}, /*index=5...) custom-call(f32[64,1024]{1,0:T(8,128)} %get-tuple-element.44.table, ...), custom_call_target="tpu_custom_call" | custom-call | tf_op jit(solution)/shard_map/outputs/pallas_call | solution.py:1879
